TPU v7x, 256 devices: a whole 4x4x8 slice. The times are simulated.
256 devices in a mesh: dp: 64 (over z_lo, x, y, core), mp: 4 (over z_hi).
Axes of the slice: x: 4, y: 4, z: 8 (z_hi: 4, z_lo: 2; z = z_hi * 2 + z_lo), core: 2. Of those that a mesh axis runs over, the one named last changes fastest.
Arguments:
- activations: bfloat16 [32768, 2560], P('dp', 'mp'), may hold values from -80 to 80
- output_grad: bfloat16 [32768, 2560], P(('dp', 'mp')), may hold values from -80 to 80
- act_inverse: bfloat16 [2560, 640], P('mp'), may hold values from -3 to 3
- grad_inverse: bfloat16 [2560, 640], replicated, may hold values from -3 to 3
Outputs:
- act_cov: float32 [2560, 640], P(('mp', 'dp'))
- grad_cov: float32 [2560, 640], P(('dp', 'mp'))
- update: bfloat16 [2560, 2560], P('mp')
All inputs are finite; a program needn't handle non-finite values.
Results may differ from a plain program's by a relative error of at most 0.0046.
The roundings to bfloat16 on the way count: a program that leaves them out, or rounds other values in their place, can miss the bound.
Values may be sent and summed in bfloat16 or wider, within the bound.
No kernel may reach another device: no remote copies, remote signals or barrier semaphores. Data moves between devices by JAX's collectives and lax.ppermute only.
A program may use at most 128 MiB of HBM per device.

v0:
```python
import jax
import jax.numpy as jnp
from jax import lax
from jax.sharding import PartitionSpec as P


def body(activations, output_grad, act_inverse, grad_inverse):
    token_count = activations.shape[0]
    width_block = activations.shape[1]
    out_width = output_grad.shape[1]
    data_count = lax.axis_size("dp")
    model_count = lax.axis_size("mp")
    row_count = out_width // data_count
    col_count = width_block // data_count
    block_total = out_width // width_block
    spread = width_block // row_count
    inv_tokens = 1.0 / (token_count * data_count)
    gathered = lax.all_gather(output_grad, "mp", axis=0, tiled=True)
    local_grad = output_grad.reshape(output_grad.shape[0], block_total, width_block)
    cov_term = jnp.einsum(
        "tjc,tjd->jcd", local_grad, local_grad, preferred_element_type=jnp.float32
    )
    cov_term = cov_term.reshape(out_width, width_block) * inv_tokens
    grad_cov = lax.psum_scatter(cov_term, ("dp", "mp"), scatter_dimension=0, tiled=True)
    act_term = (
        lax.dot_general(
            activations, activations, (((0,), (0,)), ((), ())), preferred_element_type=jnp.float32
        )
        * inv_tokens
    )
    act_cov = lax.psum_scatter(act_term, "dp", scatter_dimension=0, tiled=True)
    product = lax.dot_general(
        gathered, activations, (((0,), (0,)), ((), ())), preferred_element_type=jnp.float32
    )
    grad_rows = lax.psum_scatter(product * inv_tokens, "dp", scatter_dimension=0, tiled=True)
    mixed_rows = lax.dot_general(
        act_inverse.astype(jnp.float32),
        grad_rows,
        (((1,), (1,)), ((), ())),
        precision=lax.Precision.HIGHEST,
    )
    mixed_rows = mixed_rows.astype(jnp.bfloat16).reshape(data_count, col_count, row_count)
    inverse_blocks = grad_inverse.reshape(block_total, spread, row_count, width_block)
    pieces = lax.all_to_all(mixed_rows, "dp", split_axis=0, concat_axis=0, tiled=True)
    item_count = pieces.shape[1]
    grouped = pieces.reshape(block_total, spread, item_count, row_count)
    result = jnp.einsum(
        "jscr,jsre->cje", grouped, inverse_blocks, preferred_element_type=jnp.float32
    )
    precond = result.reshape(item_count, out_width)
    squares = jnp.sum(precond * precond)
    total_sq = lax.psum(squares, ("dp", "mp"))
    mean_square = total_sq / (width_block * model_count * out_width)
    scaled_rows = (precond * lax.rsqrt(mean_square + 1e-06)).astype(jnp.bfloat16)
    update = lax.all_gather(scaled_rows, "dp", axis=0, tiled=True)
    return (act_cov, grad_cov, update)


def solution(mesh):
    placed = (P("dp", "mp"), P(("dp", "mp"), None), P("mp", None), P())
    return jax.shard_map(
        body,
        mesh=mesh,
        in_specs=placed,
        out_specs=(P(("mp", "dp"), None), P(("dp", "mp"), None), P("mp", None)),
        check_vma=False,
    )
```

profile of v0, /device:TPU:6, one launch (start us, length us, event | category | flops | bytes accessed | tf_op | source)
XLA Modules:
  0.0 1317.4 jit_solution(8679556573259608189)
XLA Ops:
  7.2 0.7 all-gather.4.cloned.1.call-update
  8.0 65.2 %all-gather.4.cloned.1.call-done = bf16[512,2560]{1,0:T(8,128)(2,1)} async-done(((bf16[128,2560]{1,0:T(8,128)(2,1)}), bf16[512,2560]{1,0:T(8,128)(2,1)}) %all-gather.4.cloned.1.call-update) | async-done | bytes 2621456 | tf_op jit(solution)/shard_map/all_gather | solution.py:18
  73.1 6.8 convolution_multiply_fusion
  79.9 0.0 all-reduce.6.cloned.1.call-start
  80.0 3.2 convolution_multiply_fusion.1
  83.2 5.1 broadcast_multiply_fusion
  88.4 266.1 %reduce-scatter.5.cloned.1.call-done = f32[40,640]{1,0:T(8,128)} async-done(((f32[2560,640]{1,0:T(8,128)}), f32[40,640]{1,0:T(8,128)}) %reduce-scatter.5.cloned.1.call-update) | async-done | bytes 102416
  354.5 2.1 fusion
  356.6 0.8 copy.16
  357.4 1.0 reshape.26
  358.4 0.8 reshape.35
  359.2 33.4 %all_to_all.5 = bf16[64,2,200]{2,1,0:T(2,128)(2,1)} all-to-all(bf16[64,2,200]{2,1,0:T(2,128)(2,1)} %reshape.35), channel_id=1, replica_groups=mesh['dp'=64,'mp'=4] {'dp'}, dimensions={0} | all-to-all | bytes 102400 | tf_op jit(solution)/shard_map/all_to_all | solution.py:44
  392.7 1.0 reshape.36
  393.7 2.0 multiply_reduce_fusion
  395.7 74.4 %psum.7 = f32[]{:T(128)} all-reduce(f32[]{:T(128)} %get-tuple-element.3), channel_id=1, replica_groups=mesh['dp'=64,'mp'=4] {'dp','mp'}, use_global_device_ids=true, to_apply=%region_4.0 | all-reduce | flops 1 | bytes 8 | tf_op jit(solution)/shard_map/psum | solution.py:52
  470.8 0.9 fusion.3
  471.8 0.7 reshape.29
  472.5 0.6 dynamic-slice
  473.7 424.1 %all-reduce.6.cloned.1.call-done = f32[640,640]{1,0:T(8,128)} async-done(((f32[640,640]{1,0:T(8,128)}), f32[640,640]{1,0:T(8,128)}) %all-reduce.6.cloned.1.call-update) | async-done | bytes 1638416
  897.8 1.5 constant_dynamic-slice_fusion.1
  899.2 295.3 %all-reduce.8.cloned.1.call-done = f32[2560,640]{1,0:T(8,128)} async-done(((f32[2560,640]{1,0:T(8,128)}), f32[2560,640]{1,0:T(8,128)}) %all-reduce.8.cloned.1.call-update) | async-done | bytes 6553616
  1194.5 1.5 constant_dynamic-slice_fusion
  1196.0 107.9 %all-gather.6.cloned.1.call-done = bf16[64,10,2560]{2,1,0:T(8,128)(2,1)} async-done(((bf16[1,10,2560]{2,1,0:T(8,128)(2,1)}), bf16[64,10,2560]{2,1,0:T(8,128)(2,1)}) %all-gather.6.cloned.1.call-update) | async-done | bytes 3276816 | tf_op jit(solution)/shard_map/all_gather | solution.py:55
  1303.9 7.0 reshape.30
  (13 shorter events, 0.3 us)
Async XLA Ops:
  7.2 386.6 %copy-start = (bf16[2560,640]{1,0:T(8,128)(2,1)S(1)}, bf16[2560,640]{1,0:T(8,128)(2,1)}, u32[]{:S(2)}) copy-start(bf16[2560,640]{1,0:T(8,128)(2,1)} %param.7) | copy-start | bytes 9830404
  7.2 65.9 %all-gather.4.cloned.1.call-start = ((), (), s32[]{:S(2)}) async-start(), calls=%async_computation.2 | async-start | bytes 3276800 | tf_op jit(solution)/shard_map/all_gather | solution.py:18
  7.9 346.6 %reduce-scatter.5.cloned.1.call-start = ((), (), s32[]{:S(2)}) async-start(), calls=%async_computation.6 | async-start | bytes 6656000
  79.9 817.9 %all-reduce.6.cloned.1.call-start = ((), (), s32[]{:S(2)}) async-start(), calls=%async_computation.4 | async-start | bytes 3276800
  83.2 1111.3 %all-reduce.8.cloned.1.call-start = ((), (), s32[]{:S(2)}) async-start(), calls=%async_computation.5 | async-start | bytes 13107200
  88.4 384.1 %copy-start.1 = (u32[256]{0:T(256)S(1)}, u32[256]{0:T(256)}, u32[]{:S(2)}) copy-start(u32[256]{0:T(256)} %constant.13) | copy-start | bytes 3076
  88.4 1215.5 %all-gather.6.cloned.1.call-start = ((), (), s32[]{:S(2)}) async-start(), calls=%async_computation.3 | async-start | bytes 5324800 | tf_op jit(solution)/shard_map/all_gather | solution.py:55
Sparse Core Ops, SparseCore 0:
  9.8 63.2 all-gather.3
  80.1 274.4 reduce-scatter.4
  357.9 539.8 all-reduce.5
  903.2 291.2 all-reduce.7
  1196.2 107.5 all-gather.5
where the time goes:
time: 1320 us
  waiting for transfers between devices  1160 us (88%)
  blocking collectives  108 us (8%)
  matrix products  19.1 us (1%)
  between operations  15.2 us (1%)
  local copies, waits for them, and re-layouts  14.9 us (1%)
    unnamed x8, waiting for transfers between devices  986 us
    all_gather x1, waiting for transfers between devices, body(): update = lax.all_gather(scaled_rows, 'dp', axis=0, tiled=True)  108 us
    psum x1, blocking collectives, body(): total_sq = lax.psum(squares, ('dp', 'mp'))  74.4 us
    all_gather x1, waiting for transfers between devices, body(): gathered = lax.all_gather(output_grad, 'mp', axis=0, tiled=True)  65.2 us
    all_to_all x1, blocking collectives, body(): lax.all_to_all(mixed_rows, 'dp', split_axis=0, concat_axis=0, tiled=True)  33.4 us
  transfers between devices with their start and end apart: 5, of which 5 were waited for; matrix products, arithmetic and copies ran while one was open for 2% of the time, Pallas kernels for 0%

commit v1 on v0

v1 whole, which is shorter than its diff:
```python
import jax
import jax.numpy as jnp
from jax import lax
from jax.sharding import Mesh, PartitionSpec as P

DP = ("zlo", "x", "y", "core")
EVERY = DP + ("zhi",)
PLANE = ("x", "y")
BF16 = jnp.bfloat16
F32 = jnp.float32


def shift(value, axis, step):
    count = lax.axis_size(axis)
    return lax.ppermute(value, axis, [(i, (i + step) % count) for i in range(count)])


def token_dot(lhs, rhs):
    return lax.dot_general(lhs, rhs, (((0,), (0,)), ((), ())), preferred_element_type=F32)


def spread_sum(partial, inv_tokens):
    peers = lax.axis_size("x") * lax.axis_size("y")
    rows = partial.shape[0] // peers
    sent = (partial * inv_tokens).astype(BF16).reshape(peers, rows, partial.shape[1])
    got = lax.all_to_all(sent, PLANE, split_axis=0, concat_axis=0, tiled=True)
    return jnp.sum(got.astype(F32), axis=0)


def plane_gather(piece):
    peers = lax.axis_size("x") * lax.axis_size("y")
    copies = jnp.broadcast_to(piece[None], (peers,) + piece.shape)
    got = lax.all_to_all(copies, PLANE, split_axis=0, concat_axis=0, tiled=True)
    return got.reshape(peers * piece.shape[0], piece.shape[1])


def body(activations, output_grad, act_inverse, grad_inverse):
    token_count, width = activations.shape
    out_width = output_grad.shape[1]
    dp_count = 1
    for name in DP:
        dp_count *= lax.axis_size(name)
    heads = lax.axis_size("zhi")
    group = token_count // heads
    half = out_width // 2
    inv_tokens = 1.0 / (token_count * dp_count)
    core = lax.axis_index("core")
    head = lax.axis_index("zhi")
    zlo = lax.axis_index("zlo")

    def swap_core(value):
        return shift(value, "core", 1)

    chunks = []
    for part in range(2):
        kept = lax.dynamic_slice_in_dim(output_grad, core * half + part * width, width, 1)
        given = lax.dynamic_slice_in_dim(output_grad, (1 - core) * half + part * width, width, 1)
        chunks.append(jnp.concatenate([kept, swap_core(given)], axis=0))
    other_act = swap_core(activations)

    offsets = (0, heads - 1, 1, 2)
    acts = []
    for offset in offsets:
        start = lax.rem(head + offset, heads) * group
        mine = lax.dynamic_slice_in_dim(activations, start, group, 0)
        theirs = lax.dynamic_slice_in_dim(other_act, start, group, 0)
        acts.append(jnp.concatenate([mine, theirs], axis=0))

    pieces = []
    for part, chunk in enumerate(chunks):
        ahead = shift(chunk, "zhi", 1)
        back = shift(chunk, "zhi", -1)
        far = shift(ahead, "zhi", 1) if part == 0 else shift(back, "zhi", -1)
        pieces.append((chunk, ahead, back, far))

    left_t = []
    for part in range(2):
        partial = sum(token_dot(piece, act) for piece, act in zip(pieces[part], acts))
        share = spread_sum(partial, inv_tokens)
        share = share + shift(share, "zlo", 1)
        mixed = lax.dot_general(
            share,
            act_inverse.astype(F32),
            (((1,), (1,)), ((), ())),
            precision=lax.Precision.HIGHEST,
        ).astype(BF16)
        mine = plane_gather(mixed)
        theirs = swap_core(mine)
        left_t.append((jnp.where(core == 0, mine, theirs), jnp.where(core == 0, theirs, mine)))
    blocks = [left_t[0][0], left_t[1][0], left_t[0][1], left_t[1][1]]

    does_grad = core == head // 2
    total = 0.0
    for index, act in enumerate(acts):
        grad_piece = jnp.where(head % 2 == 0, pieces[0][index], pieces[1][index])
        chosen = jnp.where(does_grad, grad_piece, act)
        total = total + token_dot(chosen, chosen)
    cov = spread_sum(total, inv_tokens)
    rows = cov.shape[0] // 2
    cov_kept = lax.dynamic_slice_in_dim(cov, zlo * rows, rows, 0)
    cov_given = lax.dynamic_slice_in_dim(cov, (1 - zlo) * rows, rows, 0)
    cov = cov_kept + shift(cov_given, "zlo", 1)
    rows = rows // 2
    cov_kept = lax.dynamic_slice_in_dim(cov, core * rows, rows, 0)
    cov_given = lax.dynamic_slice_in_dim(cov, (1 - core) * rows, rows, 0)
    cov_taken = swap_core(cov_given)
    act_rows = jnp.where(does_grad, cov_taken, cov_kept)
    grad_rows = jnp.where(does_grad, cov_kept, cov_taken)
    act_perm, grad_perm = [], []
    sites = lax.axis_size("x") * lax.axis_size("y")
    for zl in range(lax.axis_size("zlo")):
        for site in range(sites):
            for co in range(2):
                source = (zl * sites + site) * 2 + co
                place = (site * 2 + zl) * 2 + co
                act_perm.append((source, place))
                for hd in range(heads):
                    grad_perm.append((source * heads + hd, hd * dp_count + place))
    act_cov = lax.ppermute(act_rows, DP, act_perm)
    grad_cov = lax.ppermute(grad_rows, EVERY, grad_perm)

    results, squares = [], 0.0
    for index, block in enumerate(blocks):
        inverse = grad_inverse[index * width : (index + 1) * width]
        result = token_dot(block, inverse)
        squares = squares + jnp.sum(result * result)
        results.append(result)
    squares = jnp.broadcast_to(squares, (8, 128))
    total_sq = squares
    for step in range(1, heads):
        total_sq = total_sq + shift(squares, "zhi", step)
    mean_square = total_sq[0, 0] / (width * heads * out_width)
    precond = jnp.concatenate(results, axis=1)
    update = (precond * lax.rsqrt(mean_square + 1e-06)).astype(BF16)
    return (act_cov, grad_cov, update)


def solution(mesh):
    fine = Mesh(mesh.devices.reshape(2, 4, 4, 2, 4), EVERY)
    return jax.shard_map(
        body,
        mesh=fine,
        in_specs=(P(DP, "zhi"), P(EVERY, None), P("zhi", None), P()),
        out_specs=(P(("zhi",) + DP, None), P(EVERY, None), P("zhi", None)),
        check_vma=False,
    )
```

time: 1320 us -> 200 us (0.15)
  waiting for transfers between devices: 1160 us -> 50.5 us
  blocking collectives: 108 us -> 0 us
  starting transfers between devices: 0.2 us -> 92.3 us
    unnamed x8 -> x0, waiting for transfers between devices: 986 us -> none
    all_gather x2 -> x0, waiting for transfers between devices: 173 us -> none  [the longest x1 108 us: body(): update = lax.all_gather(scaled_rows, 'dp', axis=0, tiled=True)]
    psum x1 -> x0, blocking collectives: 74.4 us -> none  [body(): total_sq = lax.psum(squares, ('dp', 'mp'))]
    ppermute x0 -> x20, starting transfers between devices: none -> 59.3 us  [the longest x18 49 us: shift(): lax.ppermute(value, axis, [(i, (i + step) % count) for i in range(count)])]
    ppermute x0 -> x20, waiting for transfers between devices: none -> 35.6 us  [the longest x18 35.6 us: shift(): lax.ppermute(value, axis, [(i, (i + step) % count) for i in range(count)])]
    all_to_all x1 -> x0, blocking collectives: 33.4 us -> none  [body(): lax.all_to_all(mixed_rows, 'dp', split_axis=0, concat_axis=0, tiled=True)]
    all_to_all x0 -> x5, starting transfers between devices: none -> 33.1 us  [the longest x3 18.8 us: spread_sum(): got = lax.all_to_all(sent, PLANE, split_axis=0, concat_axis=0, tiled=True)]
    all_to_all x0 -> x5, waiting for transfers between devices: none -> 14.9 us  [the longest x3 14 us: spread_sum(): got = lax.all_to_all(sent, PLANE, split_axis=0, concat_axis=0, tiled=True)]
  transfers between devices with their start and end apart: 5 -> 25, of which waited for: 5 -> 14; matrix products, arithmetic and copies ran while one was open for 2% -> 16% of each run, Pallas kernels for 0% -> 0%
where the time goes in v1:
time: 200 us; the launch traced here: 198 us
  starting transfers between devices  92.3 us (46%)
  waiting for transfers between devices  50.5 us (25%)
  matrix products  31.9 us (16%)
  local copies, waits for them, and re-layouts  11.9 us (6%)
  other arithmetic  6.53 us (3%)
  between operations  4.41 us (2%)
    ppermute x18, starting transfers between devices, shift(): lax.ppermute(value, axis, [(i, (i + step) % count) for i in range(count)])  49 us
    ppermute x18, waiting for transfers between devices, shift(): lax.ppermute(value, axis, [(i, (i + step) % count) for i in range(count)])  35.6 us
    dot_general x16, matrix products, token_dot(): lax.dot_general(lhs, rhs, (((0,), (0,)), ((), ())), preferred_element_typ...  30.2 us
    all_to_all x3, starting transfers between devices, spread_sum(): got = lax.all_to_all(sent, PLANE, split_axis=0, concat_axis=0, tiled=True)  18.8 us
    all_to_all x2, starting transfers between devices, plane_gather(): got = lax.all_to_all(copies, PLANE, split_axis=0, concat_axis=0, tiled=True)  14.3 us
    all_to_all x3, waiting for transfers between devices, spread_sum(): got = lax.all_to_all(sent, PLANE, split_axis=0, concat_axis=0, tiled=True)  14 us
    ppermute x1, starting transfers between devices, body(): act_cov = lax.ppermute(act_rows, DP, act_perm)  8.1 us
    unnamed x71, local copies, waits for them, and re-layouts  7.98 us
  transfers between devices with their start and end apart: 25, of which 14 were waited for; matrix products, arithmetic and copies ran while one was open for 16% of the time, Pallas kernels for 0%

profile of v1, /device:TPU:6, one launch (start us, length us, event | category | flops | bytes accessed | tf_op | source)
XLA Modules:
  0.0 197.5 jit_solution(13909211866079332918)
XLA Ops:
  4.3 3.3 %collective-permute-start.3 = (bf16[256,640]{1,0:T(8,128)(2,1)}, bf16[256,640]{1,0:T(8,128)(2,1)}, u32[]{:S(2)}, u32[]{:S(2)}) collective-permute-start(bf16[256,640]{1,0:T(8,128)(2,1)} %pad_maximum_fusion), channel_id=1, source_target_pairs={{0,1},{1,2},{2,3},{3,0},{4,5},{5,6},{6,7},{7,4},{8,9},{9,10},{10,1... | collective-permute-start | bytes 983048 | tf_op jit(solution)/shard_map/ppermute | solution.py:15
  8.3 3.4 %collective-permute-start.6 = (bf16[256,640]{1,0:T(8,128)(2,1)}, bf16[256,640]{1,0:T(8,128)(2,1)}, u32[]{:S(2)}, u32[]{:S(2)}) collective-permute-start(bf16[256,640]{1,0:T(8,128)(2,1)} %pad_maximum_fusion.1), channel_id=1, source_target_pairs={{0,3},{1,0},{2,1},{3,2},{4,7},{5,4},{6,5},{7,6},{8,11},{9,8},{10,9... | collective-permute-start | bytes 983048 | tf_op jit(solution)/shard_map/ppermute | solution.py:15
  12.9 3.1 %collective-permute-start.5 = (bf16[256,640]{1,0:T(8,128)(2,1)}, bf16[256,640]{1,0:T(8,128)(2,1)S(1)}, u32[]{:S(2)}, u32[]{:S(2)}) collective-permute-start(bf16[256,640]{1,0:T(8,128)(2,1)} %pad_maximum_fusion), channel_id=1, source_target_pairs={{0,3},{1,0},{2,1},{3,2},{4,7},{5,4},{6,5},{7,6},{8,11},{9,8},{10,9... | collective-permute-start | bytes 983048 | tf_op jit(solution)/shard_map/ppermute | solution.py:15
  16.1 6.3 %collective-permute-done.3 = bf16[256,640]{1,0:T(8,128)(2,1)} collective-permute-done((bf16[256,640]{1,0:T(8,128)(2,1)}, bf16[256,640]{1,0:T(8,128)(2,1)}, u32[]{:S(2)}, u32[]{:S(2)}) %collective-permute-start.3) | collective-permute-done | bytes 327712 | tf_op jit(solution)/shard_map/ppermute | solution.py:15
  23.0 12.4 %collective-permute-done.6 = bf16[256,640]{1,0:T(8,128)(2,1)} collective-permute-done((bf16[256,640]{1,0:T(8,128)(2,1)}, bf16[256,640]{1,0:T(8,128)(2,1)}, u32[]{:S(2)}, u32[]{:S(2)}) %collective-permute-start.6) | collective-permute-done | bytes 327712 | tf_op jit(solution)/shard_map/ppermute | solution.py:15
  35.4 3.3 %collective-permute-start.8 = (bf16[256,640]{1,0:T(8,128)(2,1)}, bf16[256,640]{1,0:T(8,128)(2,1)S(1)}, u32[]{:S(2)}, u32[]{:S(2)}) collective-permute-start(bf16[256,640]{1,0:T(8,128)(2,1)} %collective-permute-done.6), channel_id=1, source_target_pairs={{0,3},{1,0},{2,1},{3,2},{4,7},{5,4},{6,5},{7,6},{8,11},{9,8},{10,9... | collective-permute-start | bytes 983048 | tf_op jit(solution)/shard_map/ppermute | solution.py:15
  50.4 7.4 %all-to-all-start = ((bf16[16,40,640]{2,1,0:T(8,128)(2,1)}), bf16[16,40,640]{2,1,0:T(8,128)(2,1)S(1)}, u32[]{:S(2)}, u32[]{:S(2)}) async-start(bf16[16,40,640]{2,1,0:T(8,128)(2,1)} %bitcast.14), calls=%async_computation | async-start | bytes 1638400 | tf_op jit(solution)/shard_map/all_to_all | solution.py:26
  62.9 7.3 %all-to-all-done = bf16[16,40,640]{2,1,0:T(8,128)(2,1)S(1)} async-done(((bf16[16,40,640]{2,1,0:T(8,128)(2,1)}), bf16[16,40,640]{2,1,0:T(8,128)(2,1)S(1)}, u32[]{:S(2)}, u32[]{:S(2)}) %all-to-all-start) | async-done | bytes 819232 | tf_op jit(solution)/shard_map/all_to_all | solution.py:26
  70.2 5.7 %all-to-all-start.3 = ((bf16[16,40,640]{2,1,0:T(8,128)(2,1)}), bf16[16,40,640]{2,1,0:T(8,128)(2,1)S(1)}, u32[]{:S(2)}, u32[]{:S(2)}) async-start(bf16[16,40,640]{2,1,0:T(8,128)(2,1)} %bitcast.3), calls=%async_computation.3 | async-start | bytes 1638400 | tf_op jit(solution)/shard_map/all_to_all | solution.py:26
  80.5 6.7 %all-to-all-done.3 = bf16[16,40,640]{2,1,0:T(8,128)(2,1)S(1)} async-done(((bf16[16,40,640]{2,1,0:T(8,128)(2,1)}), bf16[16,40,640]{2,1,0:T(8,128)(2,1)S(1)}, u32[]{:S(2)}, u32[]{:S(2)}) %all-to-all-start.3) | async-done | bytes 819232 | tf_op jit(solution)/shard_map/all_to_all | solution.py:26
  87.1 5.6 %all-to-all-start.1 = ((bf16[16,40,640]{2,1,0:T(8,128)(2,1)}), bf16[16,40,640]{2,1,0:T(8,128)(2,1)S(1)}, u32[]{:S(2)}, u32[]{:S(2)}) async-start(bf16[16,40,640]{2,1,0:T(8,128)(2,1)} %bitcast.1), calls=%async_computation.1 | async-start | bytes 1638400 | tf_op jit(solution)/shard_map/all_to_all | solution.py:26
  92.9 11.6 %collective-permute-start.15 = (f32[40,640]{1,0:T(8,128)S(1)}, f32[40,640]{1,0:T(8,128)S(1)}, u32[]{:S(2)}, u32[]{:S(2)}) collective-permute-start(f32[40,640]{1,0:T(8,128)S(1)} %convert_reduce_fusion), channel_id=1, source_target_pairs={{0,128},{128,0},{1,129},{129,1},{2,130},{130,2},{3,131},{131,3},{4... | collective-permute-start | bytes 307208 | tf_op jit(solution)/shard_map/ppermute | solution.py:15
  109.0 7.2 %all-to-all-start.4 = ((bf16[16,40,640]{2,1,0:T(8,128)(2,1)}), bf16[16,40,640]{2,1,0:T(8,128)(2,1)S(1)}, u32[]{:S(2)}, u32[]{:S(2)}) async-start(bf16[16,40,640]{2,1,0:T(8,128)(2,1)} %broadcast_in_dim.7), calls=%async_computation.4 | async-start | bytes 1638400 | tf_op jit(solution)/shard_map/all_to_all | solution.py:33
  116.3 6.0 %collective-permute-start.13 = (f32[40,640]{1,0:T(8,128)S(1)}, f32[40,640]{1,0:T(8,128)S(1)}, u32[]{:S(2)}, u32[]{:S(2)}) collective-permute-start(f32[40,640]{1,0:T(8,128)S(1)} %convert_reduce_fusion.1), channel_id=1, source_target_pairs={{0,128},{128,0},{1,129},{129,1},{2,130},{130,2},{3,131},{131,3},{4... | collective-permute-start | bytes 307208 | tf_op jit(solution)/shard_map/ppermute | solution.py:15
  126.9 7.1 %all-to-all-start.2 = ((bf16[16,40,640]{2,1,0:T(8,128)(2,1)}), bf16[16,40,640]{2,1,0:T(8,128)(2,1)}, u32[]{:S(2)}, u32[]{:S(2)}) async-start(bf16[16,40,640]{2,1,0:T(8,128)(2,1)} %broadcast_in_dim.6), calls=%async_computation.2 | async-start | bytes 1638400 | tf_op jit(solution)/shard_map/all_to_all | solution.py:33
  134.1 6.4 %collective-permute-start.9 = (f32[20,640]{1,0:T(8,128)S(1)}, f32[20,640]{1,0:T(8,128)S(1)}, u32[]{:S(2)}, u32[]{:S(2)}) collective-permute-start(f32[20,640]{1,0:T(8,128)S(1)} %constant_dynamic-slice_fusion.1), channel_id=1, source_target_pairs={{0,128},{128,0},{1,129},{129,1},{2,130},{130,2},{3,131},{131,3},{4... | collective-permute-start | bytes 153608 | tf_op jit(solution)/shard_map/ppermute | solution.py:15
  144.6 8.1 %collective-permute-start.11 = (f32[10,640]{1,0:T(8,128)S(1)}, f32[10,640]{1,0:T(8,128)S(1)}, u32[]{:S(2)}, u32[]{:S(2)}) collective-permute-start(f32[10,640]{1,0:T(8,128)S(1)} %get-tuple-element.19), channel_id=1, source_target_pairs={{0,0},{4,4},{8,16},{12,20},{16,32},{20,36},{24,48},{28,52},{32,64}... | collective-permute-start | bytes 76808 | tf_op jit(solution)/shard_map/ppermute | solution.py:119
  154.9 3.2 %multiply_reduce_fusion = (f32[]{:T(128)}, f32[640,640]{0,1:T(8,128)S(1)}) fusion(bf16[2560,640]{1,0:T(8,128)(2,1)} %param.7, bf16[640,640]{1,0:T(8,128)(2,1)} %collective-permute-done.16, bf16[640,640]{1,0:T(8,128)(2,1)S(1)} %bitcast.16, pred[]{:T(512)S(6)} %eq.22), kind=kOutput, calls=%fused_computation.2 | convolution fusion | flops 525516800 | bytes 4096005 | tf_op jit(solution)/shard_map/dot_general | solution.py:19
  163.6 3.9 %multiply_reduce_fusion.3 = (f32[]{:T(128)}, f32[640,640]{0,1:T(8,128)}) fusion(bf16[2560,640]{1,0:T(8,128)(2,1)S(1)} %copy-done.33, bf16[640,640]{1,0:T(8,128)(2,1)} %bitcast.2, bf16[640,640]{1,0:T(8,128)(2,1)S(1)} %collective-permute-done.14, pred[]{:T(512)S(6)} %eq.22), kind=kOutput, calls=%fused_computation.5 | convolution fusion | flops 525516800 | bytes 4096005 | tf_op jit(solution)/shard_map/dot_general | solution.py:19
  170.1 5.7 %collective-permute-start.19 = (f32[8,128]{1,0:T(8,128)S(1)}, f32[8,128]{1,0:T(8,128)S(1)}, u32[]{:S(2)}, u32[]{:S(2)}) collective-permute-start(f32[8,128]{1,0:T(8,128)S(1)} %broadcast_in_dim.8), channel_id=1, source_target_pairs={{0,3},{1,0},{2,1},{3,2},{4,7},{5,4},{6,5},{7,6},{8,11},{9,8},{10,9... | collective-permute-start | bytes 12296 | tf_op jit(solution)/shard_map/ppermute | solution.py:15
  175.8 3.3 %collective-permute-start.18 = (f32[8,128]{1,0:T(8,128)S(1)}, f32[8,128]{1,0:T(8,128)S(1)}, u32[]{:S(2)}, u32[]{:S(2)}) collective-permute-start(f32[8,128]{1,0:T(8,128)S(1)} %broadcast_in_dim.8), channel_id=1, source_target_pairs={{0,2},{1,3},{2,0},{3,1},{4,6},{5,7},{6,4},{7,5},{8,10},{9,11},{10,... | collective-permute-start | bytes 12296 | tf_op jit(solution)/shard_map/ppermute | solution.py:15
  179.5 3.8 %collective-permute-done.18 = f32[8,128]{1,0:T(8,128)S(1)} collective-permute-done((f32[8,128]{1,0:T(8,128)S(1)}, f32[8,128]{1,0:T(8,128)S(1)}, u32[]{:S(2)}, u32[]{:S(2)}) %collective-permute-start.18) | collective-permute-done | bytes 4128 | tf_op jit(solution)/shard_map/ppermute | solution.py:15
  186.0 4.6 %fusion = bf16[640,2560]{0,1:T(8,128)(2,1)} fusion(f32[640,640]{0,1:T(8,128)S(1)} %get-tuple-element.27, f32[640,640]{0,1:T(8,128)} %get-tuple-element.25, f32[640,640]{0,1:T(8,128)} %get-tuple-element.23, f32[640,640]{0,1:T(8,128)} %get-tuple-element.21, f32[]{:T(128)} %bitcast.5), kind=kLoop, calls=%fused_computation.1 | loop fusion | flops 8192000 | bytes 9830404 | tf_op jit(solution)/shard_map/convert_element_type | solution.py:134
  190.6 5.7 %copy.7 = bf16[640,2560]{1,0:T(8,128)(2,1)} copy(bf16[640,2560]{0,1:T(8,128)(2,1)} %fusion) | data formatting | bytes 6553600
  (133 shorter events, 51.9 us)
Async XLA Ops:
  2.0 1.5 collective-permute-start
  2.1 36.6 %collective-permute-start.2 = (bf16[512,640]{1,0:T(8,128)(2,1)}, bf16[512,640]{1,0:T(8,128)(2,1)S(1)}, u32[]{:S(2)}, u32[]{:S(2)}) collective-permute-start(bf16[512,640]{1,0:T(8,128)(2,1)} %param.4), channel_id=1, source_target_pairs={{0,4},{4,0},{1,5},{5,1},{2,6},{6,2},{3,7},{7,3},{8,12},{12,8},{9,1... | collective-permute-start | bytes 1966088 | tf_op jit(solution)/shard_map/ppermute | solution.py:15
  2.6 4.9 %collective-permute-start.1 = (bf16[128,640]{1,0:T(8,128)(2,1)S(1)}, bf16[128,640]{1,0:T(8,128)(2,1)S(1)}, u32[]{:S(2)}, u32[]{:S(2)}) collective-permute-start(bf16[128,640]{1,0:T(8,128)(2,1)S(1)} %get-tuple-element.17), channel_id=1, source_target_pairs={{0,4},{4,0},{1,5},{5,1},{2,6},{6,2},{3,7},{7,3},{8,12},{12,8},{9,1... | collective-permute-start | bytes 491528 | tf_op jit(solution)/shard_map/ppermute | solution.py:15
  4.3 18.1 %collective-permute-start.3 = (bf16[256,640]{1,0:T(8,128)(2,1)}, bf16[256,640]{1,0:T(8,128)(2,1)}, u32[]{:S(2)}, u32[]{:S(2)}) collective-permute-start(bf16[256,640]{1,0:T(8,128)(2,1)} %pad_maximum_fusion), channel_id=1, source_target_pairs={{0,1},{1,2},{2,3},{3,0},{4,5},{5,6},{6,7},{7,4},{8,9},{9,10},{10,1... | collective-permute-start | bytes 983048 | tf_op jit(solution)/shard_map/ppermute | solution.py:15
  8.3 27.1 %collective-permute-start.6 = (bf16[256,640]{1,0:T(8,128)(2,1)}, bf16[256,640]{1,0:T(8,128)(2,1)}, u32[]{:S(2)}, u32[]{:S(2)}) collective-permute-start(bf16[256,640]{1,0:T(8,128)(2,1)} %pad_maximum_fusion.1), channel_id=1, source_target_pairs={{0,3},{1,0},{2,1},{3,2},{4,7},{5,4},{6,5},{7,6},{8,11},{9,8},{10,9... | collective-permute-start | bytes 983048 | tf_op jit(solution)/shard_map/ppermute | solution.py:15
  11.8 27.1 %collective-permute-start.4 = (bf16[256,640]{1,0:T(8,128)(2,1)}, bf16[256,640]{1,0:T(8,128)(2,1)S(1)}, u32[]{:S(2)}, u32[]{:S(2)}) collective-permute-start(bf16[256,640]{1,0:T(8,128)(2,1)} %pad_maximum_fusion.1), channel_id=1, source_target_pairs={{0,1},{1,2},{2,3},{3,0},{4,5},{5,6},{6,7},{7,4},{8,9},{9,10},{10,1... | collective-permute-start | bytes 983048 | tf_op jit(solution)/shard_map/ppermute | solution.py:15
  12.9 33.1 %collective-permute-start.5 = (bf16[256,640]{1,0:T(8,128)(2,1)}, bf16[256,640]{1,0:T(8,128)(2,1)S(1)}, u32[]{:S(2)}, u32[]{:S(2)}) collective-permute-start(bf16[256,640]{1,0:T(8,128)(2,1)} %pad_maximum_fusion), channel_id=1, source_target_pairs={{0,3},{1,0},{2,1},{3,2},{4,7},{5,4},{6,5},{7,6},{8,11},{9,8},{10,9... | collective-permute-start | bytes 983048 | tf_op jit(solution)/shard_map/ppermute | solution.py:15
  22.4 24.3 %collective-permute-start.7 = (bf16[256,640]{1,0:T(8,128)(2,1)}, bf16[256,640]{1,0:T(8,128)(2,1)S(1)}, u32[]{:S(2)}, u32[]{:S(2)}) collective-permute-start(bf16[256,640]{1,0:T(8,128)(2,1)} %collective-permute-done.3), channel_id=1, source_target_pairs={{0,1},{1,2},{2,3},{3,0},{4,5},{5,6},{6,7},{7,4},{8,9},{9,10},{10,1... | collective-permute-start | bytes 983048 | tf_op jit(solution)/shard_map/ppermute | solution.py:15
  35.4 13.5 %collective-permute-start.8 = (bf16[256,640]{1,0:T(8,128)(2,1)}, bf16[256,640]{1,0:T(8,128)(2,1)S(1)}, u32[]{:S(2)}, u32[]{:S(2)}) collective-permute-start(bf16[256,640]{1,0:T(8,128)(2,1)} %collective-permute-done.6), channel_id=1, source_target_pairs={{0,3},{1,0},{2,1},{3,2},{4,7},{5,4},{6,5},{7,6},{8,11},{9,8},{10,9... | collective-permute-start | bytes 983048 | tf_op jit(solution)/shard_map/ppermute | solution.py:15
  50.4 19.8 %all-to-all-start = ((bf16[16,40,640]{2,1,0:T(8,128)(2,1)}), bf16[16,40,640]{2,1,0:T(8,128)(2,1)S(1)}, u32[]{:S(2)}, u32[]{:S(2)}) async-start(bf16[16,40,640]{2,1,0:T(8,128)(2,1)} %bitcast.14), calls=%async_computation | async-start | bytes 1638400 | tf_op jit(solution)/shard_map/all_to_all | solution.py:26
  70.2 16.9 %all-to-all-start.3 = ((bf16[16,40,640]{2,1,0:T(8,128)(2,1)}), bf16[16,40,640]{2,1,0:T(8,128)(2,1)S(1)}, u32[]{:S(2)}, u32[]{:S(2)}) async-start(bf16[16,40,640]{2,1,0:T(8,128)(2,1)} %bitcast.3), calls=%async_computation.3 | async-start | bytes 1638400 | tf_op jit(solution)/shard_map/all_to_all | solution.py:26
  87.1 20.9 %all-to-all-start.1 = ((bf16[16,40,640]{2,1,0:T(8,128)(2,1)}), bf16[16,40,640]{2,1,0:T(8,128)(2,1)S(1)}, u32[]{:S(2)}, u32[]{:S(2)}) async-start(bf16[16,40,640]{2,1,0:T(8,128)(2,1)} %bitcast.1), calls=%async_computation.1 | async-start | bytes 1638400 | tf_op jit(solution)/shard_map/all_to_all | solution.py:26
  92.9 14.2 %collective-permute-start.15 = (f32[40,640]{1,0:T(8,128)S(1)}, f32[40,640]{1,0:T(8,128)S(1)}, u32[]{:S(2)}, u32[]{:S(2)}) collective-permute-start(f32[40,640]{1,0:T(8,128)S(1)} %convert_reduce_fusion), channel_id=1, source_target_pairs={{0,128},{128,0},{1,129},{129,1},{2,130},{130,2},{3,131},{131,3},{4... | collective-permute-start | bytes 307208 | tf_op jit(solution)/shard_map/ppermute | solution.py:15
  109.0 17.0 %all-to-all-start.4 = ((bf16[16,40,640]{2,1,0:T(8,128)(2,1)}), bf16[16,40,640]{2,1,0:T(8,128)(2,1)S(1)}, u32[]{:S(2)}, u32[]{:S(2)}) async-start(bf16[16,40,640]{2,1,0:T(8,128)(2,1)} %broadcast_in_dim.7), calls=%async_computation.4 | async-start | bytes 1638400 | tf_op jit(solution)/shard_map/all_to_all | solution.py:33
  116.3 8.6 %collective-permute-start.13 = (f32[40,640]{1,0:T(8,128)S(1)}, f32[40,640]{1,0:T(8,128)S(1)}, u32[]{:S(2)}, u32[]{:S(2)}) collective-permute-start(f32[40,640]{1,0:T(8,128)S(1)} %convert_reduce_fusion.1), channel_id=1, source_target_pairs={{0,128},{128,0},{1,129},{129,1},{2,130},{130,2},{3,131},{131,3},{4... | collective-permute-start | bytes 307208 | tf_op jit(solution)/shard_map/ppermute | solution.py:15
  126.9 17.1 %all-to-all-start.2 = ((bf16[16,40,640]{2,1,0:T(8,128)(2,1)}), bf16[16,40,640]{2,1,0:T(8,128)(2,1)}, u32[]{:S(2)}, u32[]{:S(2)}) async-start(bf16[16,40,640]{2,1,0:T(8,128)(2,1)} %broadcast_in_dim.6), calls=%async_computation.2 | async-start | bytes 1638400 | tf_op jit(solution)/shard_map/all_to_all | solution.py:33
  134.0 20.9 %collective-permute-start.16 = (bf16[640,640]{1,0:T(8,128)(2,1)S(1)}, bf16[640,640]{1,0:T(8,128)(2,1)}, u32[]{:S(2)}, u32[]{:S(2)}) collective-permute-start(bf16[640,640]{1,0:T(8,128)(2,1)S(1)} %bitcast.15), channel_id=1, source_target_pairs={{0,4},{4,0},{1,5},{5,1},{2,6},{6,2},{3,7},{7,3},{8,12},{12,8},{9,1... | collective-permute-start | bytes 2457608 | tf_op jit(solution)/shard_map/ppermute | solution.py:15
  134.1 9.1 %collective-permute-start.9 = (f32[20,640]{1,0:T(8,128)S(1)}, f32[20,640]{1,0:T(8,128)S(1)}, u32[]{:S(2)}, u32[]{:S(2)}) collective-permute-start(f32[20,640]{1,0:T(8,128)S(1)} %constant_dynamic-slice_fusion.1), channel_id=1, source_target_pairs={{0,128},{128,0},{1,129},{129,1},{2,130},{130,2},{3,131},{131,3},{4... | collective-permute-start | bytes 153608 | tf_op jit(solution)/shard_map/ppermute | solution.py:15
  144.0 16.9 %collective-permute-start.14 = (bf16[640,640]{1,0:T(8,128)(2,1)}, bf16[640,640]{1,0:T(8,128)(2,1)S(1)}, u32[]{:S(2)}, u32[]{:S(2)}) collective-permute-start(bf16[640,640]{1,0:T(8,128)(2,1)} %bitcast.2), channel_id=1, source_target_pairs={{0,4},{4,0},{1,5},{5,1},{2,6},{6,2},{3,7},{7,3},{8,12},{12,8},{9,1... | collective-permute-start | bytes 2457608 | tf_op jit(solution)/shard_map/ppermute | solution.py:15
  144.6 34.9 %collective-permute-start.11 = (f32[10,640]{1,0:T(8,128)S(1)}, f32[10,640]{1,0:T(8,128)S(1)}, u32[]{:S(2)}, u32[]{:S(2)}) collective-permute-start(f32[10,640]{1,0:T(8,128)S(1)} %get-tuple-element.19), channel_id=1, source_target_pairs={{0,0},{4,4},{8,16},{12,20},{16,32},{20,36},{24,48},{28,52},{32,64}... | collective-permute-start | bytes 76808 | tf_op jit(solution)/shard_map/ppermute | solution.py:119
  152.7 26.8 %collective-permute-start.12 = (f32[10,640]{1,0:T(8,128)S(1)}, f32[10,640]{1,0:T(8,128)S(1)}, u32[]{:S(2)}, u32[]{:S(2)}) collective-permute-start(f32[10,640]{1,0:T(8,128)S(1)} %get-tuple-element.18), channel_id=1, source_target_pairs={{0,0},{1,64},{2,128},{3,192},{4,1},{5,65},{6,129},{7,193},{8,4},{9... | collective-permute-start | bytes 76808 | tf_op jit(solution)/shard_map/ppermute | solution.py:120
  170.1 9.4 %collective-permute-start.19 = (f32[8,128]{1,0:T(8,128)S(1)}, f32[8,128]{1,0:T(8,128)S(1)}, u32[]{:S(2)}, u32[]{:S(2)}) collective-permute-start(f32[8,128]{1,0:T(8,128)S(1)} %broadcast_in_dim.8), channel_id=1, source_target_pairs={{0,3},{1,0},{2,1},{3,2},{4,7},{5,4},{6,5},{7,6},{8,11},{9,8},{10,9... | collective-permute-start | bytes 12296 | tf_op jit(solution)/shard_map/ppermute | solution.py:15
  175.8 7.5 %collective-permute-start.18 = (f32[8,128]{1,0:T(8,128)S(1)}, f32[8,128]{1,0:T(8,128)S(1)}, u32[]{:S(2)}, u32[]{:S(2)}) collective-permute-start(f32[8,128]{1,0:T(8,128)S(1)} %broadcast_in_dim.8), channel_id=1, source_target_pairs={{0,2},{1,3},{2,0},{3,1},{4,6},{5,7},{6,4},{7,5},{8,10},{9,11},{10,... | collective-permute-start | bytes 12296 | tf_op jit(solution)/shard_map/ppermute | solution.py:15
  179.1 5.7 %collective-permute-start.17 = (f32[8,128]{1,0:T(8,128)S(1)}, f32[8,128]{1,0:T(8,128)S(1)}, u32[]{:S(2)}, u32[]{:S(2)}) collective-permute-start(f32[8,128]{1,0:T(8,128)S(1)} %broadcast_in_dim.8), channel_id=1, source_target_pairs={{0,1},{1,2},{2,3},{3,0},{4,5},{5,6},{6,7},{7,4},{8,9},{9,10},{10,1... | collective-permute-start | bytes 12296 | tf_op jit(solution)/shard_map/ppermute | solution.py:15
  (35 other events, 466.8 us)

commit v2 on v1

v2 whole, which is shorter than its diff:
```python
import functools

import jax
import jax.numpy as jnp
from jax import lax
from jax.experimental import pallas as pl
from jax.experimental.pallas import tpu as pltpu
from jax.sharding import Mesh, PartitionSpec as P

DP = ("zlo", "x", "y", "core")
EVERY = DP + ("zhi",)
PLANE = ("x", "y")
BF16 = jnp.bfloat16
F32 = jnp.float32
LIMIT = pltpu.CompilerParams(vmem_limit_bytes=40 * 1024 * 1024)
VMEM = pl.BlockSpec(memory_space=pltpu.VMEM)
SMEM = pl.BlockSpec(memory_space=pltpu.SMEM)


def shift(value, axis, step):
    count = lax.axis_size(axis)
    return lax.ppermute(value, axis, [(i, (i + step) % count) for i in range(count)])


def after(value, *earlier):
    return lax.optimization_barrier((value,) + earlier)[0]


def token_dot(lhs, rhs):
    return lax.dot_general(lhs, rhs, (((0,), (0,)), ((), ())), preferred_element_type=F32)


def partial_kernel(scale, choice, *refs):
    first, second, acts, out = refs[:4], refs[4:8], refs[8:12], refs[12]
    sites, _, rows, _ = out.shape

    def product(lefts, rights):
        return sum(token_dot(left[...], right[...]) for left, right in zip(lefts, rights))

    cols = first[0].shape[1]
    for part, pieces in enumerate((first, second)):
        total = product(pieces, acts)
        for index in range(cols // rows):
            slab = part * (cols // rows) + index
            piece = total[index * rows : (index + 1) * rows] * scale
            out[slab // 2, slab % 2] = piece.astype(BF16)

    for which, pieces in enumerate((acts, first, second)):

        @pl.when(choice[0] == which)
        def _():
            total = product(pieces, pieces)
            for index in range(sites):
                piece = total[index * rows : (index + 1) * rows] * scale
                out[index, 2] = piece.astype(BF16)


def partial_sums(choice, pieces, acts, scale, sites):
    width = acts[0].shape[1]
    return pl.pallas_call(
        functools.partial(partial_kernel, scale),
        out_shape=jax.ShapeDtypeStruct((sites, 3, width // sites, width), BF16),
        in_specs=[SMEM] + [VMEM] * 12,
        out_specs=VMEM,
        compiler_params=LIMIT,
        cost_estimate=pl.CostEstimate(flops=6 * 1024 * width * width, bytes_accessed=8 * 2**20, transcendentals=0),
        name="partial_sums",
    )(choice, *pieces, *acts)


def right_kernel(mine, theirs, inv_mine, inv_theirs, out_mine, out_theirs, squares):
    width = mine.shape[1]
    for slot, (left, inverse, out) in enumerate(((mine, inv_mine, out_mine), (theirs, inv_theirs, out_theirs))):
        total = 0.0
        for part in range(2):
            rows = slice(part * width, (part + 1) * width)
            result = token_dot(left[rows, :], inverse[rows, :])
            out[part] = result
            total = total + jnp.sum(result * result)
        squares[slot] = jnp.broadcast_to(total, squares.shape[1:])


def right_product(mine, theirs, inv_mine, inv_theirs):
    width = mine.shape[1]
    block = jax.ShapeDtypeStruct((2, width, width), F32)
    return pl.pallas_call(
        right_kernel,
        out_shape=(block, block, jax.ShapeDtypeStruct((2, 8, 128), F32)),
        in_specs=[VMEM] * 4,
        out_specs=(VMEM, VMEM, VMEM),
        compiler_params=LIMIT,
        cost_estimate=pl.CostEstimate(flops=8 * width**3, bytes_accessed=12 * 2**20, transcendentals=0),
        name="right_product",
    )(mine, theirs, inv_mine, inv_theirs)


def final_kernel(count, core, own, sq_a, sq_b, sq_c, mine, theirs, out):
    total = own[...] + sq_a[...] + sq_b[...] + sq_c[...]
    scale = lax.rsqrt(total / count + 1e-06)[0:1, 0:1]
    width = mine.shape[2]

    def write(first, second):
        for index in range(4):
            block = (first, second)[index // 2][index % 2]
            out[:, index * width : (index + 1) * width] = (block * scale).astype(BF16)

    @pl.when(core[0] == 0)
    def _():
        write(mine, theirs)

    @pl.when(core[0] != 0)
    def _():
        write(theirs, mine)


def final_update(core, sums, blocks, count):
    width = blocks[0].shape[1]
    rows = width // 5
    small = pl.BlockSpec((8, 128), lambda i: (0, 0))
    tile = pl.BlockSpec((2, rows, width), lambda i: (0, i, 0))
    return pl.pallas_call(
        functools.partial(final_kernel, count),
        grid=(5,),
        out_shape=jax.ShapeDtypeStruct((width, 4 * width), BF16),
        in_specs=[SMEM] + [small] * 4 + [tile] * 2,
        out_specs=pl.BlockSpec((rows, 4 * width), lambda i: (i, 0)),
        compiler_params=LIMIT,
        cost_estimate=pl.CostEstimate(flops=4 * width * width, bytes_accessed=10 * 2**20, transcendentals=0),
        name="final_update",
    )(core, *sums, *blocks)


def plane_exchange(value):
    return lax.all_to_all(value, PLANE, split_axis=0, concat_axis=0, tiled=True)


def body(activations, output_grad, act_inverse, grad_inverse):
    token_count, width = activations.shape
    out_width = output_grad.shape[1]
    zlo_count = lax.axis_size("zlo")
    heads = lax.axis_size("zhi")
    sites = lax.axis_size("x") * lax.axis_size("y")
    dp_count = zlo_count * sites * 2
    group = token_count // heads
    half = out_width // 2
    rows = width // sites
    inv_tokens = 1.0 / (token_count * dp_count)
    core = lax.axis_index("core")
    head = lax.axis_index("zhi")
    zlo = lax.axis_index("zlo")

    def swap_core(value):
        return shift(value, "core", 1)

    chunks = []
    for part in range(2):
        kept = lax.dynamic_slice_in_dim(output_grad, core * half + part * width, width, 1)
        given = lax.dynamic_slice_in_dim(output_grad, (1 - core) * half + part * width, width, 1)
        chunks.append(jnp.concatenate([kept, swap_core(given)], axis=0))
    other_act = swap_core(activations)

    pieces = []
    for part, chunk in enumerate(chunks):
        ahead = shift(chunk, "zhi", 1)
        back = shift(chunk, "zhi", -1)
        far = shift(ahead, "zhi", 1) if part == 0 else shift(back, "zhi", -1)
        pieces += [chunk, ahead, back, far]

    acts = []
    for offset in (0, heads - 1, 1, 2):
        start = lax.rem(head + offset, heads) * group
        mine = lax.dynamic_slice_in_dim(activations, start, group, 0)
        theirs = lax.dynamic_slice_in_dim(other_act, start, group, 0)
        acts.append(jnp.concatenate([mine, theirs], axis=0))

    does_grad = core == head // 2
    choice = jnp.where(does_grad, 1 + head % 2, 0).astype(jnp.int32).reshape(1)
    partial = partial_sums(choice, pieces, acts, inv_tokens, sites)
    got = plane_exchange(partial)
    share = jnp.sum(got.astype(F32), axis=0)
    share = share + shift(share, "zlo", 1)

    mixed = lax.dot_general(
        share[:2].reshape(2 * rows, width),
        act_inverse.astype(F32),
        (((1,), (1,)), ((), ())),
        precision=lax.Precision.HIGHEST,
    ).astype(BF16)
    copies = jnp.broadcast_to(mixed.reshape(1, 2, rows, width), (sites, 2, rows, width))
    mine = plane_exchange(copies).reshape(half, width)

    cov = share[2].reshape(zlo_count, 2, rows // 4, width)
    cov = lax.dynamic_index_in_dim(cov, zlo, 0, False)
    kept = lax.dynamic_index_in_dim(cov, core, 0, False)
    taken = swap_core(lax.dynamic_index_in_dim(cov, 1 - core, 0, False))
    act_perm, grad_perm = [], []
    for zl in range(zlo_count):
        for site in range(sites):
            for co in range(2):
                source = (zl * sites + site) * 2 + co
                place = (site * zlo_count + zl) * 2 + co
                act_perm.append((source, place))
                for hd in range(heads):
                    grad_perm.append((source * heads + hd, hd * dp_count + place))
    act_cov = lax.ppermute(jnp.where(does_grad, taken, kept), DP, act_perm)
    grad_cov = lax.ppermute(jnp.where(does_grad, kept, taken), EVERY, grad_perm)

    mine = after(mine, act_cov, grad_cov)
    theirs = swap_core(mine)
    inv_mine = lax.dynamic_slice_in_dim(grad_inverse, core * half, half, 0)
    inv_theirs = lax.dynamic_slice_in_dim(grad_inverse, (1 - core) * half, half, 0)
    out_mine, out_theirs, squares = right_product(mine, theirs, inv_mine, inv_theirs)

    own_sq = squares[0] + squares[1]
    sums = [own_sq] + [shift(own_sq, "zhi", step) for step in range(1, heads)]
    count = width * heads * out_width
    update = final_update(core.astype(jnp.int32).reshape(1), sums, (out_mine, out_theirs), count)
    return (act_cov, grad_cov, update)


def solution(mesh):
    fine = Mesh(mesh.devices.reshape(2, 4, 4, 2, 4), EVERY)
    return jax.shard_map(
        body,
        mesh=fine,
        in_specs=(P(DP, "zhi"), P(EVERY, None), P("zhi", None), P()),
        out_specs=(P(("zhi",) + DP, None), P(EVERY, None), P("zhi", None)),
        check_vma=False,
    )
```

time: 200 us -> 158 us (0.79); the launches traced: 198 us -> 158 us
  starting transfers between devices: 92.3 us -> 35 us
  blocking collectives: 0 us -> 36.6 us
  matrix products: 31.9 us -> 0.87 us
  waiting for transfers between devices: 50.5 us -> 67.1 us
  Pallas kernels: 0 us -> 10.5 us
  other arithmetic: 6.53 us -> 0.58 us
  local copies, waits for them, and re-layouts: 11.9 us -> 6.27 us
  between operations: 4.41 us -> 0.91 us
    all_to_all x0 -> x1, blocking collectives: none -> 36.6 us  [plane_exchange(): return lax.all_to_all(value, PLANE, split_axis=0, concat_axis=0, tiled=True)]
    dot_general x18 -> x1, matrix products: 31.9 us -> 0.87 us  [body(): lax.dot_general(share[:2].reshape(2 * rows, width), act_inverse.astype(F3...]
    ppermute x18 -> x15, starting transfers between devices: 49 us -> 21.3 us  [shift(): lax.ppermute(value, axis, [(i, (i + step) % count) for i in range(count)])]
    all_to_all x5 -> x1, starting transfers between devices: 33.1 us -> 6 us  [plane_exchange(): return lax.all_to_all(value, PLANE, split_axis=0, concat_axis=0, tiled=True)]
    ppermute x18 -> x15, waiting for transfers between devices: 35.6 us -> 53 us  [shift(): lax.ppermute(value, axis, [(i, (i + step) % count) for i in range(count)])]
    all_to_all x5 -> x1, waiting for transfers between devices: 14.9 us -> 0.01 us  [plane_exchange(): return lax.all_to_all(value, PLANE, split_axis=0, concat_axis=0, tiled=True)]
    ppermute x2, waiting for transfers between devices: 0.01 us -> 14.1 us  [the longest x1 8.88 us: body(): grad_cov = lax.ppermute(jnp.where(does_grad, kept, taken), EVERY, grad_perm)]
    pallas_call x0 -> x3, Pallas kernels: none -> 10.5 us  [the longest x1 3.67 us: partial_sums(): pl.pallas_call(functools.partial(partial_kernel, scale), out_shape=jax.Sh...]
  transfers between devices with their start and end apart: 25 -> 18, of which waited for: 14 -> 13; matrix products, arithmetic and copies ran while one was open for 16% -> 2% of each run, Pallas kernels for 0% -> 0%
where the time goes in v2:
time: 158 us
  waiting for transfers between devices  67.1 us (42%)
  blocking collectives  36.6 us (23%)
  starting transfers between devices  35 us (22%)
  Pallas kernels  10.5 us (7%)
  local copies, waits for them, and re-layouts  6.27 us (4%)
    ppermute x15, waiting for transfers between devices, shift(): lax.ppermute(value, axis, [(i, (i + step) % count) for i in range(count)])  53 us
    all_to_all x1, blocking collectives, plane_exchange(): return lax.all_to_all(value, PLANE, split_axis=0, concat_axis=0, tiled=True)  36.6 us
    ppermute x15, starting transfers between devices, shift(): lax.ppermute(value, axis, [(i, (i + step) % count) for i in range(count)])  21.3 us
    ppermute x1, waiting for transfers between devices, body(): grad_cov = lax.ppermute(jnp.where(does_grad, kept, taken), EVERY, grad_perm)  8.88 us
    all_to_all x1, starting transfers between devices, plane_exchange(): return lax.all_to_all(value, PLANE, split_axis=0, concat_axis=0, tiled=True)  6 us
    ppermute x1, starting transfers between devices, body(): grad_cov = lax.ppermute(jnp.where(does_grad, kept, taken), EVERY, grad_perm)  5.77 us
    ppermute x1, waiting for transfers between devices, body(): act_cov = lax.ppermute(jnp.where(does_grad, taken, kept), DP, act_perm)  5.18 us
    pallas_call x1, Pallas kernels, partial_sums(): pl.pallas_call(functools.partial(partial_kernel, scale), out_shape=jax.Sh...  3.67 us
  transfers between devices with their start and end apart: 18, of which 13 were waited for; matrix products, arithmetic and copies ran while one was open for 2% of the time, Pallas kernels for 0%

profile of v2, /device:TPU:6, one launch (start us, length us, event | category | flops | bytes accessed | tf_op | source)
XLA Modules:
  0.0 157.8 jit_solution(13385073516581525778)
XLA Ops:
  0.7 1.3 constant_dynamic-slice_fusion.11
  3.5 6.4 %collective-permute-start.6 = (bf16[256,640]{1,0:T(8,128)(2,1)S(1)}, bf16[256,640]{1,0:T(8,128)(2,1)S(1)}, u32[]{:S(2)}, u32[]{:S(2)}) collective-permute-start(bf16[256,640]{1,0:T(8,128)(2,1)S(1)} %pad_maximum_fusion.1.refs_4_), channel_id=1, source_target_pairs={{0,3},{1,0},{2,1},{3,2},{4,7},{5,4},{6,5},{7,6},{8,11},{9,8},{10,9... | collective-permute-start | bytes 983048 | tf_op jit(solution)/shard_map/ppermute | solution.py:22
  10.2 2.5 %collective-permute-start.5 = (bf16[256,640]{1,0:T(8,128)(2,1)S(1)}, bf16[256,640]{1,0:T(8,128)(2,1)S(1)}, u32[]{:S(2)}, u32[]{:S(2)}) collective-permute-start(bf16[256,640]{1,0:T(8,128)(2,1)S(1)} %pad_maximum_fusion.1.refs_4_), channel_id=1, source_target_pairs={{0,1},{1,2},{2,3},{3,0},{4,5},{5,6},{6,7},{7,4},{8,9},{9,10},{10,1... | collective-permute-start | bytes 983048 | tf_op jit(solution)/shard_map/ppermute | solution.py:22
  12.7 1.7 %collective-permute-start.2 = (bf16[256,640]{1,0:T(8,128)(2,1)S(1)}, bf16[256,640]{1,0:T(8,128)(2,1)S(1)}, u32[]{:S(2)}, u32[]{:S(2)}) collective-permute-start(bf16[256,640]{1,0:T(8,128)(2,1)S(1)} %pad_maximum_fusion.refs_0_), channel_id=1, source_target_pairs={{0,3},{1,0},{2,1},{3,2},{4,7},{5,4},{6,5},{7,6},{8,11},{9,8},{10,9... | collective-permute-start | bytes 983048 | tf_op jit(solution)/shard_map/ppermute | solution.py:22
  14.4 15.7 %collective-permute-done.6.refs_6_ = bf16[256,640]{1,0:T(8,128)(2,1)S(1)} collective-permute-done((bf16[256,640]{1,0:T(8,128)(2,1)S(1)}, bf16[256,640]{1,0:T(8,128)(2,1)S(1)}, u32[]{:S(2)}, u32[]{:S(2)}) %collective-permute-start.6) | collective-permute-done | bytes 327712 | tf_op jit(solution)/shard_map/ppermute | solution.py:22
  30.1 4.7 %collective-permute-start.7 = (bf16[256,640]{1,0:T(8,128)(2,1)S(1)}, bf16[256,640]{1,0:T(8,128)(2,1)S(1)}, u32[]{:S(2)}, u32[]{:S(2)}) collective-permute-start(bf16[256,640]{1,0:T(8,128)(2,1)S(1)} %collective-permute-done.6.refs_6_), channel_id=1, source_target_pairs={{0,3},{1,0},{2,1},{3,2},{4,7},{5,4},{6,5},{7,6},{8,11},{9,8},{10,9... | collective-permute-start | bytes 983048 | tf_op jit(solution)/shard_map/ppermute | solution.py:22
  35.0 2.9 %collective-permute-done.5.refs_5_ = bf16[256,640]{1,0:T(8,128)(2,1)S(1)} collective-permute-done((bf16[256,640]{1,0:T(8,128)(2,1)S(1)}, bf16[256,640]{1,0:T(8,128)(2,1)S(1)}, u32[]{:S(2)}, u32[]{:S(2)}) %collective-permute-start.5) | collective-permute-done | bytes 327712 | tf_op jit(solution)/shard_map/ppermute | solution.py:22
  38.0 5.5 %collective-permute-done.2.refs_2_ = bf16[256,640]{1,0:T(8,128)(2,1)S(1)} collective-permute-done((bf16[256,640]{1,0:T(8,128)(2,1)S(1)}, bf16[256,640]{1,0:T(8,128)(2,1)S(1)}, u32[]{:S(2)}, u32[]{:S(2)}) %collective-permute-start.2) | collective-permute-done | bytes 327712 | tf_op jit(solution)/shard_map/ppermute | solution.py:22
  43.5 8.8 %collective-permute-done.7.refs_7_ = bf16[256,640]{1,0:T(8,128)(2,1)S(1)} collective-permute-done((bf16[256,640]{1,0:T(8,128)(2,1)S(1)}, bf16[256,640]{1,0:T(8,128)(2,1)S(1)}, u32[]{:S(2)}, u32[]{:S(2)}) %collective-permute-start.7) | collective-permute-done | bytes 327712 | tf_op jit(solution)/shard_map/ppermute | solution.py:22
  52.3 4.0 %collective-permute-done.3.refs_3_ = bf16[256,640]{1,0:T(8,128)(2,1)S(1)} collective-permute-done((bf16[256,640]{1,0:T(8,128)(2,1)S(1)}, bf16[256,640]{1,0:T(8,128)(2,1)S(1)}, u32[]{:S(2)}, u32[]{:S(2)}) %collective-permute-start.3) | collective-permute-done | bytes 327712 | tf_op jit(solution)/shard_map/ppermute | solution.py:22
  56.3 3.7 %partial_sums.1 = bf16[16,3,40,640]{3,2,1,0:T(8,128)(2,1)S(1)} custom-call(s32[1]{0:T(128)} %bitcast.choice, bf16[256,640]{1,0:T(8,128)(2,1)S(1)} %pad_maximum_fusion.refs_0_, bf16[256,640]{1,0:T(8,128)(2,1)S(1)} %collective-permute-done.1.refs_1_, bf16[256,640]{1,0:T(8,128)(2,1)S(1)} %collective-permute-done.2.refs_2_, ...), custom_call_target="tpu_custom_call" | custom-call | flops 2516582400 | bytes 8388608 | tf_op jit(solution)/shard_map/partial_sums/pallas_call | solution.py:60
  60.0 36.6 %all_to_all.10 = bf16[16,3,40,640]{3,2,1,0:T(8,128)(2,1)S(1)} all-to-all(bf16[16,3,40,640]{3,2,1,0:T(8,128)(2,1)S(1)} %partial_sums.1), channel_id=1, replica_groups=mesh['zlo'=2,'x'=4,'y'=4,'core'=2,'zhi'=4] {'x','y'}, dimensions={0} | all-to-all | bytes 4915200 | tf_op jit(solution)/shard_map/all_to_all | solution.py:134
  97.1 7.3 %collective-permute-done.9 = f32[3,40,640]{2,1,0:T(8,128)S(1)} collective-permute-done((f32[3,40,640]{2,1,0:T(8,128)S(1)}, f32[3,40,640]{2,1,0:T(8,128)S(1)}, u32[]{:S(2)}, u32[]{:S(2)}) %collective-permute-start.9) | collective-permute-done | bytes 307232 | tf_op jit(solution)/shard_map/ppermute | solution.py:22
  106.6 6.0 %all-to-all-start.1 = ((bf16[16,2,40,640]{3,2,1,0:T(8,128)(2,1)}), bf16[16,2,40,640]{3,2,1,0:T(8,128)(2,1)S(1)}, u32[]{:S(2)}, u32[]{:S(2)}) async-start(bf16[16,2,40,640]{3,2,1,0:T(8,128)(2,1)} %broadcast_in_dim.8), calls=%async_computation.1 | async-start | bytes 3276800 | tf_op jit(solution)/shard_map/all_to_all | solution.py:134
  114.0 5.8 %collective-permute-start.12 = (f32[10,640]{1,0:T(8,128)S(1)}, f32[10,640]{1,0:T(8,128)S(1)}, u32[]{:S(2)}, u32[]{:S(2)}) collective-permute-start(f32[10,640]{1,0:T(8,128)S(1)} %get-tuple-element.25), channel_id=1, source_target_pairs={{0,0},{1,64},{2,128},{3,192},{4,1},{5,65},{6,129},{7,193},{8,4},{9... | collective-permute-start | bytes 76808 | tf_op jit(solution)/shard_map/ppermute | solution.py:206
  119.7 1.9 %collective-permute-start.11 = (f32[10,640]{1,0:T(8,128)S(1)}, f32[10,640]{1,0:T(8,128)S(1)}, u32[]{:S(2)}, u32[]{:S(2)}) collective-permute-start(f32[10,640]{1,0:T(8,128)S(1)} %get-tuple-element.26), channel_id=1, source_target_pairs={{0,0},{4,4},{8,16},{12,20},{16,32},{20,36},{24,48},{28,52},{32,64}... | collective-permute-start | bytes 76808 | tf_op jit(solution)/shard_map/ppermute | solution.py:205
  121.7 8.9 %collective-permute-done.12 = f32[10,640]{1,0:T(8,128)S(1)} collective-permute-done((f32[10,640]{1,0:T(8,128)S(1)}, f32[10,640]{1,0:T(8,128)S(1)}, u32[]{:S(2)}, u32[]{:S(2)}) %collective-permute-start.12) | collective-permute-done | bytes 25632 | tf_op jit(solution)/shard_map/ppermute | solution.py:206
  130.6 5.2 %collective-permute-done.11 = f32[10,640]{1,0:T(8,128)S(1)} collective-permute-done((f32[10,640]{1,0:T(8,128)S(1)}, f32[10,640]{1,0:T(8,128)S(1)}, u32[]{:S(2)}, u32[]{:S(2)}) %collective-permute-start.11) | collective-permute-done | bytes 25632 | tf_op jit(solution)/shard_map/ppermute | solution.py:205
  135.7 2.2 %constant_dynamic-slice_fusion = (bf16[1280,640]{1,0:T(8,128)(2,1)S(1)}, bf16[1280,640]{1,0:T(8,128)(2,1)S(1)}) fusion(bf16[2560,640]{1,0:T(8,128)(2,1)} %param.7, s32[]{:T(128)S(6)} %select_n.79, s32[]{:T(128)S(6)} %select_n.78), kind=kLoop, calls=%fused_computation.12 | loop fusion | bytes 6553608 | tf_op jit(solution)/shard_map/dynamic_slice | solution.py:211
  139.2 3.6 %right_product.1 = (f32[2,640,640]{2,1,0:T(8,128)S(1)}, f32[2,640,640]{2,1,0:T(8,128)S(1)}, f32[2,8,128]{2,1,0:T(8,128)S(1)}) custom-call(bf16[1280,640]{1,0:T(8,128)(2,1)S(1)} %bitcast.15, bf16[1280,640]{1,0:T(8,128)(2,1)S(1)} %collective-permute-done.13.theirs, bf16[1280,640]{1,0:T(8,128)(2,1)S(1)} %get-tuple-element.12.inv_mine, ...), custom_call_target="tpu_custom_call" | custom-call | flops 2097152000 | bytes 12582912 | tf_op jit(solution)/shard_map/right_product/pallas_call | solution.py:86
  142.8 1.8 %collective-permute-start.16 = (f32[8,128]{1,0:T(8,128)S(1)}, f32[8,128]{1,0:T(8,128)S(1)}, u32[]{:S(2)}, u32[]{:S(2)}) collective-permute-start(f32[8,128]{1,0:T(8,128)S(1)} %add_bitcast_fusion.own), channel_id=1, source_target_pairs={{0,3},{1,0},{2,1},{3,2},{4,7},{5,4},{6,5},{7,6},{8,11},{9,8},{10,9... | collective-permute-start | bytes 12296 | tf_op jit(solution)/shard_map/ppermute | solution.py:22
  144.6 3.0 %collective-permute-start.15 = (f32[8,128]{1,0:T(8,128)S(1)}, f32[8,128]{1,0:T(8,128)S(1)}, u32[]{:S(2)}, u32[]{:S(2)}) collective-permute-start(f32[8,128]{1,0:T(8,128)S(1)} %add_bitcast_fusion.own), channel_id=1, source_target_pairs={{0,2},{1,3},{2,0},{3,1},{4,6},{5,7},{6,4},{7,5},{8,10},{9,11},{10,... | collective-permute-start | bytes 12296 | tf_op jit(solution)/shard_map/ppermute | solution.py:22
  147.8 4.3 %collective-permute-done.15.sq_b = f32[8,128]{1,0:T(8,128)S(1)} collective-permute-done((f32[8,128]{1,0:T(8,128)S(1)}, f32[8,128]{1,0:T(8,128)S(1)}, u32[]{:S(2)}, u32[]{:S(2)}) %collective-permute-start.15) | collective-permute-done | bytes 4128 | tf_op jit(solution)/shard_map/ppermute | solution.py:22
  153.4 3.3 %final_update.1 = bf16[640,2560]{1,0:T(8,128)(2,1)} custom-call(s32[1]{0:T(128)} %bitcast.3.core, f32[8,128]{1,0:T(8,128)S(1)} %add_bitcast_fusion.own, f32[8,128]{1,0:T(8,128)S(1)} %collective-permute-done.14.sq_a, f32[8,128]{1,0:T(8,128)S(1)} %collective-permute-done.15.sq_b, f32[8,128]{1,0:T(8,128)S(1)} %collective-permute-done.16.sq_c, ...), custom_call_target="tpu_custom_call" | custom-call | flops 1638400 | bytes 10485760 | tf_op jit(solution)/shard_map/final_update/pallas_call | solution.py:121
  (40 shorter events, 9.9 us)
Async XLA Ops:
  0.6 103.8 %copy-start = (bf16[640,640]{1,0:T(8,128)(2,1)S(1)}, bf16[640,640]{1,0:T(8,128)(2,1)}, u32[]{:S(2)}) copy-start(bf16[640,640]{1,0:T(8,128)(2,1)} %param.6) | copy-start | bytes 2457604
  0.6 9.4 %copy-start.1 = (bf16[512,640]{1,0:T(8,128)(2,1)S(1)}, bf16[512,640]{1,0:T(8,128)(2,1)}, u32[]{:S(2)}) copy-start(bf16[512,640]{1,0:T(8,128)(2,1)} %param.4) | copy-start | bytes 1966084
  2.0 1.5 collective-permute-start.4
  2.1 32.7 %collective-permute-start.8 = (bf16[512,640]{1,0:T(8,128)(2,1)}, bf16[512,640]{1,0:T(8,128)(2,1)S(1)}, u32[]{:S(2)}, u32[]{:S(2)}) collective-permute-start(bf16[512,640]{1,0:T(8,128)(2,1)} %param.4), channel_id=1, source_target_pairs={{0,4},{4,0},{1,5},{5,1},{2,6},{6,2},{3,7},{7,3},{8,12},{12,8},{9,1... | collective-permute-start | bytes 1966088 | tf_op jit(solution)/shard_map/ppermute | solution.py:22
  2.6 7.3 %collective-permute-start = (bf16[128,640]{1,0:T(8,128)(2,1)S(1)}, bf16[128,640]{1,0:T(8,128)(2,1)S(1)}, u32[]{:S(2)}, u32[]{:S(2)}) collective-permute-start(bf16[128,640]{1,0:T(8,128)(2,1)S(1)} %get-tuple-element.22), channel_id=1, source_target_pairs={{0,4},{4,0},{1,5},{5,1},{2,6},{6,2},{3,7},{7,3},{8,12},{12,8},{9,1... | collective-permute-start | bytes 491528 | tf_op jit(solution)/shard_map/ppermute | solution.py:22
  3.5 26.5 %collective-permute-start.6 = (bf16[256,640]{1,0:T(8,128)(2,1)S(1)}, bf16[256,640]{1,0:T(8,128)(2,1)S(1)}, u32[]{:S(2)}, u32[]{:S(2)}) collective-permute-start(bf16[256,640]{1,0:T(8,128)(2,1)S(1)} %pad_maximum_fusion.1.refs_4_), channel_id=1, source_target_pairs={{0,3},{1,0},{2,1},{3,2},{4,7},{5,4},{6,5},{7,6},{8,11},{9,8},{10,9... | collective-permute-start | bytes 983048 | tf_op jit(solution)/shard_map/ppermute | solution.py:22
  9.9 24.9 %collective-permute-start.1 = (bf16[256,640]{1,0:T(8,128)(2,1)S(1)}, bf16[256,640]{1,0:T(8,128)(2,1)S(1)}, u32[]{:S(2)}, u32[]{:S(2)}) collective-permute-start(bf16[256,640]{1,0:T(8,128)(2,1)S(1)} %pad_maximum_fusion.refs_0_), channel_id=1, source_target_pairs={{0,1},{1,2},{2,3},{3,0},{4,5},{5,6},{6,7},{7,4},{8,9},{9,10},{10,1... | collective-permute-start | bytes 983048 | tf_op jit(solution)/shard_map/ppermute | solution.py:22
  10.2 27.8 %collective-permute-start.5 = (bf16[256,640]{1,0:T(8,128)(2,1)S(1)}, bf16[256,640]{1,0:T(8,128)(2,1)S(1)}, u32[]{:S(2)}, u32[]{:S(2)}) collective-permute-start(bf16[256,640]{1,0:T(8,128)(2,1)S(1)} %pad_maximum_fusion.1.refs_4_), channel_id=1, source_target_pairs={{0,1},{1,2},{2,3},{3,0},{4,5},{5,6},{6,7},{7,4},{8,9},{9,10},{10,1... | collective-permute-start | bytes 983048 | tf_op jit(solution)/shard_map/ppermute | solution.py:22
  12.7 30.8 %collective-permute-start.2 = (bf16[256,640]{1,0:T(8,128)(2,1)S(1)}, bf16[256,640]{1,0:T(8,128)(2,1)S(1)}, u32[]{:S(2)}, u32[]{:S(2)}) collective-permute-start(bf16[256,640]{1,0:T(8,128)(2,1)S(1)} %pad_maximum_fusion.refs_0_), channel_id=1, source_target_pairs={{0,3},{1,0},{2,1},{3,2},{4,7},{5,4},{6,5},{7,6},{8,11},{9,8},{10,9... | collective-permute-start | bytes 983048 | tf_op jit(solution)/shard_map/ppermute | solution.py:22
  30.1 22.3 %collective-permute-start.7 = (bf16[256,640]{1,0:T(8,128)(2,1)S(1)}, bf16[256,640]{1,0:T(8,128)(2,1)S(1)}, u32[]{:S(2)}, u32[]{:S(2)}) collective-permute-start(bf16[256,640]{1,0:T(8,128)(2,1)S(1)} %collective-permute-done.6.refs_6_), channel_id=1, source_target_pairs={{0,3},{1,0},{2,1},{3,2},{4,7},{5,4},{6,5},{7,6},{8,11},{9,8},{10,9... | collective-permute-start | bytes 983048 | tf_op jit(solution)/shard_map/ppermute | solution.py:22
  34.8 21.5 %collective-permute-start.3 = (bf16[256,640]{1,0:T(8,128)(2,1)S(1)}, bf16[256,640]{1,0:T(8,128)(2,1)S(1)}, u32[]{:S(2)}, u32[]{:S(2)}) collective-permute-start(bf16[256,640]{1,0:T(8,128)(2,1)S(1)} %collective-permute-done.1.refs_1_), channel_id=1, source_target_pairs={{0,1},{1,2},{2,3},{3,0},{4,5},{5,6},{6,7},{7,4},{8,9},{9,10},{10,1... | collective-permute-start | bytes 983048 | tf_op jit(solution)/shard_map/ppermute | solution.py:22
  97.0 7.4 %collective-permute-start.9 = (f32[3,40,640]{2,1,0:T(8,128)S(1)}, f32[3,40,640]{2,1,0:T(8,128)S(1)}, u32[]{:S(2)}, u32[]{:S(2)}) collective-permute-start(f32[3,40,640]{2,1,0:T(8,128)S(1)} %convert_reduce_fusion), channel_id=1, source_target_pairs={{0,128},{128,0},{1,129},{129,1},{2,130},{130,2},{3,131},{131,3},{4... | collective-permute-start | bytes 921608 | tf_op jit(solution)/shard_map/ppermute | solution.py:22
  106.6 29.2 %all-to-all-start.1 = ((bf16[16,2,40,640]{3,2,1,0:T(8,128)(2,1)}), bf16[16,2,40,640]{3,2,1,0:T(8,128)(2,1)S(1)}, u32[]{:S(2)}, u32[]{:S(2)}) async-start(bf16[16,2,40,640]{3,2,1,0:T(8,128)(2,1)} %broadcast_in_dim.8), calls=%async_computation.1 | async-start | bytes 3276800 | tf_op jit(solution)/shard_map/all_to_all | solution.py:134
  112.6 1.3 collective-permute-start.10
  114.0 16.6 %collective-permute-start.12 = (f32[10,640]{1,0:T(8,128)S(1)}, f32[10,640]{1,0:T(8,128)S(1)}, u32[]{:S(2)}, u32[]{:S(2)}) collective-permute-start(f32[10,640]{1,0:T(8,128)S(1)} %get-tuple-element.25), channel_id=1, source_target_pairs={{0,0},{1,64},{2,128},{3,192},{4,1},{5,65},{6,129},{7,193},{8,4},{9... | collective-permute-start | bytes 76808 | tf_op jit(solution)/shard_map/ppermute | solution.py:206
  119.7 16.0 %collective-permute-start.11 = (f32[10,640]{1,0:T(8,128)S(1)}, f32[10,640]{1,0:T(8,128)S(1)}, u32[]{:S(2)}, u32[]{:S(2)}) collective-permute-start(f32[10,640]{1,0:T(8,128)S(1)} %get-tuple-element.26), channel_id=1, source_target_pairs={{0,0},{4,4},{8,16},{12,20},{16,32},{20,36},{24,48},{28,52},{32,64}... | collective-permute-start | bytes 76808 | tf_op jit(solution)/shard_map/ppermute | solution.py:205
  135.7 3.5 %collective-permute-start.13 = (bf16[1280,640]{1,0:T(8,128)(2,1)S(1)}, bf16[1280,640]{1,0:T(8,128)(2,1)S(1)}, u32[]{:S(2)}, u32[]{:S(2)}) collective-permute-start(bf16[1280,640]{1,0:T(8,128)(2,1)S(1)} %bitcast.14), channel_id=1, source_target_pairs={{0,4},{4,0},{1,5},{5,1},{2,6},{6,2},{3,7},{7,3},{8,12},{12,8},{9,1... | collective-permute-start | bytes 4915208 | tf_op jit(solution)/shard_map/ppermute | solution.py:22
  142.8 5.0 %collective-permute-start.16 = (f32[8,128]{1,0:T(8,128)S(1)}, f32[8,128]{1,0:T(8,128)S(1)}, u32[]{:S(2)}, u32[]{:S(2)}) collective-permute-start(f32[8,128]{1,0:T(8,128)S(1)} %add_bitcast_fusion.own), channel_id=1, source_target_pairs={{0,3},{1,0},{2,1},{3,2},{4,7},{5,4},{6,5},{7,6},{8,11},{9,8},{10,9... | collective-permute-start | bytes 12296 | tf_op jit(solution)/shard_map/ppermute | solution.py:22
  144.6 7.5 %collective-permute-start.15 = (f32[8,128]{1,0:T(8,128)S(1)}, f32[8,128]{1,0:T(8,128)S(1)}, u32[]{:S(2)}, u32[]{:S(2)}) collective-permute-start(f32[8,128]{1,0:T(8,128)S(1)} %add_bitcast_fusion.own), channel_id=1, source_target_pairs={{0,2},{1,3},{2,0},{3,1},{4,6},{5,7},{6,4},{7,5},{8,10},{9,11},{10,... | collective-permute-start | bytes 12296 | tf_op jit(solution)/shard_map/ppermute | solution.py:22
  147.6 5.7 %collective-permute-start.14 = (f32[8,128]{1,0:T(8,128)S(1)}, f32[8,128]{1,0:T(8,128)S(1)}, u32[]{:S(2)}, u32[]{:S(2)}) collective-permute-start(f32[8,128]{1,0:T(8,128)S(1)} %add_bitcast_fusion.own), channel_id=1, source_target_pairs={{0,1},{1,2},{2,3},{3,0},{4,5},{5,6},{6,7},{7,4},{8,9},{9,10},{10,1... | collective-permute-start | bytes 12296 | tf_op jit(solution)/shard_map/ppermute | solution.py:22

commit v3 on v2

v3 whole, which is shorter than its diff:
```python
import functools

import jax
import jax.numpy as jnp
from jax import lax
from jax.experimental import pallas as pl
from jax.experimental.pallas import tpu as pltpu
from jax.sharding import Mesh, PartitionSpec as P

DP = ("zlo", "x", "y", "core")
EVERY = DP + ("zhi",)
PLANE = ("x", "y")
BF16 = jnp.bfloat16
F32 = jnp.float32
LIMIT_MB = 16
LIMIT = pltpu.CompilerParams(vmem_limit_bytes=LIMIT_MB * 1024 * 1024)
VMEM = pl.BlockSpec(memory_space=pltpu.VMEM)
SMEM = pl.BlockSpec(memory_space=pltpu.SMEM)


def shift(value, axis, step):
    count = lax.axis_size(axis)
    return lax.ppermute(value, axis, [(i, (i + step) % count) for i in range(count)])


def after(value, *earlier):
    return lax.optimization_barrier((value,) + earlier)[0]


def token_dot(lhs, rhs):
    return lax.dot_general(lhs, rhs, (((0,), (0,)), ((), ())), preferred_element_type=F32)


def cost(flops, mib):
    return pl.CostEstimate(flops=flops, bytes_accessed=mib * 2**20, transcendentals=0)


def early_kernel(scale, *refs):
    pieces, acts, out = refs[:6], refs[6:9], refs[9]
    for part in range(2):
        total = sum(token_dot(pieces[3 * part + k][...], acts[k][...]) for k in range(3))
        out[part] = total * scale


def early_partial(pieces, acts, scale):
    width = acts[0].shape[1]
    return pl.pallas_call(
        functools.partial(early_kernel, scale),
        out_shape=jax.ShapeDtypeStruct((2, width, width), F32),
        in_specs=[VMEM] * 9,
        out_specs=VMEM,
        compiler_params=LIMIT,
        cost_estimate=cost(3 * 1024 * width * width, 6),
        name="early_partial",
    )(*pieces, *acts)


def weight_kernel(scale, early, first, second, act, out):
    rows = out.shape[1]
    for part, piece in enumerate((first, second)):
        total = early[part] + token_dot(piece[...], act[...]) * scale
        count = total.shape[0] // rows
        for index in range(count):
            out[part * count + index] = total[index * rows : (index + 1) * rows].astype(BF16)


def weight_partial(early, first, second, act, scale, sites):
    width = act.shape[1]
    return pl.pallas_call(
        functools.partial(weight_kernel, scale),
        out_shape=jax.ShapeDtypeStruct((sites, 2 * width // sites, width), BF16),
        in_specs=[VMEM] * 4,
        out_specs=VMEM,
        compiler_params=LIMIT,
        cost_estimate=cost(1024 * width * width, 6),
        name="weight_partial",
    )(early, first, second, act)


def cov_kernel(scale, first, second, acts, out):
    rows = out.shape[2]
    for slab, tokens in enumerate((first, second, acts)):
        value = tokens[...]
        total = token_dot(value, value)
        for index in range(out.shape[0]):
            out[index, slab] = (total[index * rows : (index + 1) * rows] * scale).astype(BF16)


def cov_partial(first, second, acts, scale, sites):
    width = acts.shape[1]
    return pl.pallas_call(
        functools.partial(cov_kernel, scale),
        out_shape=jax.ShapeDtypeStruct((sites, 3, width // sites, width), BF16),
        in_specs=[VMEM] * 3,
        out_specs=VMEM,
        compiler_params=LIMIT,
        cost_estimate=cost(2 * 1024 * width * width, 5),
        name="cov_partial",
    )(first, second, acts)


def right_kernel(half_index, left, inverse, out, squares):
    width = left.shape[1]
    total = 0.0
    for part in range(2):
        start = pl.multiple_of((2 * half_index[0] + part) * width, width)
        result = token_dot(left[part * width : (part + 1) * width, :], inverse[pl.ds(start, width), :])
        out[part] = result
        total = total + jnp.sum(result * result)
    squares[...] = jnp.broadcast_to(total, squares.shape)


def right_product(half_index, left, inverse):
    width = left.shape[1]
    return pl.pallas_call(
        right_kernel,
        out_shape=(jax.ShapeDtypeStruct((2, width, width), F32), jax.ShapeDtypeStruct((8, 128), F32)),
        in_specs=[SMEM, VMEM, VMEM],
        out_specs=(VMEM, VMEM),
        compiler_params=LIMIT,
        cost_estimate=cost(4 * width**3, 6),
        name="right_product",
    )(half_index, left, inverse)


def final_kernel(count, core, own, sq_a, sq_b, sq_c, act_rows, grad_rows, mine, theirs, out, act_out, grad_out):
    total = own[...] + sq_a[...] + sq_b[...] + sq_c[...]
    scale = lax.rsqrt(total / count + 1e-06)[0:1, 0:1]
    width = mine.shape[2]
    rows = out.shape[0]
    place = pl.ds(pl.multiple_of(pl.program_id(0) * rows, rows), rows)
    act_out[...] = act_rows[...]
    grad_out[...] = grad_rows[...]

    def write(first, second):
        for index in range(4):
            block = (first, second)[index // 2][index % 2, place]
            out[:, index * width : (index + 1) * width] = (block * scale).astype(BF16)

    @pl.when(core[0] == 0)
    def _():
        write(mine, theirs)

    @pl.when(core[0] != 0)
    def _():
        write(theirs, mine)


def final_update(core, sums, cov_rows, blocks, count):
    width = blocks[0].shape[1]
    rows = width // 5
    small = pl.BlockSpec((8, 128), lambda i: (0, 0))
    cov = pl.BlockSpec(cov_rows[0].shape, lambda i: (0, 0))
    cov_type = jax.ShapeDtypeStruct(cov_rows[0].shape, F32)
    return pl.pallas_call(
        functools.partial(final_kernel, count),
        grid=(5,),
        out_shape=(jax.ShapeDtypeStruct((width, 4 * width), BF16), cov_type, cov_type),
        in_specs=[SMEM] + [small] * 4 + [cov] * 2 + [VMEM] * 2,
        out_specs=(pl.BlockSpec((rows, 4 * width), lambda i: (i, 0)), cov, cov),
        compiler_params=LIMIT,
        cost_estimate=cost(4 * width * width, 10),
        name="final_update",
    )(core, *sums, *cov_rows, *blocks)


def plane_exchange(value):
    return lax.all_to_all(value, PLANE, split_axis=0, concat_axis=0, tiled=True)


def body(activations, output_grad, act_inverse, grad_inverse):
    token_count, width = activations.shape
    out_width = output_grad.shape[1]
    zlo_count = lax.axis_size("zlo")
    heads = lax.axis_size("zhi")
    sites = lax.axis_size("x") * lax.axis_size("y")
    dp_count = zlo_count * sites * 2
    group = token_count // heads
    half = out_width // 2
    rows = width // sites
    inv_tokens = 1.0 / (token_count * dp_count)
    core = lax.axis_index("core")
    head = lax.axis_index("zhi")

    def swap_core(value):
        return shift(value, "core", 1)

    chunks = []
    for part in range(2):
        kept = lax.dynamic_slice_in_dim(output_grad, core * half + part * width, width, 1)
        given = lax.dynamic_slice_in_dim(output_grad, (1 - core) * half + part * width, width, 1)
        chunks.append(jnp.concatenate([kept, swap_core(given)], axis=0))

    other_act = swap_core(activations)
    pieces = []
    for part, chunk in enumerate(chunks):
        ahead = shift(chunk, "zhi", 1)
        back = shift(chunk, "zhi", -1)
        far = shift(ahead, "zhi", 1) if part == 0 else shift(back, "zhi", -1)
        pieces += [chunk, ahead, back, far]

    acts = []
    for offset in (0, heads - 1, 1, 2):
        start = lax.rem(head + offset, heads) * group
        mine = lax.dynamic_slice_in_dim(activations, start, group, 0)
        theirs = lax.dynamic_slice_in_dim(other_act, start, group, 0)
        acts.append(jnp.concatenate([mine, theirs], axis=0))

    cov_sent = cov_partial(after(chunks[0], other_act), chunks[1], activations, inv_tokens, sites)
    cov_got = plane_exchange(cov_sent)
    cov = jnp.sum(cov_got.astype(F32), axis=0)

    def split(value, axis, index):
        place = lax.axis_index(axis)
        kept = lax.dynamic_index_in_dim(value, place, index, False)
        return kept, lax.dynamic_index_in_dim(value, 1 - place, index, False)

    grad_kept, grad_given = split(cov[:2], "zlo", 0)
    act_kept, act_given = split(cov[2].reshape(2, rows // 2, width), "zlo", 0)
    taken = shift(jnp.concatenate([grad_given, act_given], axis=0), "zlo", 1)
    grad_part = (grad_kept + taken[:rows]).reshape(heads, rows // heads, width)
    act_kept, act_given = split((act_kept + taken[rows:]).reshape(2, rows // 4, width), "core", 0)
    grad_rows = lax.dynamic_index_in_dim(grad_part, head, 0, False)
    for step in range(1, heads):
        given = lax.dynamic_index_in_dim(grad_part, lax.rem(head + step, heads), 0, False)
        grad_rows = grad_rows + shift(given, "zhi", step)
    act_rows = act_kept + swap_core(act_given)
    act_perm, grad_perm = [], []
    for zl in range(zlo_count):
        for site in range(sites):
            for co in range(2):
                source = (zl * sites + site) * 2 + co
                act_perm.append((source, (site * zlo_count + zl) * 2 + co))
                grad_perm.append((source, (co * 2 + zl) * sites + site))

    early = early_partial(pieces[:3] + pieces[4:7], acts[:3], inv_tokens)
    got = plane_exchange(weight_partial(early, pieces[3], pieces[7], acts[3], inv_tokens, sites))
    got = after(got, act_rows, grad_rows)
    share = jnp.sum(got.astype(F32), axis=0)
    mixed = lax.dot_general(
        share + shift(share, "zlo", 1),
        act_inverse.astype(F32),
        (((1,), (1,)), ((), ())),
        precision=lax.Precision.HIGHEST,
    ).astype(BF16)
    copies = jnp.broadcast_to(mixed[None], (sites, 2 * rows, width))
    mine = plane_exchange(copies).reshape(half, width)
    act_rows = lax.ppermute(act_rows, DP, act_perm)
    grad_rows = lax.ppermute(grad_rows, DP, grad_perm)

    mine = after(mine, act_rows, grad_rows)
    theirs = swap_core(mine)
    order = core.astype(jnp.int32).reshape(1)
    out_mine, sq_mine = right_product(order, mine, grad_inverse)
    out_theirs, sq_theirs = right_product(1 - order, theirs, grad_inverse)

    own_sq = sq_mine + sq_theirs
    sums = [own_sq] + [shift(own_sq, "zhi", step) for step in range(1, heads)]
    count = width * heads * out_width
    update, act_cov, grad_cov = final_update(order, sums, (act_rows, grad_rows), (out_mine, out_theirs), count)
    return (act_cov, grad_cov, update)


def solution(mesh):
    fine = Mesh(mesh.devices.reshape(2, 4, 4, 2, 4), EVERY)
    return jax.shard_map(
        body,
        mesh=fine,
        in_specs=(P(DP, "zhi"), P(EVERY, None), P("zhi", None), P()),
        out_specs=(P(("zhi",) + DP, None), P(EVERY, None), P("zhi", None)),
        check_vma=False,
    )
```

time: 158 us -> 153 us (0.968)
  blocking collectives: 36.6 us -> 0 us
  starting transfers between devices: 35 us -> 62.3 us
  Pallas kernels: 10.5 us -> 13.5 us
  other arithmetic: 0.58 us -> 2.55 us
    all_to_all x1 -> x0, blocking collectives: 36.6 us -> none  [plane_exchange(): return lax.all_to_all(value, PLANE, split_axis=0, concat_axis=0, tiled=True)]
    all_to_all x1 -> x3, starting transfers between devices: 6 us -> 21.1 us  [plane_exchange(): return lax.all_to_all(value, PLANE, split_axis=0, concat_axis=0, tiled=True)]
    ppermute x15 -> x19, starting transfers between devices: 21.3 us -> 31.5 us  [shift(): lax.ppermute(value, axis, [(i, (i + step) % count) for i in range(count)])]
    pallas_call x2 -> x5, Pallas kernels: 7.24 us -> 10.5 us  [the longest x2 4.22 us: right_product(): pl.pallas_call(right_kernel, out_shape=(jax.ShapeDtypeStruct((2, width, w...]
    dynamic_slice x1 -> x0, local copies, waits for them, and re-layouts: 2.21 us -> none  [body(): lax.dynamic_slice_in_dim(grad_inverse, (1 - core) * half, half, 0)]
    reduce_sum x0 -> x1, other arithmetic: none -> 2.07 us  [body(): cov = jnp.sum(cov_got.astype(F32), axis=0)]
    ppermute x2, starting transfers between devices: 7.69 us -> 9.74 us  [the longest x1 5.95 us: body(): grad_rows = lax.ppermute(grad_rows, DP, grad_perm)]
    ppermute x2, waiting for transfers between devices: 14.1 us -> 12.2 us  [the longest x1 12.2 us: body(): act_rows = lax.ppermute(act_rows, DP, act_perm)]
  transfers between devices with their start and end apart: 18 -> 24, of which waited for: 13 -> 15; matrix products, arithmetic and copies ran while one was open for 2% -> 3% of each run, Pallas kernels for 0% -> 4%
where the time goes in v3:
time: 153 us; the launch traced here: 152 us
  waiting for transfers between devices  66.7 us (44%)
  starting transfers between devices  62.3 us (41%)
  Pallas kernels  13.5 us (9%)
  local copies, waits for them, and re-layouts  4.84 us (3%)
  other arithmetic  2.55 us (2%)
    ppermute x19, waiting for transfers between devices, shift(): lax.ppermute(value, axis, [(i, (i + step) % count) for i in range(count)])  53.8 us
    ppermute x19, starting transfers between devices, shift(): lax.ppermute(value, axis, [(i, (i + step) % count) for i in range(count)])  31.5 us
    all_to_all x3, starting transfers between devices, plane_exchange(): return lax.all_to_all(value, PLANE, split_axis=0, concat_axis=0, tiled=True)  21.1 us
    ppermute x1, waiting for transfers between devices, body(): act_rows = lax.ppermute(act_rows, DP, act_perm)  12.2 us
    ppermute x1, starting transfers between devices, body(): grad_rows = lax.ppermute(grad_rows, DP, grad_perm)  5.95 us
    pallas_call x2, Pallas kernels, right_product(): pl.pallas_call(right_kernel, out_shape=(jax.ShapeDtypeStruct((2, width, w...  4.22 us
    ppermute x1, starting transfers between devices, body(): act_rows = lax.ppermute(act_rows, DP, act_perm)  3.78 us
  transfers between devices with their start and end apart: 24, of which 15 were waited for; matrix products, arithmetic and copies ran while one was open for 3% of the time, Pallas kernels for 4%

profile of v3, /device:TPU:6, one launch (start us, length us, event | category | flops | bytes accessed | tf_op | source)
XLA Modules:
  0.0 151.7 jit_solution(879352514432261735)
XLA Ops:
  4.0 2.7 %cov_partial.1 = bf16[16,3,40,640]{3,2,1,0:T(8,128)(2,1)} custom-call(bf16[256,640]{1,0:T(8,128)(2,1)S(1)} %pad_maximum_fusion.refs_0_.first, bf16[256,640]{1,0:T(8,128)(2,1)S(1)} %pad_maximum_fusion.1.refs_3_.second, bf16[512,640]{1,0:T(8,128)(2,1)S(1)} %copy-done.3), custom_call_target="tpu_custom_call" | custom-call | flops 838860800 | bytes 5242880 | tf_op jit(solution)/shard_map/cov_partial/pallas_call | solution.py:91
  6.7 7.4 %all-to-all-start.1 = ((bf16[16,3,40,640]{3,2,1,0:T(8,128)(2,1)}), bf16[16,3,40,640]{3,2,1,0:T(8,128)(2,1)}, u32[]{:S(2)}, u32[]{:S(2)}) async-start(bf16[16,3,40,640]{3,2,1,0:T(8,128)(2,1)} %cov_partial.1), calls=%async_computation.1 | async-start | bytes 4915200 | tf_op jit(solution)/shard_map/all_to_all | solution.py:168
  14.1 6.3 %collective-permute-start.5 = (bf16[256,640]{1,0:T(8,128)(2,1)S(1)}, bf16[256,640]{1,0:T(8,128)(2,1)S(1)}, u32[]{:S(2)}, u32[]{:S(2)}) collective-permute-start(bf16[256,640]{1,0:T(8,128)(2,1)S(1)} %pad_maximum_fusion.1.refs_3_.second), channel_id=1, source_target_pairs={{0,3},{1,0},{2,1},{3,2},{4,7},{5,4},{6,5},{7,6},{8,11},{9,8},{10,9... | collective-permute-start | bytes 983048 | tf_op jit(solution)/shard_map/ppermute | solution.py:23
  22.1 2.7 %collective-permute-start.2 = (bf16[256,640]{1,0:T(8,128)(2,1)S(1)}, bf16[256,640]{1,0:T(8,128)(2,1)S(1)}, u32[]{:S(2)}, u32[]{:S(2)}) collective-permute-start(bf16[256,640]{1,0:T(8,128)(2,1)S(1)} %pad_maximum_fusion.refs_0_.first), channel_id=1, source_target_pairs={{0,3},{1,0},{2,1},{3,2},{4,7},{5,4},{6,5},{7,6},{8,11},{9,8},{10,9... | collective-permute-start | bytes 983048 | tf_op jit(solution)/shard_map/ppermute | solution.py:23
  24.8 14.0 %collective-permute-done.5.refs_5_ = bf16[256,640]{1,0:T(8,128)(2,1)S(1)} collective-permute-done((bf16[256,640]{1,0:T(8,128)(2,1)S(1)}, bf16[256,640]{1,0:T(8,128)(2,1)S(1)}, u32[]{:S(2)}, u32[]{:S(2)}) %collective-permute-start.5) | collective-permute-done | bytes 327712 | tf_op jit(solution)/shard_map/ppermute | solution.py:23
  38.7 6.3 %collective-permute-start.8 = (bf16[256,640]{1,0:T(8,128)(2,1)S(1)}, bf16[256,640]{1,0:T(8,128)(2,1)S(1)}, u32[]{:S(2)}, u32[]{:S(2)}) collective-permute-start(bf16[256,640]{1,0:T(8,128)(2,1)S(1)} %collective-permute-done.5.refs_5_), channel_id=1, source_target_pairs={{0,3},{1,0},{2,1},{3,2},{4,7},{5,4},{6,5},{7,6},{8,11},{9,8},{10,9... | collective-permute-start | bytes 983048 | tf_op jit(solution)/shard_map/ppermute | solution.py:23
  46.8 7.4 %collective-permute-done.2.refs_2_ = bf16[256,640]{1,0:T(8,128)(2,1)S(1)} collective-permute-done((bf16[256,640]{1,0:T(8,128)(2,1)S(1)}, bf16[256,640]{1,0:T(8,128)(2,1)S(1)}, u32[]{:S(2)}, u32[]{:S(2)}) %collective-permute-start.2) | collective-permute-done | bytes 327712 | tf_op jit(solution)/shard_map/ppermute | solution.py:23
  55.9 6.4 %collective-permute-done.8.second = bf16[256,640]{1,0:T(8,128)(2,1)S(1)} collective-permute-done((bf16[256,640]{1,0:T(8,128)(2,1)S(1)}, bf16[256,640]{1,0:T(8,128)(2,1)S(1)}, u32[]{:S(2)}, u32[]{:S(2)}) %collective-permute-start.8) | collective-permute-done | bytes 327712 | tf_op jit(solution)/shard_map/ppermute | solution.py:23
  62.3 3.8 %collective-permute-done.7.first = bf16[256,640]{1,0:T(8,128)(2,1)S(1)} collective-permute-done((bf16[256,640]{1,0:T(8,128)(2,1)S(1)}, bf16[256,640]{1,0:T(8,128)(2,1)S(1)}, u32[]{:S(2)}, u32[]{:S(2)}) %collective-permute-start.7) | collective-permute-done | bytes 327712 | tf_op jit(solution)/shard_map/ppermute | solution.py:23
  68.1 7.2 %all-to-all-start = ((bf16[16,80,640]{2,1,0:T(8,128)(2,1)}), bf16[16,80,640]{2,1,0:T(8,128)(2,1)S(1)}, u32[]{:S(2)}, u32[]{:S(2)}) async-start(bf16[16,80,640]{2,1,0:T(8,128)(2,1)} %weight_partial.1), calls=%async_computation | async-start | bytes 3276800 | tf_op jit(solution)/shard_map/all_to_all | solution.py:168
  79.1 3.8 %collective-permute-done.9 = f32[60,640]{1,0:T(8,128)S(1)} collective-permute-done((f32[60,640]{1,0:T(8,128)S(1)}, f32[60,640]{1,0:T(8,128)S(1)}, u32[]{:S(2)}, u32[]{:S(2)}) %collective-permute-start.9) | collective-permute-done | bytes 153632 | tf_op jit(solution)/shard_map/ppermute | solution.py:23
  84.4 3.1 %collective-permute-start.13 = (f32[10,640]{1,0:T(8,128)S(1)}, f32[10,640]{1,0:T(8,128)S(1)}, u32[]{:S(2)}, u32[]{:S(2)}) collective-permute-start(f32[10,640]{1,0:T(8,128)S(1)} %get-tuple-element.36), channel_id=1, source_target_pairs={{0,3},{1,0},{2,1},{3,2},{4,7},{5,4},{6,5},{7,6},{8,11},{9,8},{10,9... | collective-permute-start | bytes 76808 | tf_op jit(solution)/shard_map/ppermute | solution.py:23
  87.5 2.2 %collective-permute-start.12 = (f32[10,640]{1,0:T(8,128)S(1)}, f32[10,640]{1,0:T(8,128)S(1)}, u32[]{:S(2)}, u32[]{:S(2)}) collective-permute-start(f32[10,640]{1,0:T(8,128)S(1)} %get-tuple-element.37), channel_id=1, source_target_pairs={{0,2},{1,3},{2,0},{3,1},{4,6},{5,7},{6,4},{7,5},{8,10},{9,11},{10,... | collective-permute-start | bytes 76808 | tf_op jit(solution)/shard_map/ppermute | solution.py:23
  89.9 5.7 %collective-permute-done.12 = f32[10,640]{1,0:T(8,128)S(1)} collective-permute-done((f32[10,640]{1,0:T(8,128)S(1)}, f32[10,640]{1,0:T(8,128)S(1)}, u32[]{:S(2)}, u32[]{:S(2)}) %collective-permute-start.12) | collective-permute-done | bytes 25632 | tf_op jit(solution)/shard_map/ppermute | solution.py:23
  97.3 5.2 %collective-permute-done.14 = f32[80,640]{1,0:T(8,128)S(1)} collective-permute-done((f32[80,640]{1,0:T(8,128)S(1)}, f32[80,640]{1,0:T(8,128)S(1)}, u32[]{:S(2)}, u32[]{:S(2)}) %collective-permute-start.14) | collective-permute-done | bytes 204832 | tf_op jit(solution)/shard_map/ppermute | solution.py:23
  104.7 6.4 %all-to-all-start.2 = ((bf16[16,80,640]{2,1,0:T(8,128)(2,1)}), bf16[16,80,640]{2,1,0:T(8,128)(2,1)S(1)}, u32[]{:S(2)}, u32[]{:S(2)}) async-start(bf16[16,80,640]{2,1,0:T(8,128)(2,1)} %broadcast_in_dim.2), calls=%async_computation.2 | async-start | bytes 3276800 | tf_op jit(solution)/shard_map/all_to_all | solution.py:168
  111.1 3.8 %collective-permute-start.15 = (f32[10,640]{1,0:T(8,128)S(1)}, f32[10,640]{1,0:T(8,128)S(1)}, u32[]{:S(2)}, u32[]{:S(2)}) collective-permute-start(f32[10,640]{1,0:T(8,128)S(1)} %bitcast_add_fusion.1), channel_id=1, source_target_pairs={{0,0},{4,4},{8,16},{12,20},{16,32},{20,36},{24,48},{28,52},{32,64}... | collective-permute-start | bytes 76808 | tf_op jit(solution)/shard_map/ppermute | solution.py:248
  114.9 6.0 %collective-permute-start.16 = (f32[10,640]{1,0:T(8,128)S(1)}, f32[10,640]{1,0:T(8,128)S(1)}, u32[]{:S(2)}, u32[]{:S(2)}) collective-permute-start(f32[10,640]{1,0:T(8,128)S(1)} %fusion.2), channel_id=1, source_target_pairs={{0,0},{4,128},{8,4},{12,132},{16,8},{20,136},{24,12},{28,140},{32,... | collective-permute-start | bytes 76808 | tf_op jit(solution)/shard_map/ppermute | solution.py:249
  120.9 12.2 %collective-permute-done.15.act_rows = f32[10,640]{1,0:T(8,128)S(1)} collective-permute-done((f32[10,640]{1,0:T(8,128)S(1)}, f32[10,640]{1,0:T(8,128)S(1)}, u32[]{:S(2)}, u32[]{:S(2)}) %collective-permute-start.15) | collective-permute-done | bytes 25632 | tf_op jit(solution)/shard_map/ppermute | solution.py:248
  135.0 2.1 %right_product.2 = (f32[2,640,640]{2,1,0:T(8,128)S(1)}, f32[8,128]{1,0:T(8,128)S(1)}) custom-call(s32[1]{0:T(128)} %bitcast.half_index.core, bf16[1280,640]{1,0:T(8,128)(2,1)S(1)} %bitcast.28, bf16[2560,640]{1,0:T(8,128)(2,1)S(1)} %copy-done.1), custom_call_target="tpu_custom_call" | custom-call | flops 1048576000 | bytes 6291456 | tf_op jit(solution)/shard_map/right_product/pallas_call | solution.py:115
  137.1 2.1 %right_product.3 = (f32[2,640,640]{2,1,0:T(8,128)S(1)}, f32[8,128]{1,0:T(8,128)S(1)}) custom-call(s32[1]{0:T(128)S(6)} %sub.14.half_index, bf16[1280,640]{1,0:T(8,128)(2,1)S(1)} %collective-permute-done.17.left, bf16[2560,640]{1,0:T(8,128)(2,1)S(1)} %copy-done.2), custom_call_target="tpu_custom_call" | custom-call | flops 1048576000 | bytes 6291456 | tf_op jit(solution)/shard_map/right_product/pallas_call | solution.py:115
  139.8 3.3 %collective-permute-start.19 = (f32[8,128]{1,0:T(8,128)S(1)}, f32[8,128]{1,0:T(8,128)S(1)}, u32[]{:S(2)}, u32[]{:S(2)}) collective-permute-start(f32[8,128]{1,0:T(8,128)S(1)} %add.134.own), channel_id=1, source_target_pairs={{0,2},{1,3},{2,0},{3,1},{4,6},{5,7},{6,4},{7,5},{8,10},{9,11},{10,... | collective-permute-start | bytes 12296 | tf_op jit(solution)/shard_map/ppermute | solution.py:23
  144.3 3.0 %collective-permute-done.19.sq_b = f32[8,128]{1,0:T(8,128)S(1)} collective-permute-done((f32[8,128]{1,0:T(8,128)S(1)}, f32[8,128]{1,0:T(8,128)S(1)}, u32[]{:S(2)}, u32[]{:S(2)}) %collective-permute-start.19) | collective-permute-done | bytes 4128 | tf_op jit(solution)/shard_map/ppermute | solution.py:23
  148.7 3.0 %final_update.1 = (bf16[640,2560]{1,0:T(8,128)(2,1)}, f32[10,640]{1,0:T(8,128)}, f32[10,640]{1,0:T(8,128)}) custom-call(s32[1]{0:T(128)} %bitcast.half_index.core, f32[8,128]{1,0:T(8,128)S(1)} %add.134.own, f32[8,128]{1,0:T(8,128)S(1)} %collective-permute-done.18.sq_a, f32[8,128]{1,0:T(8,128)S(1)} %collective-permute-done.19.sq_b, ...), custom_call_target="tpu_custom_call" | custom-call | flops 1638400 | bytes 10485760 | tf_op jit(solution)/shard_map/final_update/pallas_call | solution.py:155
  (64 shorter events, 24.8 us)
Async XLA Ops:
  0.7 3.3 %collective-permute-start.6 = (bf16[512,640]{1,0:T(8,128)(2,1)}, bf16[512,640]{1,0:T(8,128)(2,1)S(1)}, u32[]{:S(2)}, u32[]{:S(2)}) collective-permute-start(bf16[512,640]{1,0:T(8,128)(2,1)} %acts.1), channel_id=1, source_target_pairs={{0,4},{4,0},{1,5},{5,1},{2,6},{6,2},{3,7},{7,3},{8,12},{12,8},{9,1... | collective-permute-start | bytes 1966088 | tf_op jit(solution)/shard_map/ppermute | solution.py:23
  2.1 1.5 collective-permute-start
  2.6 1.4 collective-permute-start.3
  6.7 61.4 %all-to-all-start.1 = ((bf16[16,3,40,640]{3,2,1,0:T(8,128)(2,1)}), bf16[16,3,40,640]{3,2,1,0:T(8,128)(2,1)}, u32[]{:S(2)}, u32[]{:S(2)}) async-start(bf16[16,3,40,640]{3,2,1,0:T(8,128)(2,1)} %cov_partial.1), calls=%async_computation.1 | async-start | bytes 4915200 | tf_op jit(solution)/shard_map/all_to_all | solution.py:168
  14.1 24.6 %collective-permute-start.5 = (bf16[256,640]{1,0:T(8,128)(2,1)S(1)}, bf16[256,640]{1,0:T(8,128)(2,1)S(1)}, u32[]{:S(2)}, u32[]{:S(2)}) collective-permute-start(bf16[256,640]{1,0:T(8,128)(2,1)S(1)} %pad_maximum_fusion.1.refs_3_.second), channel_id=1, source_target_pairs={{0,3},{1,0},{2,1},{3,2},{4,7},{5,4},{6,5},{7,6},{8,11},{9,8},{10,9... | collective-permute-start | bytes 983048 | tf_op jit(solution)/shard_map/ppermute | solution.py:23
  20.4 24.6 %collective-permute-start.1 = (bf16[256,640]{1,0:T(8,128)(2,1)S(1)}, bf16[256,640]{1,0:T(8,128)(2,1)S(1)}, u32[]{:S(2)}, u32[]{:S(2)}) collective-permute-start(bf16[256,640]{1,0:T(8,128)(2,1)S(1)} %pad_maximum_fusion.refs_0_.first), channel_id=1, source_target_pairs={{0,1},{1,2},{2,3},{3,0},{4,5},{5,6},{6,7},{7,4},{8,9},{9,10},{10,1... | collective-permute-start | bytes 983048 | tf_op jit(solution)/shard_map/ppermute | solution.py:23
  20.5 26.3 %collective-permute-start.4 = (bf16[256,640]{1,0:T(8,128)(2,1)S(1)}, bf16[256,640]{1,0:T(8,128)(2,1)S(1)}, u32[]{:S(2)}, u32[]{:S(2)}) collective-permute-start(bf16[256,640]{1,0:T(8,128)(2,1)S(1)} %pad_maximum_fusion.1.refs_3_.second), channel_id=1, source_target_pairs={{0,1},{1,2},{2,3},{3,0},{4,5},{5,6},{6,7},{7,4},{8,9},{9,10},{10,1... | collective-permute-start | bytes 983048 | tf_op jit(solution)/shard_map/ppermute | solution.py:23
  22.1 32.1 %collective-permute-start.2 = (bf16[256,640]{1,0:T(8,128)(2,1)S(1)}, bf16[256,640]{1,0:T(8,128)(2,1)S(1)}, u32[]{:S(2)}, u32[]{:S(2)}) collective-permute-start(bf16[256,640]{1,0:T(8,128)(2,1)S(1)} %pad_maximum_fusion.refs_0_.first), channel_id=1, source_target_pairs={{0,3},{1,0},{2,1},{3,2},{4,7},{5,4},{6,5},{7,6},{8,11},{9,8},{10,9... | collective-permute-start | bytes 983048 | tf_op jit(solution)/shard_map/ppermute | solution.py:23
  38.7 23.6 %collective-permute-start.8 = (bf16[256,640]{1,0:T(8,128)(2,1)S(1)}, bf16[256,640]{1,0:T(8,128)(2,1)S(1)}, u32[]{:S(2)}, u32[]{:S(2)}) collective-permute-start(bf16[256,640]{1,0:T(8,128)(2,1)S(1)} %collective-permute-done.5.refs_5_), channel_id=1, source_target_pairs={{0,3},{1,0},{2,1},{3,2},{4,7},{5,4},{6,5},{7,6},{8,11},{9,8},{10,9... | collective-permute-start | bytes 983048 | tf_op jit(solution)/shard_map/ppermute | solution.py:23
  45.0 21.2 %collective-permute-start.7 = (bf16[256,640]{1,0:T(8,128)(2,1)S(1)}, bf16[256,640]{1,0:T(8,128)(2,1)S(1)}, u32[]{:S(2)}, u32[]{:S(2)}) collective-permute-start(bf16[256,640]{1,0:T(8,128)(2,1)S(1)} %collective-permute-done.1.refs_1_), channel_id=1, source_target_pairs={{0,1},{1,2},{2,3},{3,0},{4,5},{5,6},{6,7},{7,4},{8,9},{9,10},{10,1... | collective-permute-start | bytes 983048 | tf_op jit(solution)/shard_map/ppermute | solution.py:23
  68.1 28.4 %all-to-all-start = ((bf16[16,80,640]{2,1,0:T(8,128)(2,1)}), bf16[16,80,640]{2,1,0:T(8,128)(2,1)S(1)}, u32[]{:S(2)}, u32[]{:S(2)}) async-start(bf16[16,80,640]{2,1,0:T(8,128)(2,1)} %weight_partial.1), calls=%async_computation | async-start | bytes 3276800 | tf_op jit(solution)/shard_map/all_to_all | solution.py:168
  77.5 5.4 %collective-permute-start.9 = (f32[60,640]{1,0:T(8,128)S(1)}, f32[60,640]{1,0:T(8,128)S(1)}, u32[]{:S(2)}, u32[]{:S(2)}) collective-permute-start(f32[60,640]{1,0:T(8,128)S(1)} %pad_maximum_fusion.6), channel_id=1, source_target_pairs={{0,128},{128,0},{1,129},{129,1},{2,130},{130,2},{3,131},{131,3},{4... | collective-permute-start | bytes 460808 | tf_op jit(solution)/shard_map/ppermute | solution.py:23
  83.0 6.8 %collective-permute-start.10 = (f32[10,640]{1,0:T(8,128)S(1)}, f32[10,640]{1,0:T(8,128)S(1)}, u32[]{:S(2)}, u32[]{:S(2)}) collective-permute-start(f32[10,640]{1,0:T(8,128)S(1)} %dynamic-slice_bitcast_fusion.5), channel_id=1, source_target_pairs={{0,4},{4,0},{1,5},{5,1},{2,6},{6,2},{3,7},{7,3},{8,12},{12,8},{9,1... | collective-permute-start | bytes 76808 | tf_op jit(solution)/shard_map/ppermute | solution.py:23
  83.3 6.4 %collective-permute-start.11 = (f32[10,640]{1,0:T(8,128)S(1)}, f32[10,640]{1,0:T(8,128)S(1)}, u32[]{:S(2)}, u32[]{:S(2)}) collective-permute-start(f32[10,640]{1,0:T(8,128)S(1)} %get-tuple-element.35), channel_id=1, source_target_pairs={{0,1},{1,2},{2,3},{3,0},{4,5},{5,6},{6,7},{7,4},{8,9},{9,10},{10,1... | collective-permute-start | bytes 76808 | tf_op jit(solution)/shard_map/ppermute | solution.py:23
  84.4 5.5 %collective-permute-start.13 = (f32[10,640]{1,0:T(8,128)S(1)}, f32[10,640]{1,0:T(8,128)S(1)}, u32[]{:S(2)}, u32[]{:S(2)}) collective-permute-start(f32[10,640]{1,0:T(8,128)S(1)} %get-tuple-element.36), channel_id=1, source_target_pairs={{0,3},{1,0},{2,1},{3,2},{4,7},{5,4},{6,5},{7,6},{8,11},{9,8},{10,9... | collective-permute-start | bytes 76808 | tf_op jit(solution)/shard_map/ppermute | solution.py:23
  87.5 8.1 %collective-permute-start.12 = (f32[10,640]{1,0:T(8,128)S(1)}, f32[10,640]{1,0:T(8,128)S(1)}, u32[]{:S(2)}, u32[]{:S(2)}) collective-permute-start(f32[10,640]{1,0:T(8,128)S(1)} %get-tuple-element.37), channel_id=1, source_target_pairs={{0,2},{1,3},{2,0},{3,1},{4,6},{5,7},{6,4},{7,5},{8,10},{9,11},{10,... | collective-permute-start | bytes 76808 | tf_op jit(solution)/shard_map/ppermute | solution.py:23
  96.7 5.8 %collective-permute-start.14 = (f32[80,640]{1,0:T(8,128)S(1)}, f32[80,640]{1,0:T(8,128)S(1)}, u32[]{:S(2)}, u32[]{:S(2)}) collective-permute-start(f32[80,640]{1,0:T(8,128)S(1)} %convert_reduce_fusion.1), channel_id=1, source_target_pairs={{0,128},{128,0},{1,129},{129,1},{2,130},{130,2},{3,131},{131,3},{4... | collective-permute-start | bytes 614408 | tf_op jit(solution)/shard_map/ppermute | solution.py:23
  104.7 28.4 %all-to-all-start.2 = ((bf16[16,80,640]{2,1,0:T(8,128)(2,1)}), bf16[16,80,640]{2,1,0:T(8,128)(2,1)S(1)}, u32[]{:S(2)}, u32[]{:S(2)}) async-start(bf16[16,80,640]{2,1,0:T(8,128)(2,1)} %broadcast_in_dim.2), calls=%async_computation.2 | async-start | bytes 3276800 | tf_op jit(solution)/shard_map/all_to_all | solution.py:168
  111.1 21.9 %collective-permute-start.15 = (f32[10,640]{1,0:T(8,128)S(1)}, f32[10,640]{1,0:T(8,128)S(1)}, u32[]{:S(2)}, u32[]{:S(2)}) collective-permute-start(f32[10,640]{1,0:T(8,128)S(1)} %bitcast_add_fusion.1), channel_id=1, source_target_pairs={{0,0},{4,4},{8,16},{12,20},{16,32},{20,36},{24,48},{28,52},{32,64}... | collective-permute-start | bytes 76808 | tf_op jit(solution)/shard_map/ppermute | solution.py:248
  114.9 18.1 %collective-permute-start.16 = (f32[10,640]{1,0:T(8,128)S(1)}, f32[10,640]{1,0:T(8,128)S(1)}, u32[]{:S(2)}, u32[]{:S(2)}) collective-permute-start(f32[10,640]{1,0:T(8,128)S(1)} %fusion.2), channel_id=1, source_target_pairs={{0,0},{4,128},{8,4},{12,132},{16,8},{20,136},{24,12},{28,140},{32,... | collective-permute-start | bytes 76808 | tf_op jit(solution)/shard_map/ppermute | solution.py:249
  133.1 4.1 %collective-permute-start.17 = (bf16[1280,640]{1,0:T(8,128)(2,1)S(1)}, bf16[1280,640]{1,0:T(8,128)(2,1)S(1)}, u32[]{:S(2)}, u32[]{:S(2)}) collective-permute-start(bf16[1280,640]{1,0:T(8,128)(2,1)S(1)} %bitcast.27), channel_id=1, source_target_pairs={{0,4},{4,0},{1,5},{5,1},{2,6},{6,2},{3,7},{7,3},{8,12},{12,8},{9,1... | collective-permute-start | bytes 4915208 | tf_op jit(solution)/shard_map/ppermute | solution.py:23
  139.3 5.0 %collective-permute-start.20 = (f32[8,128]{1,0:T(8,128)S(1)}, f32[8,128]{1,0:T(8,128)S(1)}, u32[]{:S(2)}, u32[]{:S(2)}) collective-permute-start(f32[8,128]{1,0:T(8,128)S(1)} %add.134.own), channel_id=1, source_target_pairs={{0,3},{1,0},{2,1},{3,2},{4,7},{5,4},{6,5},{7,6},{8,11},{9,8},{10,9... | collective-permute-start | bytes 12296 | tf_op jit(solution)/shard_map/ppermute | solution.py:23
  139.8 7.5 %collective-permute-start.19 = (f32[8,128]{1,0:T(8,128)S(1)}, f32[8,128]{1,0:T(8,128)S(1)}, u32[]{:S(2)}, u32[]{:S(2)}) collective-permute-start(f32[8,128]{1,0:T(8,128)S(1)} %add.134.own), channel_id=1, source_target_pairs={{0,2},{1,3},{2,0},{3,1},{4,6},{5,7},{6,4},{7,5},{8,10},{9,11},{10,... | collective-permute-start | bytes 12296 | tf_op jit(solution)/shard_map/ppermute | solution.py:23
  143.0 5.7 %collective-permute-start.18 = (f32[8,128]{1,0:T(8,128)S(1)}, f32[8,128]{1,0:T(8,128)S(1)}, u32[]{:S(2)}, u32[]{:S(2)}) collective-permute-start(f32[8,128]{1,0:T(8,128)S(1)} %add.134.own), channel_id=1, source_target_pairs={{0,1},{1,2},{2,3},{3,0},{4,5},{5,6},{6,7},{7,4},{8,9},{9,10},{10,1... | collective-permute-start | bytes 12296 | tf_op jit(solution)/shard_map/ppermute | solution.py:23
  (4 other events, 109.3 us)

commit v4 on v3

--- a/solution.py
+++ b/solution.py
@@ -72,7 +72,7 @@
         in_specs=[VMEM] * 4,
         out_specs=VMEM,
         compiler_params=LIMIT,
-        cost_estimate=cost(1024 * width * width, 6),
+        cost_estimate=cost(12 * 1024 * width * width, 6),
         name="weight_partial",
     )(early, first, second, act)
 
@@ -234,8 +234,9 @@
                 grad_perm.append((source, (co * 2 + zl) * sites + site))
 
     early = early_partial(pieces[:3] + pieces[4:7], acts[:3], inv_tokens)
-    got = plane_exchange(weight_partial(early, pieces[3], pieces[7], acts[3], inv_tokens, sites))
-    got = after(got, act_rows, grad_rows)
+    partial = weight_partial(early, pieces[3], pieces[7], acts[3], inv_tokens, sites)
+    got = plane_exchange(after(partial, cov_got))
+    got = after(got, taken)
     share = jnp.sum(got.astype(F32), axis=0)
     mixed = lax.dot_general(
         share + shift(share, "zlo", 1),

time: 153 us -> 151 us (0.987)
  starting transfers between devices: 62.3 us -> 59.3 us
  waiting for transfers between devices: 66.7 us -> 68.4 us
    all_to_all x3, waiting for transfers between devices: 0.8 us -> 13.5 us  [plane_exchange(): return lax.all_to_all(value, PLANE, split_axis=0, concat_axis=0, tiled=True)]
    ppermute x1, waiting for transfers between devices: 12.2 us -> 3.32 us  [body(): act_rows = lax.ppermute(act_rows, DP, act_perm)]
    ppermute x19, waiting for transfers between devices: 53.8 us -> 51.5 us  [shift(): lax.ppermute(value, axis, [(i, (i + step) % count) for i in range(count)])]
    ppermute x1, starting transfers between devices: 3.78 us -> 2.18 us  [body(): act_rows = lax.ppermute(act_rows, DP, act_perm)]
  transfers between devices with their start and end apart: 24 -> 24, of which waited for: 15 -> 13; matrix products, arithmetic and copies ran while one was open for 3% -> 3% of each run, Pallas kernels for 4% -> 4%
where the time goes in v4:
time: 151 us; the launch traced here: 150 us
  waiting for transfers between devices  68.4 us (45%)
  starting transfers between devices  59.3 us (39%)
  Pallas kernels  13.5 us (9%)
  local copies, waits for them, and re-layouts  4.84 us (3%)
  other arithmetic  2.55 us (2%)
    ppermute x19, waiting for transfers between devices, shift(): lax.ppermute(value, axis, [(i, (i + step) % count) for i in range(count)])  51.5 us
    ppermute x19, starting transfers between devices, shift(): lax.ppermute(value, axis, [(i, (i + step) % count) for i in range(count)])  30.6 us
    all_to_all x3, starting transfers between devices, plane_exchange(): return lax.all_to_all(value, PLANE, split_axis=0, concat_axis=0, tiled=True)  20.8 us
    all_to_all x3, waiting for transfers between devices, plane_exchange(): return lax.all_to_all(value, PLANE, split_axis=0, concat_axis=0, tiled=True)  13.5 us
    ppermute x1, starting transfers between devices, body(): grad_rows = lax.ppermute(grad_rows, DP, grad_perm)  5.73 us
    pallas_call x2, Pallas kernels, right_product(): pl.pallas_call(right_kernel, out_shape=(jax.ShapeDtypeStruct((2, width, w...  4.23 us
    ppermute x1, waiting for transfers between devices, body(): act_rows = lax.ppermute(act_rows, DP, act_perm)  3.32 us
  transfers between devices with their start and end apart: 24, of which 13 were waited for; matrix products, arithmetic and copies ran while one was open for 3% of the time, Pallas kernels for 4%

profile of v4, /device:TPU:6, one launch (start us, length us, event | category | flops | bytes accessed | tf_op | source)
XLA Modules:
  0.0 150.4 jit_solution(14577355649835803495)
XLA Ops:
  4.0 2.7 %cov_partial.1 = bf16[16,3,40,640]{3,2,1,0:T(8,128)(2,1)} custom-call(bf16[256,640]{1,0:T(8,128)(2,1)S(1)} %pad_maximum_fusion.refs_0_.first, bf16[256,640]{1,0:T(8,128)(2,1)S(1)} %pad_maximum_fusion.1.refs_3_.second, bf16[512,640]{1,0:T(8,128)(2,1)S(1)} %copy-done.3), custom_call_target="tpu_custom_call" | custom-call | flops 838860800 | bytes 5242880 | tf_op jit(solution)/shard_map/cov_partial/pallas_call | solution.py:91
  6.7 7.4 %all-to-all-start = ((bf16[16,3,40,640]{3,2,1,0:T(8,128)(2,1)}), bf16[16,3,40,640]{3,2,1,0:T(8,128)(2,1)}, u32[]{:S(2)}, u32[]{:S(2)}) async-start(bf16[16,3,40,640]{3,2,1,0:T(8,128)(2,1)} %cov_partial.1), calls=%async_computation | async-start | bytes 4915200 | tf_op jit(solution)/shard_map/all_to_all | solution.py:168
  14.1 6.3 %collective-permute-start.5 = (bf16[256,640]{1,0:T(8,128)(2,1)S(1)}, bf16[256,640]{1,0:T(8,128)(2,1)S(1)}, u32[]{:S(2)}, u32[]{:S(2)}) collective-permute-start(bf16[256,640]{1,0:T(8,128)(2,1)S(1)} %pad_maximum_fusion.1.refs_3_.second), channel_id=1, source_target_pairs={{0,3},{1,0},{2,1},{3,2},{4,7},{5,4},{6,5},{7,6},{8,11},{9,8},{10,9... | collective-permute-start | bytes 983048 | tf_op jit(solution)/shard_map/ppermute | solution.py:23
  22.1 2.7 %collective-permute-start.2 = (bf16[256,640]{1,0:T(8,128)(2,1)S(1)}, bf16[256,640]{1,0:T(8,128)(2,1)S(1)}, u32[]{:S(2)}, u32[]{:S(2)}) collective-permute-start(bf16[256,640]{1,0:T(8,128)(2,1)S(1)} %pad_maximum_fusion.refs_0_.first), channel_id=1, source_target_pairs={{0,3},{1,0},{2,1},{3,2},{4,7},{5,4},{6,5},{7,6},{8,11},{9,8},{10,9... | collective-permute-start | bytes 983048 | tf_op jit(solution)/shard_map/ppermute | solution.py:23
  24.8 14.0 %collective-permute-done.5.refs_5_ = bf16[256,640]{1,0:T(8,128)(2,1)S(1)} collective-permute-done((bf16[256,640]{1,0:T(8,128)(2,1)S(1)}, bf16[256,640]{1,0:T(8,128)(2,1)S(1)}, u32[]{:S(2)}, u32[]{:S(2)}) %collective-permute-start.5) | collective-permute-done | bytes 327712 | tf_op jit(solution)/shard_map/ppermute | solution.py:23
  38.7 6.3 %collective-permute-start.8 = (bf16[256,640]{1,0:T(8,128)(2,1)S(1)}, bf16[256,640]{1,0:T(8,128)(2,1)S(1)}, u32[]{:S(2)}, u32[]{:S(2)}) collective-permute-start(bf16[256,640]{1,0:T(8,128)(2,1)S(1)} %collective-permute-done.5.refs_5_), channel_id=1, source_target_pairs={{0,3},{1,0},{2,1},{3,2},{4,7},{5,4},{6,5},{7,6},{8,11},{9,8},{10,9... | collective-permute-start | bytes 983048 | tf_op jit(solution)/shard_map/ppermute | solution.py:23
  46.8 7.4 %collective-permute-done.2.refs_2_ = bf16[256,640]{1,0:T(8,128)(2,1)S(1)} collective-permute-done((bf16[256,640]{1,0:T(8,128)(2,1)S(1)}, bf16[256,640]{1,0:T(8,128)(2,1)S(1)}, u32[]{:S(2)}, u32[]{:S(2)}) %collective-permute-start.2) | collective-permute-done | bytes 327712 | tf_op jit(solution)/shard_map/ppermute | solution.py:23
  56.0 6.4 %collective-permute-done.8.second = bf16[256,640]{1,0:T(8,128)(2,1)S(1)} collective-permute-done((bf16[256,640]{1,0:T(8,128)(2,1)S(1)}, bf16[256,640]{1,0:T(8,128)(2,1)S(1)}, u32[]{:S(2)}, u32[]{:S(2)}) %collective-permute-start.8) | collective-permute-done | bytes 327712 | tf_op jit(solution)/shard_map/ppermute | solution.py:23
  62.3 3.8 %collective-permute-done.7.first = bf16[256,640]{1,0:T(8,128)(2,1)S(1)} collective-permute-done((bf16[256,640]{1,0:T(8,128)(2,1)S(1)}, bf16[256,640]{1,0:T(8,128)(2,1)S(1)}, u32[]{:S(2)}, u32[]{:S(2)}) %collective-permute-start.7) | collective-permute-done | bytes 327712 | tf_op jit(solution)/shard_map/ppermute | solution.py:23
  68.0 7.2 %all-to-all-start.1 = ((bf16[16,80,640]{2,1,0:T(8,128)(2,1)}), bf16[16,80,640]{2,1,0:T(8,128)(2,1)S(1)}, u32[]{:S(2)}, u32[]{:S(2)}) async-start(bf16[16,80,640]{2,1,0:T(8,128)(2,1)} %weight_partial.1), calls=%async_computation.1 | async-start | bytes 3276800 | tf_op jit(solution)/shard_map/all_to_all | solution.py:168
  79.1 3.8 %collective-permute-done.9 = f32[60,640]{1,0:T(8,128)S(1)} collective-permute-done((f32[60,640]{1,0:T(8,128)S(1)}, f32[60,640]{1,0:T(8,128)S(1)}, u32[]{:S(2)}, u32[]{:S(2)}) %collective-permute-start.9) | collective-permute-done | bytes 153632 | tf_op jit(solution)/shard_map/ppermute | solution.py:23
  82.9 13.5 %all-to-all-done.1 = bf16[16,80,640]{2,1,0:T(8,128)(2,1)S(1)} async-done(((bf16[16,80,640]{2,1,0:T(8,128)(2,1)}), bf16[16,80,640]{2,1,0:T(8,128)(2,1)S(1)}, u32[]{:S(2)}, u32[]{:S(2)}) %all-to-all-start.1) | async-done | bytes 1638432 | tf_op jit(solution)/shard_map/all_to_all | solution.py:168
  96.9 5.7 %collective-permute-done.10 = f32[80,640]{1,0:T(8,128)S(1)} collective-permute-done((f32[80,640]{1,0:T(8,128)S(1)}, f32[80,640]{1,0:T(8,128)S(1)}, u32[]{:S(2)}, u32[]{:S(2)}) %collective-permute-start.10) | collective-permute-done | bytes 204832 | tf_op jit(solution)/shard_map/ppermute | solution.py:23
  104.9 6.1 %all-to-all-start.2 = ((bf16[16,80,640]{2,1,0:T(8,128)(2,1)}), bf16[16,80,640]{2,1,0:T(8,128)(2,1)S(1)}, u32[]{:S(2)}, u32[]{:S(2)}) async-start(bf16[16,80,640]{2,1,0:T(8,128)(2,1)} %broadcast_in_dim.2), calls=%async_computation.2 | async-start | bytes 3276800 | tf_op jit(solution)/shard_map/all_to_all | solution.py:168
  111.3 4.1 %collective-permute-start.15 = (f32[10,640]{1,0:T(8,128)S(1)}, f32[10,640]{1,0:T(8,128)S(1)}, u32[]{:S(2)}, u32[]{:S(2)}) collective-permute-start(f32[10,640]{1,0:T(8,128)S(1)} %get-tuple-element.38), channel_id=1, source_target_pairs={{0,3},{1,0},{2,1},{3,2},{4,7},{5,4},{6,5},{7,6},{8,11},{9,8},{10,9... | collective-permute-start | bytes 76808 | tf_op jit(solution)/shard_map/ppermute | solution.py:23
  115.4 2.1 %collective-permute-start.14 = (f32[10,640]{1,0:T(8,128)S(1)}, f32[10,640]{1,0:T(8,128)S(1)}, u32[]{:S(2)}, u32[]{:S(2)}) collective-permute-start(f32[10,640]{1,0:T(8,128)S(1)} %get-tuple-element.39), channel_id=1, source_target_pairs={{0,2},{1,3},{2,0},{3,1},{4,6},{5,7},{6,4},{7,5},{8,10},{9,11},{10,... | collective-permute-start | bytes 76808 | tf_op jit(solution)/shard_map/ppermute | solution.py:23
  117.5 2.2 %collective-permute-start.12 = (f32[10,640]{1,0:T(8,128)S(1)}, f32[10,640]{1,0:T(8,128)S(1)}, u32[]{:S(2)}, u32[]{:S(2)}) collective-permute-start(f32[10,640]{1,0:T(8,128)S(1)} %bitcast_add_fusion.1), channel_id=1, source_target_pairs={{0,0},{4,4},{8,16},{12,20},{16,32},{20,36},{24,48},{28,52},{32,64}... | collective-permute-start | bytes 76808 | tf_op jit(solution)/shard_map/ppermute | solution.py:249
  119.8 3.6 %collective-permute-done.14 = f32[10,640]{1,0:T(8,128)S(1)} collective-permute-done((f32[10,640]{1,0:T(8,128)S(1)}, f32[10,640]{1,0:T(8,128)S(1)}, u32[]{:S(2)}, u32[]{:S(2)}) %collective-permute-start.14) | collective-permute-done | bytes 25632 | tf_op jit(solution)/shard_map/ppermute | solution.py:23
  123.4 5.7 %collective-permute-start.16 = (f32[10,640]{1,0:T(8,128)S(1)}, f32[10,640]{1,0:T(8,128)S(1)}, u32[]{:S(2)}, u32[]{:S(2)}) collective-permute-start(f32[10,640]{1,0:T(8,128)S(1)} %fusion.2), channel_id=1, source_target_pairs={{0,0},{4,128},{8,4},{12,132},{16,8},{20,136},{24,12},{28,140},{32,... | collective-permute-start | bytes 76808 | tf_op jit(solution)/shard_map/ppermute | solution.py:250
  129.1 3.3 %collective-permute-done.12.act_rows = f32[10,640]{1,0:T(8,128)S(1)} collective-permute-done((f32[10,640]{1,0:T(8,128)S(1)}, f32[10,640]{1,0:T(8,128)S(1)}, u32[]{:S(2)}, u32[]{:S(2)}) %collective-permute-start.12) | collective-permute-done | bytes 25632 | tf_op jit(solution)/shard_map/ppermute | solution.py:249
  134.4 2.1 %right_product.2 = (f32[2,640,640]{2,1,0:T(8,128)S(1)}, f32[8,128]{1,0:T(8,128)S(1)}) custom-call(s32[1]{0:T(128)} %bitcast.half_index.core, bf16[1280,640]{1,0:T(8,128)(2,1)S(1)} %bitcast.28, bf16[2560,640]{1,0:T(8,128)(2,1)S(1)} %copy-done.1), custom_call_target="tpu_custom_call" | custom-call | flops 1048576000 | bytes 6291456 | tf_op jit(solution)/shard_map/right_product/pallas_call | solution.py:115
  136.5 2.1 %right_product.3 = (f32[2,640,640]{2,1,0:T(8,128)S(1)}, f32[8,128]{1,0:T(8,128)S(1)}) custom-call(s32[1]{0:T(128)S(6)} %sub.14.half_index, bf16[1280,640]{1,0:T(8,128)(2,1)S(1)} %collective-permute-done.17.left, bf16[2560,640]{1,0:T(8,128)(2,1)S(1)} %copy-done.2), custom_call_target="tpu_custom_call" | custom-call | flops 1048576000 | bytes 6291456 | tf_op jit(solution)/shard_map/right_product/pallas_call | solution.py:115
  143.4 3.9 %collective-permute-done.19.sq_b = f32[8,128]{1,0:T(8,128)S(1)} collective-permute-done((f32[8,128]{1,0:T(8,128)S(1)}, f32[8,128]{1,0:T(8,128)S(1)}, u32[]{:S(2)}, u32[]{:S(2)}) %collective-permute-start.19) | collective-permute-done | bytes 4128 | tf_op jit(solution)/shard_map/ppermute | solution.py:23
  147.4 3.0 %final_update.1 = (bf16[640,2560]{1,0:T(8,128)(2,1)}, f32[10,640]{1,0:T(8,128)}, f32[10,640]{1,0:T(8,128)}) custom-call(s32[1]{0:T(128)} %bitcast.half_index.core, f32[8,128]{1,0:T(8,128)S(1)} %add.134.own, f32[8,128]{1,0:T(8,128)S(1)} %collective-permute-done.18.sq_a, f32[8,128]{1,0:T(8,128)S(1)} %collective-permute-done.19.sq_b, ...), custom_call_target="tpu_custom_call" | custom-call | flops 1638400 | bytes 10485760 | tf_op jit(solution)/shard_map/final_update/pallas_call | solution.py:155
  (65 shorter events, 23.8 us)
Async XLA Ops:
  0.7 3.3 %collective-permute-start.6 = (bf16[512,640]{1,0:T(8,128)(2,1)}, bf16[512,640]{1,0:T(8,128)(2,1)S(1)}, u32[]{:S(2)}, u32[]{:S(2)}) collective-permute-start(bf16[512,640]{1,0:T(8,128)(2,1)} %acts.1), channel_id=1, source_target_pairs={{0,4},{4,0},{1,5},{5,1},{2,6},{6,2},{3,7},{7,3},{8,12},{12,8},{9,1... | collective-permute-start | bytes 1966088 | tf_op jit(solution)/shard_map/ppermute | solution.py:23
  2.1 1.5 collective-permute-start
  2.6 1.4 collective-permute-start.3
  6.7 61.4 %all-to-all-start = ((bf16[16,3,40,640]{3,2,1,0:T(8,128)(2,1)}), bf16[16,3,40,640]{3,2,1,0:T(8,128)(2,1)}, u32[]{:S(2)}, u32[]{:S(2)}) async-start(bf16[16,3,40,640]{3,2,1,0:T(8,128)(2,1)} %cov_partial.1), calls=%async_computation | async-start | bytes 4915200 | tf_op jit(solution)/shard_map/all_to_all | solution.py:168
  14.1 24.6 %collective-permute-start.5 = (bf16[256,640]{1,0:T(8,128)(2,1)S(1)}, bf16[256,640]{1,0:T(8,128)(2,1)S(1)}, u32[]{:S(2)}, u32[]{:S(2)}) collective-permute-start(bf16[256,640]{1,0:T(8,128)(2,1)S(1)} %pad_maximum_fusion.1.refs_3_.second), channel_id=1, source_target_pairs={{0,3},{1,0},{2,1},{3,2},{4,7},{5,4},{6,5},{7,6},{8,11},{9,8},{10,9... | collective-permute-start | bytes 983048 | tf_op jit(solution)/shard_map/ppermute | solution.py:23
  20.4 24.6 %collective-permute-start.1 = (bf16[256,640]{1,0:T(8,128)(2,1)S(1)}, bf16[256,640]{1,0:T(8,128)(2,1)S(1)}, u32[]{:S(2)}, u32[]{:S(2)}) collective-permute-start(bf16[256,640]{1,0:T(8,128)(2,1)S(1)} %pad_maximum_fusion.refs_0_.first), channel_id=1, source_target_pairs={{0,1},{1,2},{2,3},{3,0},{4,5},{5,6},{6,7},{7,4},{8,9},{9,10},{10,1... | collective-permute-start | bytes 983048 | tf_op jit(solution)/shard_map/ppermute | solution.py:23
  20.5 26.3 %collective-permute-start.4 = (bf16[256,640]{1,0:T(8,128)(2,1)S(1)}, bf16[256,640]{1,0:T(8,128)(2,1)S(1)}, u32[]{:S(2)}, u32[]{:S(2)}) collective-permute-start(bf16[256,640]{1,0:T(8,128)(2,1)S(1)} %pad_maximum_fusion.1.refs_3_.second), channel_id=1, source_target_pairs={{0,1},{1,2},{2,3},{3,0},{4,5},{5,6},{6,7},{7,4},{8,9},{9,10},{10,1... | collective-permute-start | bytes 983048 | tf_op jit(solution)/shard_map/ppermute | solution.py:23
  22.1 32.1 %collective-permute-start.2 = (bf16[256,640]{1,0:T(8,128)(2,1)S(1)}, bf16[256,640]{1,0:T(8,128)(2,1)S(1)}, u32[]{:S(2)}, u32[]{:S(2)}) collective-permute-start(bf16[256,640]{1,0:T(8,128)(2,1)S(1)} %pad_maximum_fusion.refs_0_.first), channel_id=1, source_target_pairs={{0,3},{1,0},{2,1},{3,2},{4,7},{5,4},{6,5},{7,6},{8,11},{9,8},{10,9... | collective-permute-start | bytes 983048 | tf_op jit(solution)/shard_map/ppermute | solution.py:23
  38.7 23.6 %collective-permute-start.8 = (bf16[256,640]{1,0:T(8,128)(2,1)S(1)}, bf16[256,640]{1,0:T(8,128)(2,1)S(1)}, u32[]{:S(2)}, u32[]{:S(2)}) collective-permute-start(bf16[256,640]{1,0:T(8,128)(2,1)S(1)} %collective-permute-done.5.refs_5_), channel_id=1, source_target_pairs={{0,3},{1,0},{2,1},{3,2},{4,7},{5,4},{6,5},{7,6},{8,11},{9,8},{10,9... | collective-permute-start | bytes 983048 | tf_op jit(solution)/shard_map/ppermute | solution.py:23
  45.0 21.2 %collective-permute-start.7 = (bf16[256,640]{1,0:T(8,128)(2,1)S(1)}, bf16[256,640]{1,0:T(8,128)(2,1)S(1)}, u32[]{:S(2)}, u32[]{:S(2)}) collective-permute-start(bf16[256,640]{1,0:T(8,128)(2,1)S(1)} %collective-permute-done.1.refs_1_), channel_id=1, source_target_pairs={{0,1},{1,2},{2,3},{3,0},{4,5},{5,6},{6,7},{7,4},{8,9},{9,10},{10,1... | collective-permute-start | bytes 983048 | tf_op jit(solution)/shard_map/ppermute | solution.py:23
  68.0 28.4 %all-to-all-start.1 = ((bf16[16,80,640]{2,1,0:T(8,128)(2,1)}), bf16[16,80,640]{2,1,0:T(8,128)(2,1)S(1)}, u32[]{:S(2)}, u32[]{:S(2)}) async-start(bf16[16,80,640]{2,1,0:T(8,128)(2,1)} %weight_partial.1), calls=%async_computation.1 | async-start | bytes 3276800 | tf_op jit(solution)/shard_map/all_to_all | solution.py:168
  77.5 5.4 %collective-permute-start.9 = (f32[60,640]{1,0:T(8,128)S(1)}, f32[60,640]{1,0:T(8,128)S(1)}, u32[]{:S(2)}, u32[]{:S(2)}) collective-permute-start(f32[60,640]{1,0:T(8,128)S(1)} %pad_maximum_fusion.6), channel_id=1, source_target_pairs={{0,128},{128,0},{1,129},{129,1},{2,130},{130,2},{3,131},{131,3},{4... | collective-permute-start | bytes 460808 | tf_op jit(solution)/shard_map/ppermute | solution.py:23
  96.7 6.0 %collective-permute-start.10 = (f32[80,640]{1,0:T(8,128)S(1)}, f32[80,640]{1,0:T(8,128)S(1)}, u32[]{:S(2)}, u32[]{:S(2)}) collective-permute-start(f32[80,640]{1,0:T(8,128)S(1)} %convert_reduce_fusion.1), channel_id=1, source_target_pairs={{0,128},{128,0},{1,129},{129,1},{2,130},{130,2},{3,131},{131,3},{4... | collective-permute-start | bytes 614408 | tf_op jit(solution)/shard_map/ppermute | solution.py:23
  104.9 27.6 %all-to-all-start.2 = ((bf16[16,80,640]{2,1,0:T(8,128)(2,1)}), bf16[16,80,640]{2,1,0:T(8,128)(2,1)S(1)}, u32[]{:S(2)}, u32[]{:S(2)}) async-start(bf16[16,80,640]{2,1,0:T(8,128)(2,1)} %broadcast_in_dim.2), calls=%async_computation.2 | async-start | bytes 3276800 | tf_op jit(solution)/shard_map/all_to_all | solution.py:168
  111.0 6.5 %collective-permute-start.11 = (f32[10,640]{1,0:T(8,128)S(1)}, f32[10,640]{1,0:T(8,128)S(1)}, u32[]{:S(2)}, u32[]{:S(2)}) collective-permute-start(f32[10,640]{1,0:T(8,128)S(1)} %dynamic-slice_bitcast_fusion.5), channel_id=1, source_target_pairs={{0,4},{4,0},{1,5},{5,1},{2,6},{6,2},{3,7},{7,3},{8,12},{12,8},{9,1... | collective-permute-start | bytes 76808 | tf_op jit(solution)/shard_map/ppermute | solution.py:23
  111.2 8.5 %collective-permute-start.13 = (f32[10,640]{1,0:T(8,128)S(1)}, f32[10,640]{1,0:T(8,128)S(1)}, u32[]{:S(2)}, u32[]{:S(2)}) collective-permute-start(f32[10,640]{1,0:T(8,128)S(1)} %get-tuple-element.37), channel_id=1, source_target_pairs={{0,1},{1,2},{2,3},{3,0},{4,5},{5,6},{6,7},{7,4},{8,9},{9,10},{10,1... | collective-permute-start | bytes 76808 | tf_op jit(solution)/shard_map/ppermute | solution.py:23
  111.3 8.4 %collective-permute-start.15 = (f32[10,640]{1,0:T(8,128)S(1)}, f32[10,640]{1,0:T(8,128)S(1)}, u32[]{:S(2)}, u32[]{:S(2)}) collective-permute-start(f32[10,640]{1,0:T(8,128)S(1)} %get-tuple-element.38), channel_id=1, source_target_pairs={{0,3},{1,0},{2,1},{3,2},{4,7},{5,4},{6,5},{7,6},{8,11},{9,8},{10,9... | collective-permute-start | bytes 76808 | tf_op jit(solution)/shard_map/ppermute | solution.py:23
  115.4 7.9 %collective-permute-start.14 = (f32[10,640]{1,0:T(8,128)S(1)}, f32[10,640]{1,0:T(8,128)S(1)}, u32[]{:S(2)}, u32[]{:S(2)}) collective-permute-start(f32[10,640]{1,0:T(8,128)S(1)} %get-tuple-element.39), channel_id=1, source_target_pairs={{0,2},{1,3},{2,0},{3,1},{4,6},{5,7},{6,4},{7,5},{8,10},{9,11},{10,... | collective-permute-start | bytes 76808 | tf_op jit(solution)/shard_map/ppermute | solution.py:23
  117.5 14.9 %collective-permute-start.12 = (f32[10,640]{1,0:T(8,128)S(1)}, f32[10,640]{1,0:T(8,128)S(1)}, u32[]{:S(2)}, u32[]{:S(2)}) collective-permute-start(f32[10,640]{1,0:T(8,128)S(1)} %bitcast_add_fusion.1), channel_id=1, source_target_pairs={{0,0},{4,4},{8,16},{12,20},{16,32},{20,36},{24,48},{28,52},{32,64}... | collective-permute-start | bytes 76808 | tf_op jit(solution)/shard_map/ppermute | solution.py:249
  123.4 9.1 %collective-permute-start.16 = (f32[10,640]{1,0:T(8,128)S(1)}, f32[10,640]{1,0:T(8,128)S(1)}, u32[]{:S(2)}, u32[]{:S(2)}) collective-permute-start(f32[10,640]{1,0:T(8,128)S(1)} %fusion.2), channel_id=1, source_target_pairs={{0,0},{4,128},{8,4},{12,132},{16,8},{20,136},{24,12},{28,140},{32,... | collective-permute-start | bytes 76808 | tf_op jit(solution)/shard_map/ppermute | solution.py:250
  132.4 4.1 %collective-permute-start.17 = (bf16[1280,640]{1,0:T(8,128)(2,1)S(1)}, bf16[1280,640]{1,0:T(8,128)(2,1)S(1)}, u32[]{:S(2)}, u32[]{:S(2)}) collective-permute-start(bf16[1280,640]{1,0:T(8,128)(2,1)S(1)} %bitcast.27), channel_id=1, source_target_pairs={{0,4},{4,0},{1,5},{5,1},{2,6},{6,2},{3,7},{7,3},{8,12},{12,8},{9,1... | collective-permute-start | bytes 4915208 | tf_op jit(solution)/shard_map/ppermute | solution.py:23
  138.6 4.8 %collective-permute-start.20 = (f32[8,128]{1,0:T(8,128)S(1)}, f32[8,128]{1,0:T(8,128)S(1)}, u32[]{:S(2)}, u32[]{:S(2)}) collective-permute-start(f32[8,128]{1,0:T(8,128)S(1)} %add.134.own), channel_id=1, source_target_pairs={{0,3},{1,0},{2,1},{3,2},{4,7},{5,4},{6,5},{7,6},{8,11},{9,8},{10,9... | collective-permute-start | bytes 12296 | tf_op jit(solution)/shard_map/ppermute | solution.py:23
  139.9 7.5 %collective-permute-start.19 = (f32[8,128]{1,0:T(8,128)S(1)}, f32[8,128]{1,0:T(8,128)S(1)}, u32[]{:S(2)}, u32[]{:S(2)}) collective-permute-start(f32[8,128]{1,0:T(8,128)S(1)} %add.134.own), channel_id=1, source_target_pairs={{0,2},{1,3},{2,0},{3,1},{4,6},{5,7},{6,4},{7,5},{8,10},{9,11},{10,... | collective-permute-start | bytes 12296 | tf_op jit(solution)/shard_map/ppermute | solution.py:23
  141.5 5.9 %collective-permute-start.18 = (f32[8,128]{1,0:T(8,128)S(1)}, f32[8,128]{1,0:T(8,128)S(1)}, u32[]{:S(2)}, u32[]{:S(2)}) collective-permute-start(f32[8,128]{1,0:T(8,128)S(1)} %add.134.own), channel_id=1, source_target_pairs={{0,1},{1,2},{2,3},{3,0},{4,5},{5,6},{6,7},{7,4},{8,9},{9,10},{10,1... | collective-permute-start | bytes 12296 | tf_op jit(solution)/shard_map/ppermute | solution.py:23
  (4 other events, 109.5 us)

commit v5 on v4

--- a/solution.py
+++ b/solution.py
@@ -249,7 +249,6 @@
     act_rows = lax.ppermute(act_rows, DP, act_perm)
     grad_rows = lax.ppermute(grad_rows, DP, grad_perm)
 
-    mine = after(mine, act_rows, grad_rows)
     theirs = swap_core(mine)
     order = core.astype(jnp.int32).reshape(1)
     out_mine, sq_mine = right_product(order, mine, grad_inverse)

time: 151 us -> 166 us (1.099)
  blocking collectives: 0 us -> 24.1 us
  starting transfers between devices: 59.3 us -> 54.2 us
  waiting for transfers between devices: 68.4 us -> 63.8 us
    all_to_all x0 -> x1, blocking collectives: none -> 24.1 us  [plane_exchange(): return lax.all_to_all(value, PLANE, split_axis=0, concat_axis=0, tiled=True)]
    all_to_all x3 -> x2, starting transfers between devices: 20.8 us -> 14.7 us  [plane_exchange(): return lax.all_to_all(value, PLANE, split_axis=0, concat_axis=0, tiled=True)]
    ppermute x1, waiting for transfers between devices: 3.32 us -> 0.01 us  [body(): act_rows = lax.ppermute(act_rows, DP, act_perm)]
    ppermute x19, starting transfers between devices: 30.6 us -> 32.3 us  [shift(): lax.ppermute(value, axis, [(i, (i + step) % count) for i in range(count)])]
    all_to_all x3 -> x2, waiting for transfers between devices: 13.5 us -> 13.5 us  [plane_exchange(): return lax.all_to_all(value, PLANE, split_axis=0, concat_axis=0, tiled=True)]
  transfers between devices with their start and end apart: 24 -> 23, of which waited for: 13 -> 13; matrix products, arithmetic and copies ran while one was open for 3% -> 2% of each run, Pallas kernels for 4% -> 6%
where the time goes in v5:
time: 166 us; the launch traced here: 165 us
  waiting for transfers between devices  63.8 us (38%)
  starting transfers between devices  54.2 us (33%)
  blocking collectives  24.1 us (15%)
  Pallas kernels  15 us (9%)
  local copies, waits for them, and re-layouts  3.67 us (2%)
  other arithmetic  2.55 us (2%)
    ppermute x19, waiting for transfers between devices, shift(): lax.ppermute(value, axis, [(i, (i + step) % count) for i in range(count)])  50.2 us
    ppermute x19, starting transfers between devices, shift(): lax.ppermute(value, axis, [(i, (i + step) % count) for i in range(count)])  32.3 us
    all_to_all x1, blocking collectives, plane_exchange(): return lax.all_to_all(value, PLANE, split_axis=0, concat_axis=0, tiled=True)  24.1 us
    all_to_all x2, starting transfers between devices, plane_exchange(): return lax.all_to_all(value, PLANE, split_axis=0, concat_axis=0, tiled=True)  14.7 us
    all_to_all x2, waiting for transfers between devices, plane_exchange(): return lax.all_to_all(value, PLANE, split_axis=0, concat_axis=0, tiled=True)  13.5 us
    pallas_call x2, Pallas kernels, right_product(): pl.pallas_call(right_kernel, out_shape=(jax.ShapeDtypeStruct((2, width, w...  5.7 us
    ppermute x1, starting transfers between devices, body(): grad_rows = lax.ppermute(grad_rows, DP, grad_perm)  4.85 us
  transfers between devices with their start and end apart: 23, of which 13 were waited for; matrix products, arithmetic and copies ran while one was open for 2% of the time, Pallas kernels for 6%

profile of v5, /device:TPU:6, one launch (start us, length us, event | category | flops | bytes accessed | tf_op | source)
XLA Modules:
  0.0 165.2 jit_solution(4946375762147841998)
XLA Ops:
  4.0 2.7 %cov_partial.1 = bf16[16,3,40,640]{3,2,1,0:T(8,128)(2,1)} custom-call(bf16[256,640]{1,0:T(8,128)(2,1)S(1)} %pad_maximum_fusion.refs_0_.first, bf16[256,640]{1,0:T(8,128)(2,1)S(1)} %pad_maximum_fusion.1.refs_3_.second, bf16[512,640]{1,0:T(8,128)(2,1)S(1)} %copy-done.3), custom_call_target="tpu_custom_call" | custom-call | flops 838860800 | bytes 5242880 | tf_op jit(solution)/shard_map/cov_partial/pallas_call | solution.py:91
  6.7 7.4 %all-to-all-start = ((bf16[16,3,40,640]{3,2,1,0:T(8,128)(2,1)}), bf16[16,3,40,640]{3,2,1,0:T(8,128)(2,1)}, u32[]{:S(2)}, u32[]{:S(2)}) async-start(bf16[16,3,40,640]{3,2,1,0:T(8,128)(2,1)} %cov_partial.1), calls=%async_computation | async-start | bytes 4915200 | tf_op jit(solution)/shard_map/all_to_all | solution.py:168
  14.1 6.3 %collective-permute-start.5 = (bf16[256,640]{1,0:T(8,128)(2,1)S(1)}, bf16[256,640]{1,0:T(8,128)(2,1)S(1)}, u32[]{:S(2)}, u32[]{:S(2)}) collective-permute-start(bf16[256,640]{1,0:T(8,128)(2,1)S(1)} %pad_maximum_fusion.1.refs_3_.second), channel_id=1, source_target_pairs={{0,3},{1,0},{2,1},{3,2},{4,7},{5,4},{6,5},{7,6},{8,11},{9,8},{10,9... | collective-permute-start | bytes 983048 | tf_op jit(solution)/shard_map/ppermute | solution.py:23
  22.1 2.7 %collective-permute-start.2 = (bf16[256,640]{1,0:T(8,128)(2,1)S(1)}, bf16[256,640]{1,0:T(8,128)(2,1)S(1)}, u32[]{:S(2)}, u32[]{:S(2)}) collective-permute-start(bf16[256,640]{1,0:T(8,128)(2,1)S(1)} %pad_maximum_fusion.refs_0_.first), channel_id=1, source_target_pairs={{0,3},{1,0},{2,1},{3,2},{4,7},{5,4},{6,5},{7,6},{8,11},{9,8},{10,9... | collective-permute-start | bytes 983048 | tf_op jit(solution)/shard_map/ppermute | solution.py:23
  24.8 14.0 %collective-permute-done.5.refs_5_ = bf16[256,640]{1,0:T(8,128)(2,1)S(1)} collective-permute-done((bf16[256,640]{1,0:T(8,128)(2,1)S(1)}, bf16[256,640]{1,0:T(8,128)(2,1)S(1)}, u32[]{:S(2)}, u32[]{:S(2)}) %collective-permute-start.5) | collective-permute-done | bytes 327712 | tf_op jit(solution)/shard_map/ppermute | solution.py:23
  38.7 6.3 %collective-permute-start.8 = (bf16[256,640]{1,0:T(8,128)(2,1)S(1)}, bf16[256,640]{1,0:T(8,128)(2,1)S(1)}, u32[]{:S(2)}, u32[]{:S(2)}) collective-permute-start(bf16[256,640]{1,0:T(8,128)(2,1)S(1)} %collective-permute-done.5.refs_5_), channel_id=1, source_target_pairs={{0,3},{1,0},{2,1},{3,2},{4,7},{5,4},{6,5},{7,6},{8,11},{9,8},{10,9... | collective-permute-start | bytes 983048 | tf_op jit(solution)/shard_map/ppermute | solution.py:23
  46.8 7.4 %collective-permute-done.2.refs_2_ = bf16[256,640]{1,0:T(8,128)(2,1)S(1)} collective-permute-done((bf16[256,640]{1,0:T(8,128)(2,1)S(1)}, bf16[256,640]{1,0:T(8,128)(2,1)S(1)}, u32[]{:S(2)}, u32[]{:S(2)}) %collective-permute-start.2) | collective-permute-done | bytes 327712 | tf_op jit(solution)/shard_map/ppermute | solution.py:23
  56.0 6.4 %collective-permute-done.8.second = bf16[256,640]{1,0:T(8,128)(2,1)S(1)} collective-permute-done((bf16[256,640]{1,0:T(8,128)(2,1)S(1)}, bf16[256,640]{1,0:T(8,128)(2,1)S(1)}, u32[]{:S(2)}, u32[]{:S(2)}) %collective-permute-start.8) | collective-permute-done | bytes 327712 | tf_op jit(solution)/shard_map/ppermute | solution.py:23
  62.3 3.8 %collective-permute-done.7.first = bf16[256,640]{1,0:T(8,128)(2,1)S(1)} collective-permute-done((bf16[256,640]{1,0:T(8,128)(2,1)S(1)}, bf16[256,640]{1,0:T(8,128)(2,1)S(1)}, u32[]{:S(2)}, u32[]{:S(2)}) %collective-permute-start.7) | collective-permute-done | bytes 327712 | tf_op jit(solution)/shard_map/ppermute | solution.py:23
  68.1 7.2 %all-to-all-start.1 = ((bf16[16,80,640]{2,1,0:T(8,128)(2,1)}), bf16[16,80,640]{2,1,0:T(8,128)(2,1)S(1)}, u32[]{:S(2)}, u32[]{:S(2)}) async-start(bf16[16,80,640]{2,1,0:T(8,128)(2,1)} %weight_partial.1), calls=%async_computation.1 | async-start | bytes 3276800 | tf_op jit(solution)/shard_map/all_to_all | solution.py:168
  75.3 2.1 %convert_reduce_fusion = f32[3,40,640]{2,1,0:T(8,128)S(1)} fusion(bf16[16,3,40,640]{3,2,1,0:T(8,128)(2,1)} %all-to-all-done), kind=kLoop, calls=%fused_computation | loop fusion | flops 2380800 | bytes 2764800 | tf_op jit(solution)/shard_map/reduce_sum | solution.py:211
  79.1 3.8 %collective-permute-done.9 = f32[60,640]{1,0:T(8,128)S(1)} collective-permute-done((f32[60,640]{1,0:T(8,128)S(1)}, f32[60,640]{1,0:T(8,128)S(1)}, u32[]{:S(2)}, u32[]{:S(2)}) %collective-permute-start.9) | collective-permute-done | bytes 153632 | tf_op jit(solution)/shard_map/ppermute | solution.py:23
  82.9 13.5 %all-to-all-done.1 = bf16[16,80,640]{2,1,0:T(8,128)(2,1)S(1)} async-done(((bf16[16,80,640]{2,1,0:T(8,128)(2,1)}), bf16[16,80,640]{2,1,0:T(8,128)(2,1)S(1)}, u32[]{:S(2)}, u32[]{:S(2)}) %all-to-all-start.1) | async-done | bytes 1638432 | tf_op jit(solution)/shard_map/all_to_all | solution.py:168
  97.0 5.7 %collective-permute-done.10 = f32[80,640]{1,0:T(8,128)S(1)} collective-permute-done((f32[80,640]{1,0:T(8,128)S(1)}, f32[80,640]{1,0:T(8,128)S(1)}, u32[]{:S(2)}, u32[]{:S(2)}) %collective-permute-start.10) | collective-permute-done | bytes 204832 | tf_op jit(solution)/shard_map/ppermute | solution.py:23
  103.7 24.1 %all_to_all.15 = bf16[16,80,640]{2,1,0:T(8,128)(2,1)S(1)} all-to-all(bf16[16,80,640]{2,1,0:T(8,128)(2,1)S(1)} %broadcast_in_dim.2), channel_id=1, replica_groups=mesh['zlo'=2,'x'=4,'y'=4,'core'=2,'zhi'=4] {'x','y'}, dimensions={0} | all-to-all | bytes 3276800 | tf_op jit(solution)/shard_map/all_to_all | solution.py:168
  128.7 4.1 %collective-permute-start.19 = (f32[10,640]{1,0:T(8,128)S(1)}, f32[10,640]{1,0:T(8,128)S(1)}, u32[]{:S(2)}, u32[]{:S(2)}) collective-permute-start(f32[10,640]{1,0:T(8,128)S(1)} %get-tuple-element.36), channel_id=1, source_target_pairs={{0,3},{1,0},{2,1},{3,2},{4,7},{5,4},{6,5},{7,6},{8,11},{9,8},{10,9... | collective-permute-start | bytes 76808 | tf_op jit(solution)/shard_map/ppermute | solution.py:23
  134.9 2.5 %collective-permute-start.16 = (f32[10,640]{1,0:T(8,128)S(1)}, f32[10,640]{1,0:T(8,128)S(1)}, u32[]{:S(2)}, u32[]{:S(2)}) collective-permute-start(f32[10,640]{1,0:T(8,128)S(1)} %bitcast_add_fusion.1), channel_id=1, source_target_pairs={{0,0},{4,4},{8,16},{12,20},{16,32},{20,36},{24,48},{28,52},{32,64}... | collective-permute-start | bytes 76808 | tf_op jit(solution)/shard_map/ppermute | solution.py:249
  137.4 3.4 %collective-permute-done.18 = f32[10,640]{1,0:T(8,128)S(1)} collective-permute-done((f32[10,640]{1,0:T(8,128)S(1)}, f32[10,640]{1,0:T(8,128)S(1)}, u32[]{:S(2)}, u32[]{:S(2)}) %collective-permute-start.18) | collective-permute-done | bytes 25632 | tf_op jit(solution)/shard_map/ppermute | solution.py:23
  140.7 4.8 %collective-permute-start.20 = (f32[10,640]{1,0:T(8,128)S(1)}, f32[10,640]{1,0:T(8,128)S(1)}, u32[]{:S(2)}, u32[]{:S(2)}) collective-permute-start(f32[10,640]{1,0:T(8,128)S(1)} %fusion.2), channel_id=1, source_target_pairs={{0,0},{4,128},{8,4},{12,132},{16,8},{20,136},{24,12},{28,140},{32,... | collective-permute-start | bytes 76808 | tf_op jit(solution)/shard_map/ppermute | solution.py:250
  147.5 2.1 %right_product.2 = (f32[2,640,640]{2,1,0:T(8,128)S(1)}, f32[8,128]{1,0:T(8,128)S(1)}) custom-call(s32[1]{0:T(128)} %bitcast.half_index.core, bf16[1280,640]{1,0:T(8,128)(2,1)S(1)} %bitcast.28, bf16[2560,640]{1,0:T(8,128)(2,1)S(1)} %copy-done.1), custom_call_target="tpu_custom_call" | custom-call | flops 1048576000 | bytes 6291456 | tf_op jit(solution)/shard_map/right_product/pallas_call | solution.py:115
  149.7 3.6 %right_product.3 = (f32[2,640,640]{2,1,0:T(8,128)S(1)}, f32[8,128]{1,0:T(8,128)S(1)}) custom-call(s32[1]{0:T(128)S(6)} %sub.14.half_index, bf16[1280,640]{1,0:T(8,128)(2,1)} %collective-permute-done.11.left, bf16[2560,640]{1,0:T(8,128)(2,1)S(1)} %copy-done.2), custom_call_target="tpu_custom_call" | custom-call | flops 1048576000 | bytes 6291456 | tf_op jit(solution)/shard_map/right_product/pallas_call | solution.py:115
  153.6 2.9 %collective-permute-start.13 = (f32[8,128]{1,0:T(8,128)S(1)}, f32[8,128]{1,0:T(8,128)S(1)}, u32[]{:S(2)}, u32[]{:S(2)}) collective-permute-start(f32[8,128]{1,0:T(8,128)S(1)} %add.121.own), channel_id=1, source_target_pairs={{0,2},{1,3},{2,0},{3,1},{4,6},{5,7},{6,4},{7,5},{8,10},{9,11},{10,... | collective-permute-start | bytes 12296 | tf_op jit(solution)/shard_map/ppermute | solution.py:23
  156.5 2.8 %collective-permute-start.12 = (f32[8,128]{1,0:T(8,128)S(1)}, f32[8,128]{1,0:T(8,128)S(1)}, u32[]{:S(2)}, u32[]{:S(2)}) collective-permute-start(f32[8,128]{1,0:T(8,128)S(1)} %add.121.own), channel_id=1, source_target_pairs={{0,1},{1,2},{2,3},{3,0},{4,5},{5,6},{6,7},{7,4},{8,9},{9,10},{10,1... | collective-permute-start | bytes 12296 | tf_op jit(solution)/shard_map/ppermute | solution.py:23
  162.2 3.0 %final_update.1 = (bf16[640,2560]{1,0:T(8,128)(2,1)}, f32[10,640]{1,0:T(8,128)}, f32[10,640]{1,0:T(8,128)}) custom-call(s32[1]{0:T(128)} %bitcast.half_index.core, f32[8,128]{1,0:T(8,128)S(1)} %add.121.own, f32[8,128]{1,0:T(8,128)S(1)} %collective-permute-done.12.sq_a, f32[8,128]{1,0:T(8,128)S(1)} %collective-permute-done.13.sq_b, ...), custom_call_target="tpu_custom_call" | custom-call | flops 1638400 | bytes 10485760 | tf_op jit(solution)/shard_map/final_update/pallas_call | solution.py:155
  (64 shorter events, 21.6 us)
Async XLA Ops:
  0.6 102.1 %copy-start = (bf16[640,640]{1,0:T(8,128)(2,1)S(1)}, bf16[640,640]{1,0:T(8,128)(2,1)}, u32[]{:S(2)}) copy-start(bf16[640,640]{1,0:T(8,128)(2,1)} %param.6) | copy-start | bytes 2457604
  0.7 3.3 %collective-permute-start.6 = (bf16[512,640]{1,0:T(8,128)(2,1)}, bf16[512,640]{1,0:T(8,128)(2,1)S(1)}, u32[]{:S(2)}, u32[]{:S(2)}) collective-permute-start(bf16[512,640]{1,0:T(8,128)(2,1)} %acts.1), channel_id=1, source_target_pairs={{0,4},{4,0},{1,5},{5,1},{2,6},{6,2},{3,7},{7,3},{8,12},{12,8},{9,1... | collective-permute-start | bytes 1966088 | tf_op jit(solution)/shard_map/ppermute | solution.py:23
  2.1 1.5 collective-permute-start
  2.6 1.4 collective-permute-start.3
  6.7 61.4 %all-to-all-start = ((bf16[16,3,40,640]{3,2,1,0:T(8,128)(2,1)}), bf16[16,3,40,640]{3,2,1,0:T(8,128)(2,1)}, u32[]{:S(2)}, u32[]{:S(2)}) async-start(bf16[16,3,40,640]{3,2,1,0:T(8,128)(2,1)} %cov_partial.1), calls=%async_computation | async-start | bytes 4915200 | tf_op jit(solution)/shard_map/all_to_all | solution.py:168
  14.1 24.6 %collective-permute-start.5 = (bf16[256,640]{1,0:T(8,128)(2,1)S(1)}, bf16[256,640]{1,0:T(8,128)(2,1)S(1)}, u32[]{:S(2)}, u32[]{:S(2)}) collective-permute-start(bf16[256,640]{1,0:T(8,128)(2,1)S(1)} %pad_maximum_fusion.1.refs_3_.second), channel_id=1, source_target_pairs={{0,3},{1,0},{2,1},{3,2},{4,7},{5,4},{6,5},{7,6},{8,11},{9,8},{10,9... | collective-permute-start | bytes 983048 | tf_op jit(solution)/shard_map/ppermute | solution.py:23
  20.4 24.6 %collective-permute-start.1 = (bf16[256,640]{1,0:T(8,128)(2,1)S(1)}, bf16[256,640]{1,0:T(8,128)(2,1)S(1)}, u32[]{:S(2)}, u32[]{:S(2)}) collective-permute-start(bf16[256,640]{1,0:T(8,128)(2,1)S(1)} %pad_maximum_fusion.refs_0_.first), channel_id=1, source_target_pairs={{0,1},{1,2},{2,3},{3,0},{4,5},{5,6},{6,7},{7,4},{8,9},{9,10},{10,1... | collective-permute-start | bytes 983048 | tf_op jit(solution)/shard_map/ppermute | solution.py:23
  20.5 26.3 %collective-permute-start.4 = (bf16[256,640]{1,0:T(8,128)(2,1)S(1)}, bf16[256,640]{1,0:T(8,128)(2,1)S(1)}, u32[]{:S(2)}, u32[]{:S(2)}) collective-permute-start(bf16[256,640]{1,0:T(8,128)(2,1)S(1)} %pad_maximum_fusion.1.refs_3_.second), channel_id=1, source_target_pairs={{0,1},{1,2},{2,3},{3,0},{4,5},{5,6},{6,7},{7,4},{8,9},{9,10},{10,1... | collective-permute-start | bytes 983048 | tf_op jit(solution)/shard_map/ppermute | solution.py:23
  22.1 32.1 %collective-permute-start.2 = (bf16[256,640]{1,0:T(8,128)(2,1)S(1)}, bf16[256,640]{1,0:T(8,128)(2,1)S(1)}, u32[]{:S(2)}, u32[]{:S(2)}) collective-permute-start(bf16[256,640]{1,0:T(8,128)(2,1)S(1)} %pad_maximum_fusion.refs_0_.first), channel_id=1, source_target_pairs={{0,3},{1,0},{2,1},{3,2},{4,7},{5,4},{6,5},{7,6},{8,11},{9,8},{10,9... | collective-permute-start | bytes 983048 | tf_op jit(solution)/shard_map/ppermute | solution.py:23
  38.7 23.6 %collective-permute-start.8 = (bf16[256,640]{1,0:T(8,128)(2,1)S(1)}, bf16[256,640]{1,0:T(8,128)(2,1)S(1)}, u32[]{:S(2)}, u32[]{:S(2)}) collective-permute-start(bf16[256,640]{1,0:T(8,128)(2,1)S(1)} %collective-permute-done.5.refs_5_), channel_id=1, source_target_pairs={{0,3},{1,0},{2,1},{3,2},{4,7},{5,4},{6,5},{7,6},{8,11},{9,8},{10,9... | collective-permute-start | bytes 983048 | tf_op jit(solution)/shard_map/ppermute | solution.py:23
  45.0 21.2 %collective-permute-start.7 = (bf16[256,640]{1,0:T(8,128)(2,1)S(1)}, bf16[256,640]{1,0:T(8,128)(2,1)S(1)}, u32[]{:S(2)}, u32[]{:S(2)}) collective-permute-start(bf16[256,640]{1,0:T(8,128)(2,1)S(1)} %collective-permute-done.1.refs_1_), channel_id=1, source_target_pairs={{0,1},{1,2},{2,3},{3,0},{4,5},{5,6},{6,7},{7,4},{8,9},{9,10},{10,1... | collective-permute-start | bytes 983048 | tf_op jit(solution)/shard_map/ppermute | solution.py:23
  68.1 28.4 %all-to-all-start.1 = ((bf16[16,80,640]{2,1,0:T(8,128)(2,1)}), bf16[16,80,640]{2,1,0:T(8,128)(2,1)S(1)}, u32[]{:S(2)}, u32[]{:S(2)}) async-start(bf16[16,80,640]{2,1,0:T(8,128)(2,1)} %weight_partial.1), calls=%async_computation.1 | async-start | bytes 3276800 | tf_op jit(solution)/shard_map/all_to_all | solution.py:168
  77.5 5.4 %collective-permute-start.9 = (f32[60,640]{1,0:T(8,128)S(1)}, f32[60,640]{1,0:T(8,128)S(1)}, u32[]{:S(2)}, u32[]{:S(2)}) collective-permute-start(f32[60,640]{1,0:T(8,128)S(1)} %pad_maximum_fusion.6), channel_id=1, source_target_pairs={{0,128},{128,0},{1,129},{129,1},{2,130},{130,2},{3,131},{131,3},{4... | collective-permute-start | bytes 460808 | tf_op jit(solution)/shard_map/ppermute | solution.py:23
  96.7 6.0 %collective-permute-start.10 = (f32[80,640]{1,0:T(8,128)S(1)}, f32[80,640]{1,0:T(8,128)S(1)}, u32[]{:S(2)}, u32[]{:S(2)}) collective-permute-start(f32[80,640]{1,0:T(8,128)S(1)} %convert_reduce_fusion.1), channel_id=1, source_target_pairs={{0,128},{128,0},{1,129},{129,1},{2,130},{130,2},{3,131},{131,3},{4... | collective-permute-start | bytes 614408 | tf_op jit(solution)/shard_map/ppermute | solution.py:23
  127.9 21.8 %collective-permute-start.11 = (bf16[1280,640]{1,0:T(8,128)(2,1)S(1)}, bf16[1280,640]{1,0:T(8,128)(2,1)}, u32[]{:S(2)}, u32[]{:S(2)}) collective-permute-start(bf16[1280,640]{1,0:T(8,128)(2,1)S(1)} %bitcast.27), channel_id=1, source_target_pairs={{0,4},{4,0},{1,5},{5,1},{2,6},{6,2},{3,7},{7,3},{8,12},{12,8},{9,1... | collective-permute-start | bytes 4915208 | tf_op jit(solution)/shard_map/ppermute | solution.py:23
  127.9 7.0 %collective-permute-start.15 = (f32[10,640]{1,0:T(8,128)S(1)}, f32[10,640]{1,0:T(8,128)S(1)}, u32[]{:S(2)}, u32[]{:S(2)}) collective-permute-start(f32[10,640]{1,0:T(8,128)S(1)} %dynamic-slice_bitcast_fusion.5), channel_id=1, source_target_pairs={{0,4},{4,0},{1,5},{5,1},{2,6},{6,2},{3,7},{7,3},{8,12},{12,8},{9,1... | collective-permute-start | bytes 76808 | tf_op jit(solution)/shard_map/ppermute | solution.py:23
  128.6 8.8 %collective-permute-start.17 = (f32[10,640]{1,0:T(8,128)S(1)}, f32[10,640]{1,0:T(8,128)S(1)}, u32[]{:S(2)}, u32[]{:S(2)}) collective-permute-start(f32[10,640]{1,0:T(8,128)S(1)} %get-tuple-element.35), channel_id=1, source_target_pairs={{0,1},{1,2},{2,3},{3,0},{4,5},{5,6},{6,7},{7,4},{8,9},{9,10},{10,1... | collective-permute-start | bytes 76808 | tf_op jit(solution)/shard_map/ppermute | solution.py:23
  128.7 8.7 %collective-permute-start.19 = (f32[10,640]{1,0:T(8,128)S(1)}, f32[10,640]{1,0:T(8,128)S(1)}, u32[]{:S(2)}, u32[]{:S(2)}) collective-permute-start(f32[10,640]{1,0:T(8,128)S(1)} %get-tuple-element.36), channel_id=1, source_target_pairs={{0,3},{1,0},{2,1},{3,2},{4,7},{5,4},{6,5},{7,6},{8,11},{9,8},{10,9... | collective-permute-start | bytes 76808 | tf_op jit(solution)/shard_map/ppermute | solution.py:23
  132.8 7.9 %collective-permute-start.18 = (f32[10,640]{1,0:T(8,128)S(1)}, f32[10,640]{1,0:T(8,128)S(1)}, u32[]{:S(2)}, u32[]{:S(2)}) collective-permute-start(f32[10,640]{1,0:T(8,128)S(1)} %get-tuple-element.37), channel_id=1, source_target_pairs={{0,2},{1,3},{2,0},{3,1},{4,6},{5,7},{6,4},{7,5},{8,10},{9,11},{10,... | collective-permute-start | bytes 76808 | tf_op jit(solution)/shard_map/ppermute | solution.py:23
  134.9 24.4 %collective-permute-start.16 = (f32[10,640]{1,0:T(8,128)S(1)}, f32[10,640]{1,0:T(8,128)S(1)}, u32[]{:S(2)}, u32[]{:S(2)}) collective-permute-start(f32[10,640]{1,0:T(8,128)S(1)} %bitcast_add_fusion.1), channel_id=1, source_target_pairs={{0,0},{4,4},{8,16},{12,20},{16,32},{20,36},{24,48},{28,52},{32,64}... | collective-permute-start | bytes 76808 | tf_op jit(solution)/shard_map/ppermute | solution.py:249
  140.7 18.5 %collective-permute-start.20 = (f32[10,640]{1,0:T(8,128)S(1)}, f32[10,640]{1,0:T(8,128)S(1)}, u32[]{:S(2)}, u32[]{:S(2)}) collective-permute-start(f32[10,640]{1,0:T(8,128)S(1)} %fusion.2), channel_id=1, source_target_pairs={{0,0},{4,128},{8,4},{12,132},{16,8},{20,136},{24,12},{28,140},{32,... | collective-permute-start | bytes 76808 | tf_op jit(solution)/shard_map/ppermute | solution.py:250
  153.3 6.0 %collective-permute-start.14 = (f32[8,128]{1,0:T(8,128)S(1)}, f32[8,128]{1,0:T(8,128)S(1)}, u32[]{:S(2)}, u32[]{:S(2)}) collective-permute-start(f32[8,128]{1,0:T(8,128)S(1)} %add.121.own), channel_id=1, source_target_pairs={{0,3},{1,0},{2,1},{3,2},{4,7},{5,4},{6,5},{7,6},{8,11},{9,8},{10,9... | collective-permute-start | bytes 12296 | tf_op jit(solution)/shard_map/ppermute | solution.py:23
  153.6 7.5 %collective-permute-start.13 = (f32[8,128]{1,0:T(8,128)S(1)}, f32[8,128]{1,0:T(8,128)S(1)}, u32[]{:S(2)}, u32[]{:S(2)}) collective-permute-start(f32[8,128]{1,0:T(8,128)S(1)} %add.121.own), channel_id=1, source_target_pairs={{0,2},{1,3},{2,0},{3,1},{4,6},{5,7},{6,4},{7,5},{8,10},{9,11},{10,... | collective-permute-start | bytes 12296 | tf_op jit(solution)/shard_map/ppermute | solution.py:23
  156.5 5.7 %collective-permute-start.12 = (f32[8,128]{1,0:T(8,128)S(1)}, f32[8,128]{1,0:T(8,128)S(1)}, u32[]{:S(2)}, u32[]{:S(2)}) collective-permute-start(f32[8,128]{1,0:T(8,128)S(1)} %add.121.own), channel_id=1, source_target_pairs={{0,1},{1,2},{2,3},{3,0},{4,5},{5,6},{6,7},{7,4},{8,9},{9,10},{10,1... | collective-permute-start | bytes 12296 | tf_op jit(solution)/shard_map/ppermute | solution.py:23
  (3 other events, 7.4 us)

commit v6 on v5

--- a/solution.py
+++ b/solution.py
@@ -246,9 +246,11 @@
     ).astype(BF16)
     copies = jnp.broadcast_to(mixed[None], (sites, 2 * rows, width))
     mine = plane_exchange(copies).reshape(half, width)
+    summed_rows = (act_rows, grad_rows)
     act_rows = lax.ppermute(act_rows, DP, act_perm)
     grad_rows = lax.ppermute(grad_rows, DP, grad_perm)
 
+    mine = after(mine, *summed_rows)
     theirs = swap_core(mine)
     order = core.astype(jnp.int32).reshape(1)
     out_mine, sq_mine = right_product(order, mine, grad_inverse)

time: 166 us -> 158 us (0.952)
  blocking collectives: 24.1 us -> 0 us
  waiting for transfers between devices: 63.8 us -> 73.4 us
  starting transfers between devices: 54.2 us -> 61.4 us
    all_to_all x1 -> x0, blocking collectives: 24.1 us -> none  [plane_exchange(): return lax.all_to_all(value, PLANE, split_axis=0, concat_axis=0, tiled=True)]
    all_to_all x2 -> x3, waiting for transfers between devices: 13.5 us -> 19.8 us  [plane_exchange(): return lax.all_to_all(value, PLANE, split_axis=0, concat_axis=0, tiled=True)]
    all_to_all x2 -> x3, starting transfers between devices: 14.7 us -> 20.8 us  [plane_exchange(): return lax.all_to_all(value, PLANE, split_axis=0, concat_axis=0, tiled=True)]
    ppermute x19, waiting for transfers between devices: 50.2 us -> 53.6 us  [shift(): lax.ppermute(value, axis, [(i, (i + step) % count) for i in range(count)])]
    ppermute x1, starting transfers between devices: 4.85 us -> 7.56 us  [body(): grad_rows = lax.ppermute(grad_rows, DP, grad_perm)]
  transfers between devices with their start and end apart: 23 -> 24, of which waited for: 13 -> 14; matrix products, arithmetic and copies ran while one was open for 2% -> 2% of each run, Pallas kernels for 6% -> 5%
where the time goes in v6:
time: 158 us
  waiting for transfers between devices  73.4 us (46%)
  starting transfers between devices  61.4 us (39%)
  Pallas kernels  13.5 us (9%)
  local copies, waits for them, and re-layouts  4.84 us (3%)
  other arithmetic  2.55 us (2%)
    ppermute x19, waiting for transfers between devices, shift(): lax.ppermute(value, axis, [(i, (i + step) % count) for i in range(count)])  53.6 us
    ppermute x19, starting transfers between devices, shift(): lax.ppermute(value, axis, [(i, (i + step) % count) for i in range(count)])  30.9 us
    all_to_all x3, starting transfers between devices, plane_exchange(): return lax.all_to_all(value, PLANE, split_axis=0, concat_axis=0, tiled=True)  20.8 us
    all_to_all x3, waiting for transfers between devices, plane_exchange(): return lax.all_to_all(value, PLANE, split_axis=0, concat_axis=0, tiled=True)  19.8 us
    ppermute x1, starting transfers between devices, body(): grad_rows = lax.ppermute(grad_rows, DP, grad_perm)  7.56 us
    pallas_call x2, Pallas kernels, right_product(): pl.pallas_call(right_kernel, out_shape=(jax.ShapeDtypeStruct((2, width, w...  4.22 us
  transfers between devices with their start and end apart: 24, of which 14 were waited for; matrix products, arithmetic and copies ran while one was open for 2% of the time, Pallas kernels for 5%

profile of v6, /device:TPU:6, one launch (start us, length us, event | category | flops | bytes accessed | tf_op | source)
XLA Modules:
  0.0 157.6 jit_solution(1637200016758425659)
XLA Ops:
  4.0 2.7 %cov_partial.1 = bf16[16,3,40,640]{3,2,1,0:T(8,128)(2,1)} custom-call(bf16[256,640]{1,0:T(8,128)(2,1)S(1)} %pad_maximum_fusion.refs_0_.first, bf16[256,640]{1,0:T(8,128)(2,1)S(1)} %pad_maximum_fusion.1.refs_3_.second, bf16[512,640]{1,0:T(8,128)(2,1)S(1)} %copy-done.3), custom_call_target="tpu_custom_call" | custom-call | flops 838860800 | bytes 5242880 | tf_op jit(solution)/shard_map/cov_partial/pallas_call | solution.py:91
  6.7 7.4 %all-to-all-start = ((bf16[16,3,40,640]{3,2,1,0:T(8,128)(2,1)}), bf16[16,3,40,640]{3,2,1,0:T(8,128)(2,1)}, u32[]{:S(2)}, u32[]{:S(2)}) async-start(bf16[16,3,40,640]{3,2,1,0:T(8,128)(2,1)} %cov_partial.1), calls=%async_computation | async-start | bytes 4915200 | tf_op jit(solution)/shard_map/all_to_all | solution.py:168
  14.1 6.3 %collective-permute-start.5 = (bf16[256,640]{1,0:T(8,128)(2,1)S(1)}, bf16[256,640]{1,0:T(8,128)(2,1)S(1)}, u32[]{:S(2)}, u32[]{:S(2)}) collective-permute-start(bf16[256,640]{1,0:T(8,128)(2,1)S(1)} %pad_maximum_fusion.1.refs_3_.second), channel_id=1, source_target_pairs={{0,3},{1,0},{2,1},{3,2},{4,7},{5,4},{6,5},{7,6},{8,11},{9,8},{10,9... | collective-permute-start | bytes 983048 | tf_op jit(solution)/shard_map/ppermute | solution.py:23
  22.1 2.7 %collective-permute-start.2 = (bf16[256,640]{1,0:T(8,128)(2,1)S(1)}, bf16[256,640]{1,0:T(8,128)(2,1)S(1)}, u32[]{:S(2)}, u32[]{:S(2)}) collective-permute-start(bf16[256,640]{1,0:T(8,128)(2,1)S(1)} %pad_maximum_fusion.refs_0_.first), channel_id=1, source_target_pairs={{0,3},{1,0},{2,1},{3,2},{4,7},{5,4},{6,5},{7,6},{8,11},{9,8},{10,9... | collective-permute-start | bytes 983048 | tf_op jit(solution)/shard_map/ppermute | solution.py:23
  24.8 14.0 %collective-permute-done.5.refs_5_ = bf16[256,640]{1,0:T(8,128)(2,1)S(1)} collective-permute-done((bf16[256,640]{1,0:T(8,128)(2,1)S(1)}, bf16[256,640]{1,0:T(8,128)(2,1)S(1)}, u32[]{:S(2)}, u32[]{:S(2)}) %collective-permute-start.5) | collective-permute-done | bytes 327712 | tf_op jit(solution)/shard_map/ppermute | solution.py:23
  38.7 6.3 %collective-permute-start.8 = (bf16[256,640]{1,0:T(8,128)(2,1)S(1)}, bf16[256,640]{1,0:T(8,128)(2,1)S(1)}, u32[]{:S(2)}, u32[]{:S(2)}) collective-permute-start(bf16[256,640]{1,0:T(8,128)(2,1)S(1)} %collective-permute-done.5.refs_5_), channel_id=1, source_target_pairs={{0,3},{1,0},{2,1},{3,2},{4,7},{5,4},{6,5},{7,6},{8,11},{9,8},{10,9... | collective-permute-start | bytes 983048 | tf_op jit(solution)/shard_map/ppermute | solution.py:23
  46.8 7.4 %collective-permute-done.2.refs_2_ = bf16[256,640]{1,0:T(8,128)(2,1)S(1)} collective-permute-done((bf16[256,640]{1,0:T(8,128)(2,1)S(1)}, bf16[256,640]{1,0:T(8,128)(2,1)S(1)}, u32[]{:S(2)}, u32[]{:S(2)}) %collective-permute-start.2) | collective-permute-done | bytes 327712 | tf_op jit(solution)/shard_map/ppermute | solution.py:23
  56.0 6.4 %collective-permute-done.8.second = bf16[256,640]{1,0:T(8,128)(2,1)S(1)} collective-permute-done((bf16[256,640]{1,0:T(8,128)(2,1)S(1)}, bf16[256,640]{1,0:T(8,128)(2,1)S(1)}, u32[]{:S(2)}, u32[]{:S(2)}) %collective-permute-start.8) | collective-permute-done | bytes 327712 | tf_op jit(solution)/shard_map/ppermute | solution.py:23
  62.3 3.8 %collective-permute-done.7.first = bf16[256,640]{1,0:T(8,128)(2,1)S(1)} collective-permute-done((bf16[256,640]{1,0:T(8,128)(2,1)S(1)}, bf16[256,640]{1,0:T(8,128)(2,1)S(1)}, u32[]{:S(2)}, u32[]{:S(2)}) %collective-permute-start.7) | collective-permute-done | bytes 327712 | tf_op jit(solution)/shard_map/ppermute | solution.py:23
  68.0 7.2 %all-to-all-start.1 = ((bf16[16,80,640]{2,1,0:T(8,128)(2,1)}), bf16[16,80,640]{2,1,0:T(8,128)(2,1)S(1)}, u32[]{:S(2)}, u32[]{:S(2)}) async-start(bf16[16,80,640]{2,1,0:T(8,128)(2,1)} %weight_partial.1), calls=%async_computation.1 | async-start | bytes 3276800 | tf_op jit(solution)/shard_map/all_to_all | solution.py:168
  79.1 3.8 %collective-permute-done.9 = f32[60,640]{1,0:T(8,128)S(1)} collective-permute-done((f32[60,640]{1,0:T(8,128)S(1)}, f32[60,640]{1,0:T(8,128)S(1)}, u32[]{:S(2)}, u32[]{:S(2)}) %collective-permute-start.9) | collective-permute-done | bytes 153632 | tf_op jit(solution)/shard_map/ppermute | solution.py:23
  82.9 13.5 %all-to-all-done.1 = bf16[16,80,640]{2,1,0:T(8,128)(2,1)S(1)} async-done(((bf16[16,80,640]{2,1,0:T(8,128)(2,1)}), bf16[16,80,640]{2,1,0:T(8,128)(2,1)S(1)}, u32[]{:S(2)}, u32[]{:S(2)}) %all-to-all-start.1) | async-done | bytes 1638432 | tf_op jit(solution)/shard_map/all_to_all | solution.py:168
  96.9 5.7 %collective-permute-done.10 = f32[80,640]{1,0:T(8,128)S(1)} collective-permute-done((f32[80,640]{1,0:T(8,128)S(1)}, f32[80,640]{1,0:T(8,128)S(1)}, u32[]{:S(2)}, u32[]{:S(2)}) %collective-permute-start.10) | collective-permute-done | bytes 204832 | tf_op jit(solution)/shard_map/ppermute | solution.py:23
  104.9 6.1 %all-to-all-start.2 = ((bf16[16,80,640]{2,1,0:T(8,128)(2,1)}), bf16[16,80,640]{2,1,0:T(8,128)(2,1)S(1)}, u32[]{:S(2)}, u32[]{:S(2)}) async-start(bf16[16,80,640]{2,1,0:T(8,128)(2,1)} %broadcast_in_dim.2), calls=%async_computation.2 | async-start | bytes 3276800 | tf_op jit(solution)/shard_map/all_to_all | solution.py:168
  111.3 4.1 %collective-permute-start.14 = (f32[10,640]{1,0:T(8,128)S(1)}, f32[10,640]{1,0:T(8,128)S(1)}, u32[]{:S(2)}, u32[]{:S(2)}) collective-permute-start(f32[10,640]{1,0:T(8,128)S(1)} %get-tuple-element.38), channel_id=1, source_target_pairs={{0,3},{1,0},{2,1},{3,2},{4,7},{5,4},{6,5},{7,6},{8,11},{9,8},{10,9... | collective-permute-start | bytes 76808 | tf_op jit(solution)/shard_map/ppermute | solution.py:23
  119.1 4.2 %collective-permute-done.13 = f32[10,640]{1,0:T(8,128)S(1)} collective-permute-done((f32[10,640]{1,0:T(8,128)S(1)}, f32[10,640]{1,0:T(8,128)S(1)}, u32[]{:S(2)}, u32[]{:S(2)}) %collective-permute-start.13) | collective-permute-done | bytes 25632 | tf_op jit(solution)/shard_map/ppermute | solution.py:23
  123.4 6.3 %all-to-all-done.2 = bf16[16,80,640]{2,1,0:T(8,128)(2,1)S(1)} async-done(((bf16[16,80,640]{2,1,0:T(8,128)(2,1)}), bf16[16,80,640]{2,1,0:T(8,128)(2,1)S(1)}, u32[]{:S(2)}, u32[]{:S(2)}) %all-to-all-start.2) | async-done | bytes 1638432 | tf_op jit(solution)/shard_map/all_to_all | solution.py:168
  129.6 2.2 %collective-permute-start.19 = (f32[10,640]{1,0:T(8,128)S(1)}, f32[10,640]{1,0:T(8,128)S(1)}, u32[]{:S(2)}, u32[]{:S(2)}) collective-permute-start(f32[10,640]{1,0:T(8,128)S(1)} %bitcast_add_fusion.1), channel_id=1, source_target_pairs={{0,0},{4,4},{8,16},{12,20},{16,32},{20,36},{24,48},{28,52},{32,64}... | collective-permute-start | bytes 76808 | tf_op jit(solution)/shard_map/ppermute | solution.py:250
  131.8 7.6 %collective-permute-start.20 = (f32[10,640]{1,0:T(8,128)S(1)}, f32[10,640]{1,0:T(8,128)S(1)}, u32[]{:S(2)}, u32[]{:S(2)}) collective-permute-start(f32[10,640]{1,0:T(8,128)S(1)} %fusion.2), channel_id=1, source_target_pairs={{0,0},{4,128},{8,4},{12,132},{16,8},{20,136},{24,12},{28,140},{32,... | collective-permute-start | bytes 76808 | tf_op jit(solution)/shard_map/ppermute | solution.py:251
  141.3 2.1 %right_product.2 = (f32[2,640,640]{2,1,0:T(8,128)S(1)}, f32[8,128]{1,0:T(8,128)S(1)}) custom-call(s32[1]{0:T(128)} %bitcast.half_index.core, bf16[1280,640]{1,0:T(8,128)(2,1)S(1)} %bitcast.28, bf16[2560,640]{1,0:T(8,128)(2,1)S(1)} %copy-done.1), custom_call_target="tpu_custom_call" | custom-call | flops 1048576000 | bytes 6291456 | tf_op jit(solution)/shard_map/right_product/pallas_call | solution.py:115
  143.4 2.1 %right_product.3 = (f32[2,640,640]{2,1,0:T(8,128)S(1)}, f32[8,128]{1,0:T(8,128)S(1)}) custom-call(s32[1]{0:T(128)S(6)} %sub.14.half_index, bf16[1280,640]{1,0:T(8,128)(2,1)S(1)} %collective-permute-done.15.left, bf16[2560,640]{1,0:T(8,128)(2,1)S(1)} %copy-done.2), custom_call_target="tpu_custom_call" | custom-call | flops 1048576000 | bytes 6291456 | tf_op jit(solution)/shard_map/right_product/pallas_call | solution.py:115
  148.2 2.4 %collective-permute-start.16 = (f32[8,128]{1,0:T(8,128)S(1)}, f32[8,128]{1,0:T(8,128)S(1)}, u32[]{:S(2)}, u32[]{:S(2)}) collective-permute-start(f32[8,128]{1,0:T(8,128)S(1)} %add.134.own), channel_id=1, source_target_pairs={{0,1},{1,2},{2,3},{3,0},{4,5},{5,6},{6,7},{7,4},{8,9},{9,10},{10,1... | collective-permute-start | bytes 12296 | tf_op jit(solution)/shard_map/ppermute | solution.py:23
  150.7 3.9 %collective-permute-done.17.sq_b = f32[8,128]{1,0:T(8,128)S(1)} collective-permute-done((f32[8,128]{1,0:T(8,128)S(1)}, f32[8,128]{1,0:T(8,128)S(1)}, u32[]{:S(2)}, u32[]{:S(2)}) %collective-permute-start.17) | collective-permute-done | bytes 4128 | tf_op jit(solution)/shard_map/ppermute | solution.py:23
  154.5 3.0 %final_update.1 = (bf16[640,2560]{1,0:T(8,128)(2,1)}, f32[10,640]{1,0:T(8,128)}, f32[10,640]{1,0:T(8,128)}) custom-call(s32[1]{0:T(128)} %bitcast.half_index.core, f32[8,128]{1,0:T(8,128)S(1)} %add.134.own, f32[8,128]{1,0:T(8,128)S(1)} %collective-permute-done.16.sq_a, f32[8,128]{1,0:T(8,128)S(1)} %collective-permute-done.17.sq_b, ...), custom_call_target="tpu_custom_call" | custom-call | flops 1638400 | bytes 10485760 | tf_op jit(solution)/shard_map/final_update/pallas_call | solution.py:155
  (65 shorter events, 25.3 us)
Async XLA Ops:
  0.7 3.3 %collective-permute-start.6 = (bf16[512,640]{1,0:T(8,128)(2,1)}, bf16[512,640]{1,0:T(8,128)(2,1)S(1)}, u32[]{:S(2)}, u32[]{:S(2)}) collective-permute-start(bf16[512,640]{1,0:T(8,128)(2,1)} %acts.1), channel_id=1, source_target_pairs={{0,4},{4,0},{1,5},{5,1},{2,6},{6,2},{3,7},{7,3},{8,12},{12,8},{9,1... | collective-permute-start | bytes 1966088 | tf_op jit(solution)/shard_map/ppermute | solution.py:23
  2.1 1.5 collective-permute-start
  2.6 1.4 collective-permute-start.3
  6.7 61.4 %all-to-all-start = ((bf16[16,3,40,640]{3,2,1,0:T(8,128)(2,1)}), bf16[16,3,40,640]{3,2,1,0:T(8,128)(2,1)}, u32[]{:S(2)}, u32[]{:S(2)}) async-start(bf16[16,3,40,640]{3,2,1,0:T(8,128)(2,1)} %cov_partial.1), calls=%async_computation | async-start | bytes 4915200 | tf_op jit(solution)/shard_map/all_to_all | solution.py:168
  14.1 24.6 %collective-permute-start.5 = (bf16[256,640]{1,0:T(8,128)(2,1)S(1)}, bf16[256,640]{1,0:T(8,128)(2,1)S(1)}, u32[]{:S(2)}, u32[]{:S(2)}) collective-permute-start(bf16[256,640]{1,0:T(8,128)(2,1)S(1)} %pad_maximum_fusion.1.refs_3_.second), channel_id=1, source_target_pairs={{0,3},{1,0},{2,1},{3,2},{4,7},{5,4},{6,5},{7,6},{8,11},{9,8},{10,9... | collective-permute-start | bytes 983048 | tf_op jit(solution)/shard_map/ppermute | solution.py:23
  20.4 24.6 %collective-permute-start.1 = (bf16[256,640]{1,0:T(8,128)(2,1)S(1)}, bf16[256,640]{1,0:T(8,128)(2,1)S(1)}, u32[]{:S(2)}, u32[]{:S(2)}) collective-permute-start(bf16[256,640]{1,0:T(8,128)(2,1)S(1)} %pad_maximum_fusion.refs_0_.first), channel_id=1, source_target_pairs={{0,1},{1,2},{2,3},{3,0},{4,5},{5,6},{6,7},{7,4},{8,9},{9,10},{10,1... | collective-permute-start | bytes 983048 | tf_op jit(solution)/shard_map/ppermute | solution.py:23
  20.5 26.3 %collective-permute-start.4 = (bf16[256,640]{1,0:T(8,128)(2,1)S(1)}, bf16[256,640]{1,0:T(8,128)(2,1)S(1)}, u32[]{:S(2)}, u32[]{:S(2)}) collective-permute-start(bf16[256,640]{1,0:T(8,128)(2,1)S(1)} %pad_maximum_fusion.1.refs_3_.second), channel_id=1, source_target_pairs={{0,1},{1,2},{2,3},{3,0},{4,5},{5,6},{6,7},{7,4},{8,9},{9,10},{10,1... | collective-permute-start | bytes 983048 | tf_op jit(solution)/shard_map/ppermute | solution.py:23
  22.1 32.1 %collective-permute-start.2 = (bf16[256,640]{1,0:T(8,128)(2,1)S(1)}, bf16[256,640]{1,0:T(8,128)(2,1)S(1)}, u32[]{:S(2)}, u32[]{:S(2)}) collective-permute-start(bf16[256,640]{1,0:T(8,128)(2,1)S(1)} %pad_maximum_fusion.refs_0_.first), channel_id=1, source_target_pairs={{0,3},{1,0},{2,1},{3,2},{4,7},{5,4},{6,5},{7,6},{8,11},{9,8},{10,9... | collective-permute-start | bytes 983048 | tf_op jit(solution)/shard_map/ppermute | solution.py:23
  38.7 23.6 %collective-permute-start.8 = (bf16[256,640]{1,0:T(8,128)(2,1)S(1)}, bf16[256,640]{1,0:T(8,128)(2,1)S(1)}, u32[]{:S(2)}, u32[]{:S(2)}) collective-permute-start(bf16[256,640]{1,0:T(8,128)(2,1)S(1)} %collective-permute-done.5.refs_5_), channel_id=1, source_target_pairs={{0,3},{1,0},{2,1},{3,2},{4,7},{5,4},{6,5},{7,6},{8,11},{9,8},{10,9... | collective-permute-start | bytes 983048 | tf_op jit(solution)/shard_map/ppermute | solution.py:23
  45.0 21.2 %collective-permute-start.7 = (bf16[256,640]{1,0:T(8,128)(2,1)S(1)}, bf16[256,640]{1,0:T(8,128)(2,1)S(1)}, u32[]{:S(2)}, u32[]{:S(2)}) collective-permute-start(bf16[256,640]{1,0:T(8,128)(2,1)S(1)} %collective-permute-done.1.refs_1_), channel_id=1, source_target_pairs={{0,1},{1,2},{2,3},{3,0},{4,5},{5,6},{6,7},{7,4},{8,9},{9,10},{10,1... | collective-permute-start | bytes 983048 | tf_op jit(solution)/shard_map/ppermute | solution.py:23
  68.0 28.4 %all-to-all-start.1 = ((bf16[16,80,640]{2,1,0:T(8,128)(2,1)}), bf16[16,80,640]{2,1,0:T(8,128)(2,1)S(1)}, u32[]{:S(2)}, u32[]{:S(2)}) async-start(bf16[16,80,640]{2,1,0:T(8,128)(2,1)} %weight_partial.1), calls=%async_computation.1 | async-start | bytes 3276800 | tf_op jit(solution)/shard_map/all_to_all | solution.py:168
  77.5 5.4 %collective-permute-start.9 = (f32[60,640]{1,0:T(8,128)S(1)}, f32[60,640]{1,0:T(8,128)S(1)}, u32[]{:S(2)}, u32[]{:S(2)}) collective-permute-start(f32[60,640]{1,0:T(8,128)S(1)} %pad_maximum_fusion.6), channel_id=1, source_target_pairs={{0,128},{128,0},{1,129},{129,1},{2,130},{130,2},{3,131},{131,3},{4... | collective-permute-start | bytes 460808 | tf_op jit(solution)/shard_map/ppermute | solution.py:23
  96.7 6.0 %collective-permute-start.10 = (f32[80,640]{1,0:T(8,128)S(1)}, f32[80,640]{1,0:T(8,128)S(1)}, u32[]{:S(2)}, u32[]{:S(2)}) collective-permute-start(f32[80,640]{1,0:T(8,128)S(1)} %convert_reduce_fusion.1), channel_id=1, source_target_pairs={{0,128},{128,0},{1,129},{129,1},{2,130},{130,2},{3,131},{131,3},{4... | collective-permute-start | bytes 614408 | tf_op jit(solution)/shard_map/ppermute | solution.py:23
  104.9 24.8 %all-to-all-start.2 = ((bf16[16,80,640]{2,1,0:T(8,128)(2,1)}), bf16[16,80,640]{2,1,0:T(8,128)(2,1)S(1)}, u32[]{:S(2)}, u32[]{:S(2)}) async-start(bf16[16,80,640]{2,1,0:T(8,128)(2,1)} %broadcast_in_dim.2), calls=%async_computation.2 | async-start | bytes 3276800 | tf_op jit(solution)/shard_map/all_to_all | solution.py:168
  111.0 6.5 %collective-permute-start.11 = (f32[10,640]{1,0:T(8,128)S(1)}, f32[10,640]{1,0:T(8,128)S(1)}, u32[]{:S(2)}, u32[]{:S(2)}) collective-permute-start(f32[10,640]{1,0:T(8,128)S(1)} %dynamic-slice_bitcast_fusion.5), channel_id=1, source_target_pairs={{0,4},{4,0},{1,5},{5,1},{2,6},{6,2},{3,7},{7,3},{8,12},{12,8},{9,1... | collective-permute-start | bytes 76808 | tf_op jit(solution)/shard_map/ppermute | solution.py:23
  111.2 6.3 %collective-permute-start.12 = (f32[10,640]{1,0:T(8,128)S(1)}, f32[10,640]{1,0:T(8,128)S(1)}, u32[]{:S(2)}, u32[]{:S(2)}) collective-permute-start(f32[10,640]{1,0:T(8,128)S(1)} %get-tuple-element.37), channel_id=1, source_target_pairs={{0,1},{1,2},{2,3},{3,0},{4,5},{5,6},{6,7},{7,4},{8,9},{9,10},{10,1... | collective-permute-start | bytes 76808 | tf_op jit(solution)/shard_map/ppermute | solution.py:23
  111.3 7.8 %collective-permute-start.14 = (f32[10,640]{1,0:T(8,128)S(1)}, f32[10,640]{1,0:T(8,128)S(1)}, u32[]{:S(2)}, u32[]{:S(2)}) collective-permute-start(f32[10,640]{1,0:T(8,128)S(1)} %get-tuple-element.38), channel_id=1, source_target_pairs={{0,3},{1,0},{2,1},{3,2},{4,7},{5,4},{6,5},{7,6},{8,11},{9,8},{10,9... | collective-permute-start | bytes 76808 | tf_op jit(solution)/shard_map/ppermute | solution.py:23
  115.4 7.9 %collective-permute-start.13 = (f32[10,640]{1,0:T(8,128)S(1)}, f32[10,640]{1,0:T(8,128)S(1)}, u32[]{:S(2)}, u32[]{:S(2)}) collective-permute-start(f32[10,640]{1,0:T(8,128)S(1)} %get-tuple-element.39), channel_id=1, source_target_pairs={{0,2},{1,3},{2,0},{3,1},{4,6},{5,7},{6,4},{7,5},{8,10},{9,11},{10,... | collective-permute-start | bytes 76808 | tf_op jit(solution)/shard_map/ppermute | solution.py:23
  129.6 13.8 %collective-permute-start.15 = (bf16[1280,640]{1,0:T(8,128)(2,1)S(1)}, bf16[1280,640]{1,0:T(8,128)(2,1)S(1)}, u32[]{:S(2)}, u32[]{:S(2)}) collective-permute-start(bf16[1280,640]{1,0:T(8,128)(2,1)S(1)} %bitcast.27), channel_id=1, source_target_pairs={{0,4},{4,0},{1,5},{5,1},{2,6},{6,2},{3,7},{7,3},{8,12},{12,8},{9,1... | collective-permute-start | bytes 4915208 | tf_op jit(solution)/shard_map/ppermute | solution.py:23
  129.6 21.0 %collective-permute-start.19 = (f32[10,640]{1,0:T(8,128)S(1)}, f32[10,640]{1,0:T(8,128)S(1)}, u32[]{:S(2)}, u32[]{:S(2)}) collective-permute-start(f32[10,640]{1,0:T(8,128)S(1)} %bitcast_add_fusion.1), channel_id=1, source_target_pairs={{0,0},{4,4},{8,16},{12,20},{16,32},{20,36},{24,48},{28,52},{32,64}... | collective-permute-start | bytes 76808 | tf_op jit(solution)/shard_map/ppermute | solution.py:250
  131.8 18.9 %collective-permute-start.20 = (f32[10,640]{1,0:T(8,128)S(1)}, f32[10,640]{1,0:T(8,128)S(1)}, u32[]{:S(2)}, u32[]{:S(2)}) collective-permute-start(f32[10,640]{1,0:T(8,128)S(1)} %fusion.2), channel_id=1, source_target_pairs={{0,0},{4,128},{8,4},{12,132},{16,8},{20,136},{24,12},{28,140},{32,... | collective-permute-start | bytes 76808 | tf_op jit(solution)/shard_map/ppermute | solution.py:251
  145.6 5.1 %collective-permute-start.18 = (f32[8,128]{1,0:T(8,128)S(1)}, f32[8,128]{1,0:T(8,128)S(1)}, u32[]{:S(2)}, u32[]{:S(2)}) collective-permute-start(f32[8,128]{1,0:T(8,128)S(1)} %add.134.own), channel_id=1, source_target_pairs={{0,3},{1,0},{2,1},{3,2},{4,7},{5,4},{6,5},{7,6},{8,11},{9,8},{10,9... | collective-permute-start | bytes 12296 | tf_op jit(solution)/shard_map/ppermute | solution.py:23
  147.0 7.5 %collective-permute-start.17 = (f32[8,128]{1,0:T(8,128)S(1)}, f32[8,128]{1,0:T(8,128)S(1)}, u32[]{:S(2)}, u32[]{:S(2)}) collective-permute-start(f32[8,128]{1,0:T(8,128)S(1)} %add.134.own), channel_id=1, source_target_pairs={{0,2},{1,3},{2,0},{3,1},{4,6},{5,7},{6,4},{7,5},{8,10},{9,11},{10,... | collective-permute-start | bytes 12296 | tf_op jit(solution)/shard_map/ppermute | solution.py:23
  148.2 6.3 %collective-permute-start.16 = (f32[8,128]{1,0:T(8,128)S(1)}, f32[8,128]{1,0:T(8,128)S(1)}, u32[]{:S(2)}, u32[]{:S(2)}) collective-permute-start(f32[8,128]{1,0:T(8,128)S(1)} %add.134.own), channel_id=1, source_target_pairs={{0,1},{1,2},{2,3},{3,0},{4,5},{5,6},{6,7},{7,4},{8,9},{9,10},{10,1... | collective-permute-start | bytes 12296 | tf_op jit(solution)/shard_map/ppermute | solution.py:23
  (4 other events, 109.5 us)
